TPU v7x, 128 devices: a whole 4x4x4 slice. The times are simulated.
128 devices in a mesh: replica: 8 (over y, core), tensor: 16 (over x, z).
Axes of the slice: x: 4, y: 4, z: 4, core: 2. Of those that a mesh axis runs over, the one named last changes fastest.
Arguments:
- queries: bfloat16 [512, 2, 8192], P(('replica', 'tensor')), may hold values from -200 to 200
- cached_key_rows: bfloat16 [512, 2, 64, 1024], P(('replica', 'tensor')), may hold values from -7 to 7
- cached_value_rows: bfloat16 [512, 2, 64, 1024], P(('replica', 'tensor')), may hold values from -6 to 6
- current_token_key: bfloat16 [512, 2, 1024], P(('replica', 'tensor')), may hold values from -7 to 7
- current_token_value: bfloat16 [512, 2, 1024], P(('replica', 'tensor')), may hold values from -6 to 6
- lengths: int32 [512], P(('replica', 'tensor')), may hold values from 1 to 64, as said below
- residual: bfloat16 [512, 2, 8192], P(('replica', 'tensor')), may hold values from -250 to 250
- output_projection_weight: bfloat16 [8192, 8192], P('tensor'), may hold values from -0.0625 to 0.0625
- request_adapter_index: int32 [512], P('replica'), may hold values from 0 to 383, as said below
- lowrank_down_factors: bfloat16 [384, 16, 8192], P('replica', None, 'tensor'), may hold values from -0.0625 to 0.0625
- lowrank_up_factors: bfloat16 [384, 16, 8192], P('replica', None, 'tensor'), may hold values from -1.5 to 1.5
- final_norm_scale: bfloat16 [8192], replicated, may hold values from 0.5 to 1.5
- vocabulary_head_matrix: bfloat16 [8192, 98304], P(None, ('replica', 'tensor')), may hold values from -2 to 2
Outputs:
- contrast: float32 [512, 98304], P(None, ('replica', 'tensor'))
Inputs may be any that keep to these rules, and one draw needn't show every extreme that they name: `lengths`: at least one request has exactly 64 cached positions. `request_adapter_index`: adapter id // 48 is the replica group that holds the adapter; among the 64 requests of one replica group at most 16 name adapters of one holding group, and in every draw one holding group is named by exactly 16 requests of every replica group.
All inputs are finite; a program needn't handle non-finite values.
Results may differ from a plain program's by a relative error of at most 0.0023.
Values may be sent and summed in bfloat16 or wider, within the bound.
No kernel may reach another device: no remote copies, remote signals or barrier semaphores. Data moves between devices by JAX's collectives and lax.ppermute only.
A program may use at most 128 MiB of HBM per device.

v0:
```python
import math

import jax
import jax.numpy as jnp
from jax import lax
from jax.sharding import PartitionSpec as P

HEADS = 64
KVH = 8
HD = 128


BETA = 0.5
LOWRANK_SCALE = 2.0
EPS = 1e-05
HIGH_PRECISION = lax.Precision.HIGHEST


def attend(
    queries, cached_key_rows, cached_value_rows, current_token_key, current_token_value, lengths
):
    count = queries.shape[0]
    group = HEADS // KVH
    scale = 1.0 / math.sqrt(HD)
    query = queries.reshape(count, 2, KVH, group, HD)
    keys = cached_key_rows.reshape(count, 2, -1, KVH, HD)
    values = cached_value_rows.reshape(count, 2, -1, KVH, HD)
    fresh_key = current_token_key.reshape(count, 2, KVH, HD)
    fresh_value = current_token_value.reshape(count, 2, KVH, HD).astype(jnp.float32)
    scores = (
        jnp.einsum("rbkgd,rbpkd->rbkgp", query, keys, preferred_element_type=jnp.float32) * scale
    )
    own_score = (
        jnp.einsum("rbkgd,rbkd->rbkg", query, fresh_key, preferred_element_type=jnp.float32) * scale
    )
    places = jnp.arange(keys.shape[2], dtype=jnp.int32)
    valid = (places[None, :] < lengths[:, None])[:, None, None, None, :]
    highest = jnp.maximum(jnp.max(jnp.where(valid, scores, -1e30), axis=-1), own_score)
    powers = jnp.where(valid, jnp.exp(scores - highest[..., None]), 0.0)
    fresh = jnp.exp(own_score - highest)
    summed = jnp.sum(powers, axis=-1) + fresh
    weights = (powers / summed[..., None]).astype(jnp.bfloat16)
    fresh_weight = (fresh / summed).astype(jnp.bfloat16)
    mixed = jnp.einsum("rbkgp,rbpkd->rbkgd", weights, values, preferred_element_type=jnp.float32)
    mixed = mixed + fresh_weight.astype(jnp.float32)[..., None] * fresh_value[:, :, :, None, :]
    return mixed.reshape(count, 2, HEADS * HD).astype(jnp.bfloat16)


def normalize(hidden, gain):
    values = hidden.astype(jnp.float32)
    square = jnp.mean(values * values, axis=-1, keepdims=True)
    return (values * lax.rsqrt(square + EPS) * gain.astype(jnp.float32)).astype(jnp.bfloat16)


def per_device(
    queries,
    cached_key_rows,
    cached_value_rows,
    current_token_key,
    current_token_value,
    lengths,
    residual,
    output_projection_weight,
    request_adapter_index,
    lowrank_down_factors,
    lowrank_up_factors,
    final_norm_scale,
    vocabulary_head_matrix,
):
    attended = attend(
        queries, cached_key_rows, cached_value_rows, current_token_key, current_token_value, lengths
    )
    features = lax.all_to_all(attended, "tensor", split_axis=2, concat_axis=0, tiled=True)
    width = features.shape[2]
    offset = lax.axis_index("tensor") * width
    expert_in = features[:, 0, :]
    down_factor_part = lax.all_gather(lowrank_down_factors, "replica", axis=0, tiled=True)
    up_factor_part = lax.all_gather(lowrank_up_factors, "replica", axis=0, tiled=True)
    select = (
        request_adapter_index[:, None]
        == jnp.arange(down_factor_part.shape[0], dtype=jnp.int32)[None, :]
    ).astype(jnp.bfloat16)
    down_factor_rows = jnp.einsum(
        "ra,akf->rkf", select, down_factor_part, preferred_element_type=jnp.float32
    ).astype(jnp.bfloat16)
    up_factor_rows = jnp.einsum(
        "ra,akf->rkf", select, up_factor_part, preferred_element_type=jnp.float32
    ).astype(jnp.bfloat16)
    partial_value = jnp.einsum(
        "rf,rkf->rk", expert_in, down_factor_rows, preferred_element_type=jnp.float32
    )
    partial_rank = partial_value
    rank_activation = lax.psum(partial_rank, "tensor")
    lowrank_update = LOWRANK_SCALE * jnp.einsum(
        "vc,vcm->vm", rank_activation, up_factor_rows.astype(jnp.float32), precision=HIGH_PRECISION
    )
    partial_value = jnp.einsum(
        "rbf,fd->rbd", features, output_projection_weight, preferred_element_type=jnp.float32
    )
    corner = (
        lax.dynamic_slice(
            partial_value, (0, 0, offset), (lax.axis_size("tensor") * residual.shape[0], 1, width)
        )
        + lowrank_update[:, None, :]
    )
    mixed = lax.psum_scatter(
        lax.dynamic_update_slice(partial_value, corner, (0, 0, offset)),
        "tensor",
        scatter_dimension=0,
        tiled=True,
    )
    hidden = (residual.astype(jnp.float32) + mixed).astype(jnp.bfloat16)
    normed = normalize(hidden, final_norm_scale)
    logits = jnp.einsum(
        "rbd,dv->rbv",
        lax.all_gather(normed, ("replica", "tensor"), axis=0, tiled=True),
        vocabulary_head_matrix,
        preferred_element_type=jnp.float32,
    )
    local_peak = jnp.max(logits, axis=-1)
    highest = lax.pmax(local_peak, ("replica", "tensor"))
    summed = lax.psum(jnp.sum(jnp.exp(logits - highest[..., None]), axis=-1), ("replica", "tensor"))
    norm_log = highest + jnp.log(summed)
    logprob = logits - norm_log[..., None]
    return (1.0 + BETA) * logprob[:, 0, :] - BETA * logprob[:, 1, :]


def solution(mesh):
    in_specs = (
        P(("replica", "tensor"), None, None),
        P(("replica", "tensor"), None, None, None),
        P(("replica", "tensor"), None, None, None),
        P(("replica", "tensor"), None, None),
        P(("replica", "tensor"), None, None),
        P(("replica", "tensor")),
        P(("replica", "tensor"), None, None),
        P("tensor", None),
        P("replica"),
        P("replica", None, "tensor"),
        P("replica", None, "tensor"),
        P(),
        P(None, ("replica", "tensor")),
    )
    out_specs = P(None, ("replica", "tensor"))
    return jax.shard_map(
        per_device, mesh=mesh, in_specs=in_specs, out_specs=out_specs, check_vma=False
    )
```

profile of v0, /device:TPU:1, one launch (start us, length us, event | category | flops | bytes accessed | tf_op | source)
XLA Modules:
  0.0 532.0 jit_solution(3577235775137107045)
XLA Ops:
  9.5 1.0 reshape.59
  11.4 2.0 select_reduce_fusion
  14.2 4.9 copy.42
  19.1 9.3 %reshape.78 = bf16[16,2,2048]{2,1,0:T(2,128)(2,1)} reshape(bf16[8192,2,4]{2,1,0:T(2,128)(2,1)} %bitcast.61) | data formatting | bytes 262144
  28.4 8.5 %all-to-all-start = ((bf16[16,2,2048]{2,1,0:T(2,128)(2,1)}), bf16[16,2,2048]{2,1,0:T(2,128)(2,1)S(1)}, u32[]{:S(2)}, u32[]{:S(2)}) async-start(bf16[16,2,2048]{2,1,0:T(2,128)(2,1)} %reshape.78), calls=%async_computation | async-start | bytes 262144 | tf_op jit(solution)/shard_map/all_to_all | solution.py:73
  37.5 6.3 %all-to-all-done = bf16[16,2,2048]{2,1,0:T(2,128)(2,1)S(1)} async-done(((bf16[16,2,2048]{2,1,0:T(2,128)(2,1)}), bf16[16,2,2048]{2,1,0:T(2,128)(2,1)S(1)}, u32[]{:S(2)}, u32[]{:S(2)}) %all-to-all-start) | async-done | bytes 131104 | tf_op jit(solution)/shard_map/all_to_all | solution.py:73
  43.8 10.0 %reshape.79 = bf16[8192,2,4]{2,1,0:T(2,128)(2,1)} reshape(bf16[16,2,2048]{2,1,0:T(2,128)(2,1)S(1)} %all-to-all-done) | data formatting | bytes 262144
  53.8 9.7 %copy.29 = bf16[4,2,16,512]{3,0,2,1:T(4,128)(2,1)S(1)} copy(bf16[4,2,16,512]{0,1,3,2:T(2,128)(2,1)} %bitcast.62) | data formatting | bytes 262144 | tf_op jit(solution)/shard_map/all_to_all | solution.py:73
  63.5 7.5 %fusion.3 = f32[64,2,8192]{2,0,1:T(8,128)} fusion(bf16[64,2,512]{2,0,1:T(8,128)(2,1)S(1)} %all_to_all.16, bf16[512,8192]{1,0:T(8,128)(2,1)} %param.20), kind=kOutput, calls=%fused_computation.3 | convolution fusion | flops 1073741824 | bytes 12713984 | tf_op jit(solution)/shard_map/rbf,fd->rbd/dot_general | solution.py:97
  71.1 10.0 %fusion.11 = bf16[64,16,512]{2,0,1:T(8,128)(2,1)S(1)} fusion(bf16[384,16,512]{2,1,0:T(8,128)(2,1)} %all-gather.4.cloned.1.call-done, s32[64]{0:T(128)S(1)} %copy-done.4), kind=kOutput, calls=%fused_computation.15 | convolution fusion | flops 403202048 | bytes 7340288 | tf_op jit(solution)/shard_map/ra,akf->rkf/dot_general | solution.py:83
  81.7 56.1 %psum.14 = f32[64,16]{1,0:T(8,128)S(1)} all-reduce(f32[64,16]{1,0:T(8,128)S(1)} %bitcast.67), channel_id=1, replica_groups=mesh['replica'=8,'tensor'=16] {'tensor'}, use_global_device_ids=true, to_apply=%region_2.3 | all-reduce | flops 1024 | bytes 8192 | tf_op jit(solution)/shard_map/psum | solution.py:93
  137.9 9.8 %fusion.14 = bf16[64,16,512]{2,0,1:T(8,128)(2,1)S(1)} fusion(bf16[384,16,512]{2,1,0:T(8,128)(2,1)} %all-gather.6.cloned.1.call-done, s32[64]{0:T(128)S(1)} %copy-done.4), kind=kOutput, calls=%fused_computation.16 | convolution fusion | flops 403202048 | bytes 7340288 | tf_op jit(solution)/shard_map/ra,akf->rkf/dot_general | solution.py:86
  147.7 1.1 fusion.22
  148.8 1.6 fusion.31
  151.8 114.5 %all-reduce.3.cloned.1.call-done = f32[64,2,8192]{2,0,1:T(8,128)} async-done(((f32[64,2,8192]{2,0,1:T(8,128)}), f32[64,2,8192]{2,0,1:T(8,128)}) %all-reduce.3.cloned.1.call-update) | async-done | bytes 4194320
  266.3 1.3 fusion.26
  267.8 0.8 copy.32
  268.6 81.3 %all-gather.8.cloned.1.call-done = bf16[512,2,8192]{2,1,0:T(2,128)(2,1)} async-done(((bf16[4,2,8192]{2,1,0:T(2,128)(2,1)}), bf16[512,2,8192]{2,1,0:T(2,128)(2,1)}) %all-gather.8.cloned.1.call-update) | async-done | bytes 16777232 | tf_op jit(solution)/shard_map/all_gather | solution.py:116
  349.9 40.6 %fusion.46 = (f32[512,2]{0,1:T(2,128)S(1)}, f32[512,2,768]{2,0,1:T(8,128)}) fusion(bf16[8192,768]{1,0:T(8,128)(2,1)} %param.25, bf16[512,2,8192]{2,1,0:T(2,128)(2,1)} %all-gather.8.cloned.1.call-done), kind=kOutput, calls=%fused_computation.61 | convolution fusion | flops 12885687296 | bytes 32509952 | tf_op jit(solution)/shard_map/rbd,dv->rbv/dot_general | solution.py:114
  390.6 64.5 %pmax.7 = f32[512,2]{0,1:T(2,128)S(1)} all-reduce(f32[512,2]{0,1:T(2,128)S(1)} %get-tuple-element.11), channel_id=1, replica_groups=mesh['replica'=8,'tensor'=16] {'replica','tensor'}, use_global_device_ids=true, to_apply=%region_6.7 | all-reduce | flops 1024 | bytes 8192 | tf_op jit(solution)/shard_map/pmax | solution.py:121
  455.0 2.6 exponential_reduce_fusion
  457.6 64.0 %psum.15 = f32[512,2]{0,1:T(2,128)S(1)} all-reduce(f32[512,2]{0,1:T(2,128)S(1)} %exponential_reduce_fusion), channel_id=1, replica_groups=mesh['replica'=8,'tensor'=16] {'replica','tensor'}, use_global_device_ids=true, to_apply=%region_8.9 | all-reduce | flops 1024 | bytes 8192 | tf_op jit(solution)/shard_map/psum | solution.py:122
  521.7 2.2 broadcast_subtract_fusion
  523.9 1.3 fusion.10
  (38 shorter events, 6.8 us)
Async XLA Ops:
  6.5 7.2 %copy-start = (bf16[4,2,64,1024]{3,2,1,0:T(8,128)(2,1)S(1)}, bf16[4,2,64,1024]{3,2,1,0:T(8,128)(2,1)}, u32[]{:S(2)}) copy-start(bf16[4,2,64,1024]{3,2,1,0:T(8,128)(2,1)} %param.15) | copy-start | bytes 3145732
  6.5 64.5 %all-gather.4.cloned.1.call-start = ((), (), s32[]{:S(2)}) async-start(), calls=%async_computation.1 | async-start | bytes 7077888 | tf_op jit(solution)/shard_map/all_gather | solution.py:77
  7.3 130.6 %all-gather.6.cloned.1.call-start = ((), (), s32[]{:S(2)}) async-start(), calls=%async_computation.2 | async-start | bytes 7077888 | tf_op jit(solution)/shard_map/all_gather | solution.py:78
  28.4 15.4 %all-to-all-start = ((bf16[16,2,2048]{2,1,0:T(2,128)(2,1)}), bf16[16,2,2048]{2,1,0:T(2,128)(2,1)S(1)}, u32[]{:S(2)}, u32[]{:S(2)}) async-start(bf16[16,2,2048]{2,1,0:T(2,128)(2,1)} %reshape.78), calls=%async_computation | async-start | bytes 262144 | tf_op jit(solution)/shard_map/all_to_all | solution.py:73
  36.9 229.4 %all-reduce.3.cloned.1.call-start = ((), (), s32[]{:S(2)}) async-start(), calls=%async_computation.4 | async-start | bytes 8388608
  63.5 7.5 %copy-start.4 = (s32[64]{0:T(128)S(1)}, s32[64]{0:T(128)}, u32[]{:S(2)}) copy-start(s32[64]{0:T(128)} %param.21) | copy-start | bytes 772
  147.7 2.8 copy-start.3
  147.7 2.8 copy-start.5
  147.7 118.6 %copy-start.2 = (bf16[4,2,8192]{2,1,0:T(2,128)(2,1)S(1)}, bf16[4,2,8192]{2,1,0:T(2,128)(2,1)}, u32[]{:S(2)}) copy-start(bf16[4,2,8192]{2,1,0:T(2,128)(2,1)} %param.19) | copy-start | bytes 393220
  150.4 199.5 %all-gather.8.cloned.1.call-start = ((), (), s32[]{:S(2)}) async-start(), calls=%async_computation.3 | async-start | bytes 16908288 | tf_op jit(solution)/shard_map/all_gather | solution.py:116
  521.6 3.6 copy-start.1
Sparse Core Ops, SparseCore 0:
  9.0 44.5 all-gather.3
  55.3 40.9 all-gather.5
  150.6 115.7 all-reduce.2
  269.3 80.5 all-gather.7
where the time goes:
time: 536 us; the launch traced here: 532 us
  waiting for transfers between devices  204 us (38%)
  blocking collectives  185 us (35%)
  matrix products  72.3 us (13%)
  local copies, waits for them, and re-layouts  37.8 us (7%)
  between operations  14.2 us (3%)
  other arithmetic  10.3 us (2%)
  starting transfers between devices  9.15 us (2%)
    unnamed x5, waiting for transfers between devices  116 us
    all_gather x1, waiting for transfers between devices, per_device(): lax.all_gather(normed, ('replica', 'tensor'), axis=0, tiled=True)  81.3 us
    pmax x1, blocking collectives, per_device(): highest = lax.pmax(local_peak, ('replica', 'tensor'))  64.5 us
    psum x1, blocking collectives, per_device(): lax.psum(jnp.sum(jnp.exp(logits - highest[..., None]), axis=-1), ('replic...  64 us
    psum x1, blocking collectives, per_device(): rank_activation = lax.psum(partial_rank, 'tensor')  56.1 us
    dot_general x1, matrix products, per_device(): jnp.einsum('rbd,dv->rbv', lax.all_gather(normed, ('replica', 'tensor'), a...  40.6 us
    unnamed x15, local copies, waits for them, and re-layouts  19.9 us
  transfers between devices with their start and end apart: 5, of which 3 were waited for; matrix products, arithmetic and copies ran while one was open for 11% of the time, Pallas kernels for 0%

commit v1 on v0

v1 whole, which is shorter than its diff:
```python
import math

import jax
import jax.numpy as jnp
import numpy as np
from jax import lax
from jax.experimental import pallas as pl
from jax.experimental.pallas import tpu as pltpu
from jax.sharding import Mesh
from jax.sharding import PartitionSpec as P

WIDTH = 8192
HD = 128
CTX = 64
RANK = 16
HELD = 48
REQ = 64
TEN = 16
COLS = WIDTH // TEN
VOC = 768
NY = 4
BETA = 0.5
LOWRANK_SCALE = 2.0
EPS = 1e-05
MIB = 1 << 20
LAST = (((1,), (1,)), ((), ()))
F32 = jnp.float32
BF16 = jnp.bfloat16


def params(mib):
    return pltpu.CompilerParams(vmem_limit_bytes=mib * MIB)


GROUPS = 4


def attention_kernel(len_ref, q_ref, k_ref, v_ref, ck_ref, cv_ref, res_ref, o_ref, q_s, r_s, ck_s, cv_s):
    scale = 1.0 / math.sqrt(HD)
    for r in range(4):
        q_s[2 * r : 2 * r + 2, :] = q_ref[r].astype(F32)
        r_s[2 * r : 2 * r + 2, :] = res_ref[r].astype(F32)
        ck_s[2 * r : 2 * r + 2, :] = ck_ref[r].astype(F32)
        cv_s[2 * r : 2 * r + 2, :] = cv_ref[r].astype(F32)
    row = lax.broadcasted_iota(jnp.int32, (64, 8 * CTX), 0)
    col = lax.broadcasted_iota(jnp.int32, (64, 8 * CTX), 1)
    owner = col // CTX
    limit = jnp.zeros((64, 8 * CTX), jnp.int32)
    for r in range(4):
        limit = jnp.where(owner // 2 == r, len_ref[r], limit)
    valid = (row % 8 == owner) & (col % CTX < limit)
    for g in range(GROUPS):
        lanes = slice(g * HD, (g + 1) * HD)
        base = g * 8 * HD
        q = jnp.concatenate([q_s[:, base + h * HD : base + (h + 1) * HD] for h in range(8)], axis=0)
        keys = k_ref[:, :, :, lanes].reshape(8 * CTX, HD)
        values = v_ref[:, :, :, lanes].reshape(8 * CTX, HD)
        scores = lax.dot_general(q.astype(BF16), keys, LAST, preferred_element_type=F32) * scale
        fresh_key = jnp.concatenate([ck_s[:, lanes]] * 8, axis=0)
        fresh_value = jnp.concatenate([cv_s[:, lanes]] * 8, axis=0)
        own = jnp.sum(q * fresh_key, axis=1, keepdims=True) * scale
        highest = jnp.max(jnp.where(valid, scores, -1e30), axis=1, keepdims=True)
        highest = jnp.maximum(highest, own)
        powers = jnp.where(valid, jnp.exp(scores - highest), 0.0)
        fresh = jnp.exp(own - highest)
        summed = jnp.sum(powers, axis=1, keepdims=True) + fresh
        weights = (powers / summed).astype(BF16)
        fresh_weight = (fresh / summed).astype(BF16).astype(F32)
        mixed = jnp.dot(weights, values, preferred_element_type=F32) + fresh_weight * fresh_value
        for h in range(8):
            both = jnp.concatenate(
                [mixed[h * 8 : (h + 1) * 8, :], r_s[:, base + h * HD : base + (h + 1) * HD]], axis=0
            )
            o_ref[2 * g + h // 4, :, (h % 4) * HD : (h % 4 + 1) * HD] = both.astype(BF16)


def attention(queries, keys, values, fresh_key, fresh_value, lengths, residual):
    wide = pl.BlockSpec((4, 2, GROUPS * 1024), lambda g: (0, 0, g))
    cache = pl.BlockSpec((4, 2, CTX, GROUPS * HD), lambda g: (0, 0, 0, g))
    narrow = pl.BlockSpec((4, 2, GROUPS * HD), lambda g: (0, 0, g))
    return pl.pallas_call(
        attention_kernel,
        grid=(8 // GROUPS,),
        in_specs=[
            pl.BlockSpec(memory_space=pltpu.SMEM),
            wide,
            cache,
            cache,
            narrow,
            narrow,
            wide,
        ],
        out_specs=pl.BlockSpec((2 * GROUPS, 16, COLS), lambda g: (g, 0, 0)),
        out_shape=jax.ShapeDtypeStruct((TEN, 16, COLS), BF16),
        scratch_shapes=[
            pltpu.VMEM((8, GROUPS * 1024), F32),
            pltpu.VMEM((8, GROUPS * 1024), F32),
            pltpu.VMEM((8, GROUPS * HD), F32),
            pltpu.VMEM((8, GROUPS * HD), F32),
        ],
        compiler_params=params(56),
        cost_estimate=pl.CostEstimate(flops=3 * 10**8, bytes_accessed=3 * MIB, transcendentals=262144),
    )(lengths, queries, keys, values, fresh_key, fresh_value, residual)


def start_rows(slot_ref, tables, rows_s, sem):
    held = tables[0].shape[0]

    def one(r, carry):
        slot = slot_ref[r]
        for n, table_ref in enumerate(tables):

            @pl.when((slot >= n * held) & (slot < (n + 1) * held))
            def _():
                pltpu.make_async_copy(table_ref.at[slot - n * held], rows_s.at[r], sem).start()

        return carry

    lax.fori_loop(0, REQ, one, 0, unroll=4)


def wait_rows(tables, rows_s, sem):
    pltpu.make_async_copy(tables[0].at[pl.ds(0, REQ)], rows_s, sem).wait()


def own_lanes(rows, lanes, first):
    row = lax.broadcasted_iota(jnp.int32, (rows, lanes), 0)
    lane = lax.broadcasted_iota(jnp.int32, (rows, lanes), 1)
    return row == 2 * (lane // RANK + first)


def attended_rows(got_ref):
    return got_ref[...].astype(F32)[:, 0:8, :].reshape(128, COLS).astype(BF16)


WIDE = 4


def projection_kernel(got_ref, w_ref, o_ref, att_s):
    @pl.when(pl.program_id(0) == 0)
    def _():
        att_s[...] = attended_rows(got_ref)

    for t in range(WIDE):
        part = jnp.dot(
            att_s[...], w_ref[:, t * COLS : (t + 1) * COLS], preferred_element_type=F32
        )
        o_ref[t] = part.astype(BF16)


def projection(got, weight):
    return pl.pallas_call(
        projection_kernel,
        grid=(TEN // WIDE,),
        in_specs=[
            pl.BlockSpec((TEN, 16, COLS), lambda j: (0, 0, 0)),
            pl.BlockSpec((COLS, WIDE * COLS), lambda j: (0, j)),
        ],
        out_specs=pl.BlockSpec((WIDE, 128, COLS), lambda j: (j, 0, 0)),
        out_shape=jax.ShapeDtypeStruct((TEN, 128, COLS), BF16),
        scratch_shapes=[pltpu.VMEM((128, COLS), BF16)],
        compiler_params=params(56),
        cost_estimate=pl.CostEstimate(flops=11 * 10**8, bytes_accessed=11 * MIB, transcendentals=0),
    )(got, weight)


def rank_kernel(idx_ref, got_ref, table_ref, o_ref, rows_s, sem):
    start_rows(idx_ref, [table_ref], rows_s, sem)
    attended = attended_rows(got_ref)
    wait_rows([table_ref], rows_s, sem)
    rows = rows_s[...].reshape(REQ * RANK, COLS)
    product = lax.dot_general(attended, rows, LAST, preferred_element_type=F32)
    mask = own_lanes(128, REQ * RANK, 0)
    o_ref[...] = jnp.sum(jnp.where(mask, product, 0.0), axis=0, keepdims=True)


def rank_sums(index, got, table):
    near = pl.BlockSpec(memory_space=pltpu.VMEM)
    return pl.pallas_call(
        rank_kernel,
        in_specs=[
            pl.BlockSpec(memory_space=pltpu.SMEM),
            near,
            pl.BlockSpec(memory_space=pl.ANY),
        ],
        out_specs=near,
        out_shape=jax.ShapeDtypeStruct((1, REQ * RANK), F32),
        scratch_shapes=[pltpu.VMEM((REQ, RANK, COLS), BF16), pltpu.SemaphoreType.DMA],
        compiler_params=params(56),
        cost_estimate=pl.CostEstimate(flops=14 * 10**7, bytes_accessed=2 * MIB, transcendentals=0),
    )(index, got, table)


def hidden_kernel(
    slot_ref, sums_ref, k0_ref, k1_ref, k2_ref, k3_ref, got_ref, gain_ref, own_ref, sib_ref,
    oa_ref, ob_ref, rows_s, hid_s, sem,
):
    tables = [own_ref, sib_ref]
    start_rows(slot_ref, tables, rows_s, sem)
    total = sums_ref[0].astype(F32)
    for t in range(1, TEN):
        total = total + sums_ref[t].astype(F32)
    rank = (k0_ref[...] + k1_ref[...]) + (k2_ref[...] + k3_ref[...])
    base = got_ref[...].astype(F32)[:, 8:16, :].reshape(128, COLS)
    spread = jnp.where(own_lanes(128, REQ * RANK, 0), rank, 0.0)
    high = spread.astype(BF16)
    low = (spread - high.astype(F32)).astype(BF16)
    wait_rows(tables, rows_s, sem)
    rows = rows_s[...].reshape(REQ * RANK, COLS)
    delta = jnp.dot(high, rows, preferred_element_type=F32)
    delta = delta + jnp.dot(low, rows, preferred_element_type=F32)
    hidden = (base + (total + LOWRANK_SCALE * delta)).astype(BF16).astype(F32)
    scaled = hidden * gain_ref[...].astype(F32)
    for j in range(COLS // HD):
        lanes = slice(j * HD, (j + 1) * HD)
        hid_s[j] = scaled[:, lanes]
        o_ref = oa_ref if j * HD < HALF else ob_ref
        lanes = slice(j * HD % HALF, j * HD % HALF + HD)
        for kind in range(2):
            rows = hid_s[j, pl.ds(kind, REQ, stride=2), :]
            o_ref[kind * REQ : (kind + 1) * REQ, lanes] = rows.astype(BF16)


HALF = COLS // 2


def hidden_slice(slots, sums, rank, got, gain, own, sib):
    near = pl.BlockSpec(memory_space=pltpu.VMEM)
    far = pl.BlockSpec(memory_space=pl.ANY)
    return pl.pallas_call(
        hidden_kernel,
        in_specs=[pl.BlockSpec(memory_space=pltpu.SMEM)] + [near] * 7 + [far] * 2,
        out_specs=[near, near],
        out_shape=[jax.ShapeDtypeStruct((128, HALF), BF16)] * 2,
        scratch_shapes=[
            pltpu.VMEM((REQ, RANK, COLS), BF16),
            pltpu.VMEM((COLS // HD, 128, HD), F32),
            pltpu.SemaphoreType.DMA,
        ],
        compiler_params=params(16),
        cost_estimate=pl.CostEstimate(flops=3 * 10**8, bytes_accessed=4 * MIB, transcendentals=0),
    )(slots, sums, *rank, got, gain, own, sib)


TILE = 256
TILES = 2 * VOC // TILE


def tensor_index(at, first, second):
    along_x = jnp.where(at[3] == 0, first, second)
    along_z = jnp.where(at[3] == 0, second, first)
    return lax.rem(at[1] + along_x, 4) * 4 + lax.rem(at[2] + along_z, 4)


def head_kernel(pieces, first, last, at_ref, inv_ref, *refs):
    count = 1 + max(piece[0] for piece in pieces)
    x_refs, wo_ref, ws_ref, refs = refs[:count], refs[count], refs[count + 1], refs[count + 2 :]
    if not first:
        sums_ref, square_ref, refs = refs[0], refs[1], refs[2:]
    if last:
        uo_ref, us_ref, lse_ref, x_s, w_s, acc_s, sq_s, x_sem, w_sem, in_sem, q_sem = refs
    else:
        out_ref, squares_ref, x_s, w_s, acc_s, sq_s, x_sem, w_sem, in_sem, q_sem, out_sem = refs

    for n, (which, block, offsets, absolute) in enumerate(pieces):
        lanes = pl.ds(n * HALF, HALF)
        for y in range(NY):
            if absolute:
                source = x_refs[which].at[y, block]
                place = y
            else:
                source = x_refs[which].at[block, y]
                place = lax.rem(at_ref[0] + y, NY)
            pltpu.make_async_copy(source, x_s.at[place, :, lanes], x_sem).start()
    starts = []
    for _, block, offsets, absolute in pieces:
        index = block if absolute else tensor_index(at_ref, *offsets)
        starts.append(pl.multiple_of(index * COLS + (HALF if absolute else 0), HALF))
    for tile in range(TILES):
        w_ref = wo_ref if tile < TILES // 2 else ws_ref
        columns = pl.ds(tile % (TILES // 2) * TILE, TILE)
        for n, start in enumerate(starts):
            pltpu.make_async_copy(
                w_ref.at[pl.ds(start, HALF), columns],
                w_s.at[tile, pl.ds(n * HALF, HALF), :],
                w_sem.at[tile],
            ).start()
        if not first:
            pltpu.make_async_copy(sums_ref.at[tile], acc_s.at[tile], in_sem.at[tile]).start()
    if not first:
        pltpu.make_async_copy(square_ref, sq_s, q_sem).start()
        pltpu.make_async_copy(square_ref, sq_s, q_sem).wait()
    pltpu.make_async_copy(x_s, x_s, x_sem).wait()

    def one(tile, carry):
        pltpu.make_async_copy(w_s.at[tile], w_s.at[tile], w_sem.at[tile]).wait()
        x = x_s[...].reshape(512, len(pieces) * HALF)
        part = jnp.dot(x, w_s[tile], preferred_element_type=F32)
        if first:
            acc_s[tile] = part
        else:
            pltpu.make_async_copy(sums_ref.at[tile], acc_s.at[tile], in_sem.at[tile]).wait()
            acc_s[tile] += part
        if not last:
            pltpu.make_async_copy(acc_s.at[tile], out_ref.at[tile], out_sem.at[tile]).start()
        return carry

    lax.fori_loop(0, TILES, one, 0)

    square = jnp.zeros((512, HD), F32) if first else sq_s[...]
    for n, start in enumerate(starts):
        for j in range(HALF // HD):
            piece = x_s[:, :, n * HALF + j * HD : n * HALF + (j + 1) * HD].reshape(512, HD).astype(F32)
            inverse = inv_ref[:, pl.ds(pl.multiple_of(start + j * HD, HD), HD)]
            square = square + piece * piece * inverse
    if not last:
        sq_s[...] = square
        pltpu.make_async_copy(sq_s, squares_ref, q_sem).start()
        pltpu.make_async_copy(sq_s, squares_ref, q_sem).wait()
        for tile in range(TILES):
            pltpu.make_async_copy(acc_s.at[tile], out_ref.at[tile], out_sem.at[tile]).wait()
        return

    mean = jnp.sum(square, axis=1, keepdims=True) * (1.0 / WIDTH)
    factor = lax.rsqrt(mean + EPS)
    peak = acc_s[0]
    for tile in range(1, TILES):
        peak = jnp.maximum(peak, acc_s[tile])
    peak = jnp.max(peak, axis=1, keepdims=True) * factor
    total = jnp.exp(acc_s[0] * factor - peak)
    for tile in range(1, TILES):
        total = total + jnp.exp(acc_s[tile] * factor - peak)
    lse = peak + jnp.log(jnp.sum(total, axis=1, keepdims=True))
    sq_s[...] = jnp.broadcast_to(lse, (512, HD))
    lse_ref[...] = jnp.transpose(sq_s[...])[0:1, :]
    for y in range(NY):
        a, b, c = y * 128, y * 128 + REQ, y * 128 + 128
        expert = (1.0 + BETA) * factor[a:b]
        amateur = BETA * factor[b:c]
        for tile in range(TILES):
            u_ref = uo_ref if tile < TILES // 2 else us_ref
            lanes = slice(tile % (TILES // 2) * TILE, (tile % (TILES // 2) + 1) * TILE)
            u_ref[y * REQ : (y + 1) * REQ, lanes] = (
                expert * acc_s[tile, a:b, :] - amateur * acc_s[tile, b:c, :]
            )


def head_part(place, arrays, pieces, inverse, w_own, w_sib, sums=None, last=False):
    first = sums is None
    depth = len(pieces) * HALF
    near = pl.BlockSpec(memory_space=pltpu.VMEM)
    far = pl.BlockSpec(memory_space=pl.ANY)
    partial = [(TILES, 512, TILE), (512, HD)]
    shapes = [(NY * REQ, VOC), (NY * REQ, VOC), (1, 512)] if last else partial
    dma = pltpu.SemaphoreType.DMA
    return pl.pallas_call(
        lambda *refs: head_kernel(pieces, first, last, *refs),
        in_specs=[pl.BlockSpec(memory_space=pltpu.SMEM), near]
        + [far] * (len(arrays) + 2 + (0 if first else 2)),
        out_specs=[near] * 3 if last else [far] * 2,
        out_shape=[jax.ShapeDtypeStruct(shape, F32) for shape in shapes],
        scratch_shapes=[
            pltpu.VMEM((NY, 128, depth), BF16),
            pltpu.VMEM((TILES, depth, TILE), BF16),
            pltpu.VMEM((TILES, 512, TILE), F32),
            pltpu.VMEM((512, HD), F32),
            dma,
            dma((TILES,)),
            dma((TILES,)),
            dma,
        ]
        + ([] if last else [dma((TILES,))]),
        compiler_params=params(56),
        cost_estimate=pl.CostEstimate(
            flops=2 * 512 * depth * 2 * VOC,
            bytes_accessed=depth * 4096 + (3 if first else 6) * MIB,
            transcendentals=786432 if last else 0,
        ),
    )(place, inverse, *arrays, w_own, w_sib, *(sums or ()))


def contrast_kernel(core_ref, uo_ref, us_ref, no_ref, ns_ref, o_ref):
    core = core_ref[0]
    for u_ref, n_ref, parity in ((uo_ref, no_ref, core), (us_ref, ns_ref, 1 - core)):
        column = jnp.transpose(jnp.broadcast_to(n_ref[...], (HD, 512)))
        for y in range(NY):
            a, b, c = y * 128, y * 128 + REQ, y * 128 + 128
            shift = (1.0 + BETA) * column[a:b] - BETA * column[b:c]
            rows = pl.ds(pl.multiple_of((2 * y + parity) * REQ, REQ), REQ)
            for j in range(VOC // HD):
                lanes = slice(j * HD, (j + 1) * HD)
                o_ref[rows, lanes] = u_ref[y * REQ : (y + 1) * REQ, lanes] - shift


def contrast(core, u_own, u_sib, norm_own, norm_sib):
    near = pl.BlockSpec(memory_space=pltpu.VMEM)
    return pl.pallas_call(
        contrast_kernel,
        in_specs=[pl.BlockSpec(memory_space=pltpu.SMEM)] + [near] * 4,
        out_specs=near,
        out_shape=jax.ShapeDtypeStruct((512, VOC), F32),
        compiler_params=params(16),
        cost_estimate=pl.CostEstimate(flops=10**6, bytes_accessed=4 * MIB, transcendentals=65536),
    )(core, u_own, u_sib, norm_own, norm_sib)


TENSOR = ("x", "z")
SWAP = [(0, 1), (1, 0)]


def combine(lse):
    peak = lse[0]
    for part in lse[1:]:
        peak = jnp.maximum(peak, part)
    total = jnp.exp(lse[0] - peak)
    for part in lse[1:]:
        total = total + jnp.exp(part - peak)
    return peak + jnp.log(total)


def from_offset(array, axis, offset):
    return lax.ppermute(array, axis, [((i + offset) % 4, i) for i in range(4)])


def from_core_offset(array, axes, offset):
    pairs = []
    for c in range(2):
        for x in range(4):
            for z in range(4):
                far_x = (x + offset) % 4 if axes[c] == "x" else x
                far_z = (z + offset) % 4 if axes[c] == "z" else z
                pairs.append((c * 16 + far_x * 4 + far_z, c * 16 + x * 4 + z))
    return lax.ppermute(array, ("c", "x", "z"), pairs)


FIRST = ("x", "z")
SECOND = ("z", "x")


def opposite(after, before, axes):
    half = after.shape[0] // 2
    return from_core_offset(after[:half], axes, 1), from_core_offset(before[half:], axes, 3)


def per_device(
    queries,
    cached_key_rows,
    cached_value_rows,
    current_token_key,
    current_token_value,
    lengths,
    residual,
    output_projection_weight,
    request_adapter_index,
    lowrank_down_factors,
    lowrank_up_factors,
    final_norm_scale,
    vocabulary_head_matrix,
):
    core = lax.axis_index("c").astype(jnp.int32).reshape(1)
    place = jnp.stack([lax.axis_index(axis) for axis in ("y", "x", "z", "c")]).astype(jnp.int32)
    head_sib = lax.ppermute(vocabulary_head_matrix, "c", SWAP)
    down = lax.all_gather(lowrank_down_factors, ("y", "c"), axis=0, tiled=True)
    up_after = from_offset(lowrank_up_factors, "y", 1)
    up_before = from_offset(lowrank_up_factors, "y", 3)
    owner = request_adapter_index // HELD
    slots = ((owner // 2 - place[0]) % NY) * HELD + request_adapter_index % HELD
    slots = slots + jnp.where(owner % 2 == place[3], 0, NY * HELD)
    gain = lax.dynamic_slice(final_norm_scale, (lax.axis_index(TENSOR) * COLS,), (COLS,))
    inverse = 1.0 / final_norm_scale.astype(F32)
    inverse = (inverse * inverse).reshape(1, WIDTH)

    sent = attention(
        queries,
        cached_key_rows,
        cached_value_rows,
        current_token_key,
        current_token_value,
        lengths,
        residual,
    )
    got = lax.all_to_all(sent, TENSOR, split_axis=0, concat_axis=0, tiled=True)
    partial = projection(got, output_projection_weight)
    up_after, up_before, partial = lax.optimization_barrier((up_after, up_before, partial))
    sums = lax.all_to_all(partial, TENSOR, split_axis=0, concat_axis=0, tiled=True)
    half = HELD // 2
    up_own = jnp.concatenate(
        [
            lowrank_up_factors,
            up_after,
            from_offset(up_after[:half], "y", 1),
            from_offset(up_before[half:], "y", 3),
            up_before,
        ],
        axis=0,
    )
    up_sib = lax.ppermute(up_own, "c", SWAP)
    rank = rank_sums(request_adapter_index, got, down)
    rank = sum([from_offset(rank, "x", d) for d in range(1, 4)], rank)
    rank = [rank] + [from_offset(rank, "z", d) for d in range(1, 4)]
    own, rest = hidden_slice(slots, sums, rank, got, gain.reshape(1, COLS), up_own, up_sib)

    gathered = lax.all_gather(rest, ("y", "x", "z"), axis=0, tiled=False)
    gathered = gathered.reshape(NY, TEN, 128, HALF)
    plane = jnp.stack([own] + [from_offset(own, "y", d) for d in range(1, 4)])
    after = from_core_offset(plane, FIRST, 1)
    before = from_core_offset(plane, FIRST, 3)
    far = opposite(after, before, FIRST)
    mine = jnp.stack([plane, after, jnp.concatenate(far, axis=0), before])
    after = from_core_offset(mine, SECOND, 1)
    before = from_core_offset(mine, SECOND, 3)
    weights = (inverse, vocabulary_head_matrix, head_sib)
    pieces = [(0, n, (n, 0), False) for n in range(4)]
    partial = head_part(place, [mine], pieces, *weights)
    after, before, *partial = lax.optimization_barrier((after, before, *partial))
    far = opposite(after, before, SECOND)
    pieces = [(n // 4, n % 4, (n % 4, 1 + 2 * (n // 4)), False) for n in range(8)]
    partial = head_part(place, [after, before], pieces, *weights, sums=partial)
    pieces = [(n // 2, n % 2, (n, 2), False) for n in range(4)]
    partial = head_part(place, far, pieces, *weights, sums=partial)
    pieces = [(0, n, None, True) for n in range(TEN)]
    u_own, u_send, lse = head_part(place, [gathered], pieces, *weights, sums=partial, last=True)
    for axis in ("y", "x", "z"):
        lse = combine([lse] + [from_offset(lse, axis, d) for d in range(1, 4)])
        if axis == "y":
            u_send, lse = lax.optimization_barrier((u_send, lse))
            u_sib = lax.ppermute(u_send, "c", SWAP)
    return contrast(core, u_own, u_sib, lse, lax.ppermute(lse, "c", SWAP))


def solution(mesh):
    fine = Mesh(np.asarray(mesh.devices).reshape(NY, 2, 4, 4), ("y", "c", "x", "z"))
    every = ("y", "c", "x", "z")
    group = ("y", "c")
    in_specs = (
        P(every, None, None),
        P(every, None, None, None),
        P(every, None, None, None),
        P(every, None, None),
        P(every, None, None),
        P(every),
        P(every, None, None),
        P(TENSOR, None),
        P(group),
        P(group, None, TENSOR),
        P(group, None, TENSOR),
        P(),
        P(None, every),
    )
    return jax.shard_map(
        per_device, mesh=fine, in_specs=in_specs, out_specs=P(None, every), check_vma=False
    )
```

time: 536 us -> 239 us (0.45)
  blocking collectives: 185 us -> 15.3 us
  waiting for transfers between devices: 204 us -> 87.4 us
  matrix products: 72.3 us -> 0 us
  Pallas kernels: 0 us -> 63.3 us
  starting transfers between devices: 9.15 us -> 48.8 us
  local copies, waits for them, and re-layouts: 37.8 us -> 6.81 us
  other arithmetic: 10.3 us -> 2.93 us
    psum x2 -> x0, blocking collectives: 120 us -> none  [the longest x1 64 us: per_device(): lax.psum(jnp.sum(jnp.exp(logits - highest[..., None]), axis=-1), ('replic...]
    unnamed x5 -> x2, waiting for transfers between devices: 116 us -> 0.73 us
    ppermute x0 -> x34, waiting for transfers between devices: none -> 75.8 us  [the longest x22 57.3 us: from_offset(): return lax.ppermute(array, axis, [((i + offset) % 4, i) for i in range(4)])]
    dot_general x9 -> x0, matrix products: 72.3 us -> none  [the longest x1 40.6 us: per_device(): jnp.einsum('rbd,dv->rbv', lax.all_gather(normed, ('replica', 'tensor'), a...]
    all_gather x3 -> x2, waiting for transfers between devices: 81.3 us -> 10.9 us  [the longest x1 10.6 us: per_device(): gathered = lax.all_gather(rest, ('y', 'x', 'z'), axis=0, tiled=False)]
    pmax x1 -> x0, blocking collectives: 64.5 us -> none  [per_device(): highest = lax.pmax(local_peak, ('replica', 'tensor'))]
    pallas_call x0 -> x9, Pallas kernels: none -> 63.3 us  [the longest x4 44.7 us: head_part(): pl.pallas_call(lambda *refs: head_kernel(pieces, first, last, *refs), in_...]
    ppermute x0 -> x34, starting transfers between devices: none -> 43.3 us  [the longest x22 19.5 us: from_offset(): return lax.ppermute(array, axis, [((i + offset) % 4, i) for i in range(4)])]
  transfers between devices with their start and end apart: 5 -> 37, of which waited for: 3 -> 26; matrix products, arithmetic and copies ran while one was open for 11% -> 3% of each run, Pallas kernels for 0% -> 18%
where the time goes in v1:
time: 239 us; the launch traced here: 238 us
  waiting for transfers between devices  87.4 us (37%)
  Pallas kernels  63.3 us (26%)
  starting transfers between devices  48.8 us (20%)
  blocking collectives  15.3 us (6%)
  between operations  13.7 us (6%)
  local copies, waits for them, and re-layouts  6.81 us (3%)
  other arithmetic  2.93 us (1%)
    ppermute x22, waiting for transfers between devices, from_offset(): return lax.ppermute(array, axis, [((i + offset) % 4, i) for i in range(4)])  57.3 us
    pallas_call x4, Pallas kernels, head_part(): pl.pallas_call(lambda *refs: head_kernel(pieces, first, last, *refs), in_...  44.7 us
    ppermute x22, starting transfers between devices, from_offset(): return lax.ppermute(array, axis, [((i + offset) % 4, i) for i in range(4)])  19.5 us
    ppermute x8, waiting for transfers between devices, from_core_offset(): return lax.ppermute(array, ('c', 'x', 'z'), pairs)  17.7 us
    all_to_all x1, blocking collectives, per_device(): got = lax.all_to_all(sent, TENSOR, split_axis=0, concat_axis=0, tiled=True)  15.3 us
    all_gather x1, waiting for transfers between devices, per_device(): gathered = lax.all_gather(rest, ('y', 'x', 'z'), axis=0, tiled=False)  10.6 us
    ppermute x1, starting transfers between devices, per_device(): u_sib = lax.ppermute(u_send, 'c', SWAP)  8.53 us
    ppermute x8, starting transfers between devices, from_core_offset(): return lax.ppermute(array, ('c', 'x', 'z'), pairs)  7.27 us
  transfers between devices with their start and end apart: 37, of which 26 were waited for; matrix products, arithmetic and copies ran while one was open for 3% of the time, Pallas kernels for 18%

profile of v1, /device:TPU:1, one launch (start us, length us, event | category | flops | bytes accessed | tf_op | source)
XLA Modules:
  0.0 238.2 jit_solution(15388901505366673417)
XLA Ops:
  8.8 2.8 %collective-permute-start = (bf16[48,16,512]{2,1,0:T(8,128)(2,1)}, bf16[48,16,512]{2,1,0:T(8,128)(2,1)S(1)}, u32[]{:S(2)}, u32[]{:S(2)}) collective-permute-start(bf16[48,16,512]{2,1,0:T(8,128)(2,1)} %param.23), channel_id=1, source_target_pairs={{32,0},{64,32},{96,64},{0,96},{33,1},{65,33},{97,65},{1,97},{34,2}... | collective-permute-start | bytes 2359304 | tf_op jit(solution)/shard_map/ppermute | solution.py:422
  11.6 5.0 %shard_map.127 = bf16[16,16,512]{2,1,0:T(8,128)(2,1)} custom-call(s32[4]{0:T(128)} %len_ref.1, bf16[4,2,8192]{2,1,0:T(2,128)(2,1)} %q_ref.1, bf16[4,2,64,1024]{3,2,1,0:T(8,128)(2,1)} %k_ref.1, bf16[4,2,64,1024]{3,2,1,0:T(8,128)(2,1)} %v_ref.1, bf16[4,2,1024]{2,1,0:T(2,128)(2,1)} %ck_ref.1, bf16[4,2,1024]{2,1,0:T(2,128)(2,1)} %cv_ref.1, ...), custom_call_target="tpu_custom_call" | custom-call | flops 300000000 | bytes 3145728 | tf_op jit(solution)/shard_map/pallas_call | solution.py:81
  16.6 15.3 %all_to_all.10.got_ref = bf16[16,16,512]{2,1,0:T(8,128)(2,1)} all-to-all(bf16[16,16,512]{2,1,0:T(8,128)(2,1)} %shard_map.127), channel_id=1, replica_groups=mesh['y'=4,'c'=2,'x'=4,'z'=4] {'x','z'}, dimensions={0} | all-to-all | bytes 524288 | tf_op jit(solution)/shard_map/all_to_all | solution.py:482
  31.9 6.2 %shard_map.128 = bf16[16,128,512]{2,1,0:T(8,128)(2,1)} custom-call(bf16[16,16,512]{2,1,0:T(8,128)(2,1)} %all_to_all.10.got_ref, bf16[512,8192]{1,0:T(8,128)(2,1)} %w_ref.1), custom_call_target="tpu_custom_call" | custom-call | flops 1100000000 | bytes 11534336 | tf_op jit(solution)/shard_map/pallas_call | solution.py:152
  38.1 2.5 %collective-permute-start.8 = (bf16[24,16,512]{2,1,0:T(8,128)(2,1)S(1)}, bf16[24,16,512]{2,1,0:T(8,128)(2,1)S(1)}, u32[]{:S(2)}, u32[]{:S(2)}) collective-permute-start(bf16[24,16,512]{2,1,0:T(8,128)(2,1)S(1)} %slice.18), channel_id=1, source_target_pairs={{32,0},{64,32},{96,64},{0,96},{33,1},{65,33},{97,65},{1,97},{34,2}... | collective-permute-start | bytes 1179656 | tf_op jit(solution)/shard_map/ppermute | solution.py:422
  42.6 14.5 %collective-permute-done.8 = bf16[24,16,512]{2,1,0:T(8,128)(2,1)S(1)} collective-permute-done((bf16[24,16,512]{2,1,0:T(8,128)(2,1)S(1)}, bf16[24,16,512]{2,1,0:T(8,128)(2,1)S(1)}, u32[]{:S(2)}, u32[]{:S(2)}) %collective-permute-start.8) | collective-permute-done | bytes 393248 | tf_op jit(solution)/shard_map/ppermute | solution.py:422
  57.9 2.8 %collective-permute-done.9 = bf16[24,16,512]{2,1,0:T(8,128)(2,1)S(1)} collective-permute-done((bf16[24,16,512]{2,1,0:T(8,128)(2,1)S(1)}, bf16[24,16,512]{2,1,0:T(8,128)(2,1)S(1)}, u32[]{:S(2)}, u32[]{:S(2)}) %collective-permute-start.9) | collective-permute-done | bytes 393248 | tf_op jit(solution)/shard_map/ppermute | solution.py:422
  62.4 3.2 %collective-permute-start.10 = (bf16[192,16,512]{2,1,0:T(8,128)(2,1)}, bf16[192,16,512]{2,1,0:T(8,128)(2,1)}, u32[]{:S(2)}, u32[]{:S(2)}) collective-permute-start(bf16[192,16,512]{2,1,0:T(8,128)(2,1)} %constant_dynamic-update-slice_fusion.own_ref), channel_id=1, source_target_pairs={{0,16},{16,0},{1,17},{17,1},{2,18},{18,2},{3,19},{19,3},{4,20},{20... | collective-permute-start | bytes 9437192 | tf_op jit(solution)/shard_map/ppermute | solution.py:497
  65.6 5.5 %all-to-all-start.1 = ((bf16[16,128,512]{2,1,0:T(8,128)(2,1)}), bf16[16,128,512]{2,1,0:T(8,128)(2,1)S(1)}, u32[]{:S(2)}, u32[]{:S(2)}) async-start(bf16[16,128,512]{2,1,0:T(8,128)(2,1)} %shard_map.128), calls=%async_computation.1 | async-start | bytes 4194304 | tf_op jit(solution)/shard_map/all_to_all | solution.py:485
  71.4 3.2 %shard_map.129 = f32[1,1024]{1,0:T(1,128)} custom-call(s32[64]{0:T(128)} %idx_ref.1, bf16[16,16,512]{2,1,0:T(8,128)(2,1)} %all_to_all.10.got_ref, bf16[384,16,512]{2,1,0:T(8,128)(2,1)} %all-gather.4.cloned.1.call-done.table_ref), custom_call_target="tpu_custom_call" | custom-call | flops 140000000 | bytes 2097152 | tf_op jit(solution)/shard_map/pallas_call | solution.py:179
  78.2 18.1 %collective-permute-done.2 = f32[1,1024]{1,0:T(1,128)S(1)} collective-permute-done((f32[1,1024]{1,0:T(1,128)}, f32[1,1024]{1,0:T(1,128)S(1)}, u32[]{:S(2)}, u32[]{:S(2)}) %collective-permute-start.2) | collective-permute-done | bytes 4128 | tf_op jit(solution)/shard_map/ppermute | solution.py:422
  96.3 3.8 %collective-permute-done.3 = f32[1,1024]{1,0:T(1,128)S(1)} collective-permute-done((f32[1,1024]{1,0:T(1,128)}, f32[1,1024]{1,0:T(1,128)S(1)}, u32[]{:S(2)}, u32[]{:S(2)}) %collective-permute-start.3) | collective-permute-done | bytes 4128 | tf_op jit(solution)/shard_map/ppermute | solution.py:422
  107.3 2.9 %shard_map.130 = (bf16[128,256]{1,0:T(8,128)(2,1)S(1)}, bf16[128,256]{1,0:T(8,128)(2,1)}) custom-call(s32[64]{0:T(128)S(1)} %fusion.1.slot_ref, bf16[16,128,512]{2,1,0:T(8,128)(2,1)S(1)} %all-to-all-done.1.sums_ref, f32[1,1024]{1,0:T(1,128)S(1)} %add_add_fusion.k0_ref, f32[1,1024]{1,0:T(1,128)S(1)} %collective-permute-done.5.k1_ref, ...), custom_call_target="tpu_custom_call" | custom-call | flops 300000000 | bytes 4194304 | tf_op jit(solution)/shard_map/pallas_call | solution.py:230
  118.4 3.8 %collective-permute-done.15 = bf16[4,128,256]{2,1,0:T(8,128)(2,1)S(1)} collective-permute-done((bf16[4,128,256]{2,1,0:T(8,128)(2,1)S(1)}, bf16[4,128,256]{2,1,0:T(8,128)(2,1)S(1)}, u32[]{:S(2)}, u32[]{:S(2)}) %collective-permute-start.15) | collective-permute-done | bytes 262176 | tf_op jit(solution)/shard_map/ppermute | solution.py:433
  126.3 2.7 %collective-permute-done.18 = bf16[2,128,256]{2,1,0:T(8,128)(2,1)S(1)} collective-permute-done((bf16[2,128,256]{2,1,0:T(8,128)(2,1)S(1)}, bf16[2,128,256]{2,1,0:T(8,128)(2,1)S(1)}, u32[]{:S(2)}, u32[]{:S(2)}) %collective-permute-start.18) | collective-permute-done | bytes 131104 | tf_op jit(solution)/shard_map/ppermute | solution.py:433
  132.6 6.8 %shard_map.131 = (f32[6,512,256]{2,1,0:T(8,128)}, f32[512,128]{1,0:T(8,128)}) custom-call(s32[4]{0:T(128)} %pad_add_fusion.refs_0_, f32[1,8192]{1,0:T(1,128)} %bitcast.18, bf16[4,4,128,256]{3,2,1,0:T(8,128)(2,1)} %copy-done.2, bf16[8192,768]{1,0:T(8,128)(2,1)} %refs_3_.3, bf16[8192,768]{1,0:T(8,128)(2,1)} %collective-permute-done.11.refs_4_.refs_5_), custom_call_target="tpu_custom_call" | custom-call | flops 1610612736 | bytes 7340032 | tf_op jit(solution)/shard_map/pallas_call | solution.py:356
  139.4 5.9 %collective-permute-done.19.refs_2_ = bf16[4,4,128,256]{3,2,1,0:T(8,128)(2,1)S(1)} collective-permute-done((bf16[4,4,128,256]{3,2,1,0:T(8,128)(2,1)S(1)}, bf16[4,4,128,256]{3,2,1,0:T(8,128)(2,1)S(1)}, u32[]{:S(2)}, u32[]{:S(2)}) %collective-permute-start.19) | collective-permute-done | bytes 1048608 | tf_op jit(solution)/shard_map/ppermute | solution.py:433
  145.3 3.1 %collective-permute-done.20.refs_3_ = bf16[4,4,128,256]{3,2,1,0:T(8,128)(2,1)S(1)} collective-permute-done((bf16[4,4,128,256]{3,2,1,0:T(8,128)(2,1)S(1)}, bf16[4,4,128,256]{3,2,1,0:T(8,128)(2,1)S(1)}, u32[]{:S(2)}, u32[]{:S(2)}) %collective-permute-start.20) | collective-permute-done | bytes 1048608 | tf_op jit(solution)/shard_map/ppermute | solution.py:433
  150.1 11.4 %shard_map.132 = (f32[6,512,256]{2,1,0:T(8,128)}, f32[512,128]{1,0:T(8,128)}) custom-call(s32[4]{0:T(128)} %pad_add_fusion.refs_0_, f32[1,8192]{1,0:T(1,128)} %bitcast.19, bf16[4,4,128,256]{3,2,1,0:T(8,128)(2,1)} %copy-done.3, bf16[4,4,128,256]{3,2,1,0:T(8,128)(2,1)} %copy-done.4, bf16[8192,768]{1,0:T(8,128)(2,1)} %refs_3_.3, ...), custom_call_target="tpu_custom_call" | custom-call | flops 3221225472 | bytes 14680064 | tf_op jit(solution)/shard_map/pallas_call | solution.py:356
  162.5 8.1 %shard_map.133 = (f32[6,512,256]{2,1,0:T(8,128)}, f32[512,128]{1,0:T(8,128)}) custom-call(s32[4]{0:T(128)} %pad_add_fusion.refs_0_, f32[1,8192]{1,0:T(1,128)} %bitcast.20, bf16[2,4,128,256]{3,2,1,0:T(8,128)(2,1)} %copy-done.6, bf16[2,4,128,256]{3,2,1,0:T(8,128)(2,1)} %copy-done.7, bf16[8192,768]{1,0:T(8,128)(2,1)} %refs_3_.3, ...), custom_call_target="tpu_custom_call" | custom-call | flops 1610612736 | bytes 10485760 | tf_op jit(solution)/shard_map/pallas_call | solution.py:356
  170.7 10.6 %all-gather.6.cloned.1.call-done = bf16[8192,256]{1,0:T(8,128)(2,1)} async-done(((bf16[128,256]{1,0:T(8,128)(2,1)}), bf16[8192,256]{1,0:T(8,128)(2,1)}) %all-gather.6.cloned.1.call-update) | async-done | bytes 4194320 | tf_op jit(solution)/shard_map/all_gather | solution.py:503
  181.2 18.4 %shard_map.134 = (f32[256,768]{1,0:T(8,128)}, f32[256,768]{1,0:T(8,128)}, f32[1,512]{1,0:T(1,128)}) custom-call(s32[4]{0:T(128)} %pad_add_fusion.refs_0_, f32[1,8192]{1,0:T(1,128)} %bitcast.21, bf16[4,16,128,256]{3,2,1,0:T(8,128)(2,1)} %bitcast.17, bf16[8192,768]{1,0:T(8,128)(2,1)} %refs_3_.3, bf16[8192,768]{1,0:T(8,128)(2,1)} %collective-permute-done.11.refs_4_.refs_5_, ...), custom_call_target="tpu_custom_call" | custom-call | flops 6442450944 | bytes 23068672 | tf_op jit(solution)/shard_map/pallas_call | solution.py:356
  205.9 8.5 %collective-permute-start.26 = (f32[256,768]{1,0:T(8,128)}, f32[256,768]{1,0:T(8,128)S(1)}, u32[]{:S(2)}, u32[]{:S(2)}) collective-permute-start(f32[256,768]{1,0:T(8,128)} %get-tuple-element.43), channel_id=1, source_target_pairs={{0,16},{16,0},{1,17},{17,1},{2,18},{18,2},{3,19},{19,3},{4,20},{20... | collective-permute-start | bytes 2359304 | tf_op jit(solution)/shard_map/ppermute | solution.py:527
  224.7 3.3 %collective-permute-start.33 = (f32[1,512]{1,0:T(1,128)S(1)}, f32[1,512]{1,0:T(1,128)S(1)}, u32[]{:S(2)}, u32[]{:S(2)}) collective-permute-start(f32[1,512]{1,0:T(1,128)S(1)} %log_add_fusion.no_ref), channel_id=1, source_target_pairs={{0,16},{16,0},{1,17},{17,1},{2,18},{18,2},{3,19},{19,3},{4,20},{20... | collective-permute-start | bytes 6152 | tf_op jit(solution)/shard_map/ppermute | solution.py:528
  (105 shorter events, 56.3 us)
Async XLA Ops:
  6.5 64.9 %all-gather.4.cloned.1.call-start = ((), (), s32[]{:S(2)}) async-start(), calls=%async_computation.2 | async-start | bytes 7077888 | tf_op jit(solution)/shard_map/all_gather | solution.py:463
  7.3 125.4 %collective-permute-start.11 = (bf16[8192,768]{1,0:T(8,128)(2,1)}, bf16[8192,768]{1,0:T(8,128)(2,1)}, u32[]{:S(2)}, u32[]{:S(2)}) collective-permute-start(bf16[8192,768]{1,0:T(8,128)(2,1)} %refs_3_.3), channel_id=1, source_target_pairs={{0,16},{16,0},{1,17},{17,1},{2,18},{18,2},{3,19},{19,3},{4,20},{20... | collective-permute-start | bytes 37748744 | tf_op jit(solution)/shard_map/ppermute | solution.py:462
  8.8 29.3 %collective-permute-start = (bf16[48,16,512]{2,1,0:T(8,128)(2,1)}, bf16[48,16,512]{2,1,0:T(8,128)(2,1)S(1)}, u32[]{:S(2)}, u32[]{:S(2)}) collective-permute-start(bf16[48,16,512]{2,1,0:T(8,128)(2,1)} %param.23), channel_id=1, source_target_pairs={{32,0},{64,32},{96,64},{0,96},{33,1},{65,33},{97,65},{1,97},{34,2}... | collective-permute-start | bytes 2359304 | tf_op jit(solution)/shard_map/ppermute | solution.py:422
  11.6 26.5 %collective-permute-start.1 = (bf16[48,16,512]{2,1,0:T(8,128)(2,1)}, bf16[48,16,512]{2,1,0:T(8,128)(2,1)S(1)}, u32[]{:S(2)}, u32[]{:S(2)}) collective-permute-start(bf16[48,16,512]{2,1,0:T(8,128)(2,1)} %param.23), channel_id=1, source_target_pairs={{96,0},{0,32},{32,64},{64,96},{97,1},{1,33},{33,65},{65,97},{98,2}... | collective-permute-start | bytes 2359304 | tf_op jit(solution)/shard_map/ppermute | solution.py:422
  38.1 19.0 %collective-permute-start.8 = (bf16[24,16,512]{2,1,0:T(8,128)(2,1)S(1)}, bf16[24,16,512]{2,1,0:T(8,128)(2,1)S(1)}, u32[]{:S(2)}, u32[]{:S(2)}) collective-permute-start(bf16[24,16,512]{2,1,0:T(8,128)(2,1)S(1)} %slice.18), channel_id=1, source_target_pairs={{32,0},{64,32},{96,64},{0,96},{33,1},{65,33},{97,65},{1,97},{34,2}... | collective-permute-start | bytes 1179656 | tf_op jit(solution)/shard_map/ppermute | solution.py:422
  40.7 19.9 %collective-permute-start.9 = (bf16[24,16,512]{2,1,0:T(8,128)(2,1)S(1)}, bf16[24,16,512]{2,1,0:T(8,128)(2,1)S(1)}, u32[]{:S(2)}, u32[]{:S(2)}) collective-permute-start(bf16[24,16,512]{2,1,0:T(8,128)(2,1)S(1)} %slice.19), channel_id=1, source_target_pairs={{96,0},{0,32},{32,64},{64,96},{97,1},{1,33},{33,65},{65,97},{98,2}... | collective-permute-start | bytes 1179656 | tf_op jit(solution)/shard_map/ppermute | solution.py:422
  62.4 41.4 %collective-permute-start.10 = (bf16[192,16,512]{2,1,0:T(8,128)(2,1)}, bf16[192,16,512]{2,1,0:T(8,128)(2,1)}, u32[]{:S(2)}, u32[]{:S(2)}) collective-permute-start(bf16[192,16,512]{2,1,0:T(8,128)(2,1)} %constant_dynamic-update-slice_fusion.own_ref), channel_id=1, source_target_pairs={{0,16},{16,0},{1,17},{17,1},{2,18},{18,2},{3,19},{19,3},{4,20},{20... | collective-permute-start | bytes 9437192 | tf_op jit(solution)/shard_map/ppermute | solution.py:497
  65.6 38.2 %all-to-all-start.1 = ((bf16[16,128,512]{2,1,0:T(8,128)(2,1)}), bf16[16,128,512]{2,1,0:T(8,128)(2,1)S(1)}, u32[]{:S(2)}, u32[]{:S(2)}) async-start(bf16[16,128,512]{2,1,0:T(8,128)(2,1)} %shard_map.128), calls=%async_computation.1 | async-start | bytes 4194304 | tf_op jit(solution)/shard_map/all_to_all | solution.py:485
  71.1 110.2 %all-gather.6.cloned.1.call-start = ((), (), s32[]{:S(2)}) async-start(), calls=%async_computation.3 | async-start | bytes 4259840 | tf_op jit(solution)/shard_map/all_gather | solution.py:503
  74.6 21.7 %collective-permute-start.2 = (f32[1,1024]{1,0:T(1,128)}, f32[1,1024]{1,0:T(1,128)S(1)}, u32[]{:S(2)}, u32[]{:S(2)}) collective-permute-start(f32[1,1024]{1,0:T(1,128)} %shard_map.129), channel_id=1, source_target_pairs={{4,0},{8,4},{12,8},{0,12},{5,1},{9,5},{13,9},{1,13},{6,2},{10,6},{... | collective-permute-start | bytes 12296 | tf_op jit(solution)/shard_map/ppermute | solution.py:422
  77.1 23.0 %collective-permute-start.3 = (f32[1,1024]{1,0:T(1,128)}, f32[1,1024]{1,0:T(1,128)S(1)}, u32[]{:S(2)}, u32[]{:S(2)}) collective-permute-start(f32[1,1024]{1,0:T(1,128)} %shard_map.129), channel_id=1, source_target_pairs={{8,0},{12,4},{0,8},{4,12},{9,1},{13,5},{1,9},{5,13},{10,2},{14,6},... | collective-permute-start | bytes 12296 | tf_op jit(solution)/shard_map/ppermute | solution.py:422
  77.6 22.5 %collective-permute-start.4 = (f32[1,1024]{1,0:T(1,128)}, f32[1,1024]{1,0:T(1,128)S(1)}, u32[]{:S(2)}, u32[]{:S(2)}) collective-permute-start(f32[1,1024]{1,0:T(1,128)} %shard_map.129), channel_id=1, source_target_pairs={{12,0},{0,4},{4,8},{8,12},{13,1},{1,5},{5,9},{9,13},{14,2},{2,6},{... | collective-permute-start | bytes 12296 | tf_op jit(solution)/shard_map/ppermute | solution.py:422
  110.7 4.6 %collective-permute-start.13 = (bf16[128,256]{1,0:T(8,128)(2,1)S(1)}, bf16[128,256]{1,0:T(8,128)(2,1)S(1)}, u32[]{:S(2)}, u32[]{:S(2)}) collective-permute-start(bf16[128,256]{1,0:T(8,128)(2,1)S(1)} %get-tuple-element.29), channel_id=1, source_target_pairs={{64,0},{96,32},{0,64},{32,96},{65,1},{97,33},{1,65},{33,97},{66,2}... | collective-permute-start | bytes 196616 | tf_op jit(solution)/shard_map/ppermute | solution.py:422
  112.5 4.3 %collective-permute-start.14 = (bf16[128,256]{1,0:T(8,128)(2,1)S(1)}, bf16[128,256]{1,0:T(8,128)(2,1)S(1)}, u32[]{:S(2)}, u32[]{:S(2)}) collective-permute-start(bf16[128,256]{1,0:T(8,128)(2,1)S(1)} %get-tuple-element.29), channel_id=1, source_target_pairs={{96,0},{0,32},{32,64},{64,96},{97,1},{1,33},{33,65},{65,97},{98,2}... | collective-permute-start | bytes 196616 | tf_op jit(solution)/shard_map/ppermute | solution.py:422
  116.9 5.3 %collective-permute-start.15 = (bf16[4,128,256]{2,1,0:T(8,128)(2,1)S(1)}, bf16[4,128,256]{2,1,0:T(8,128)(2,1)S(1)}, u32[]{:S(2)}, u32[]{:S(2)}) collective-permute-start(bf16[4,128,256]{2,1,0:T(8,128)(2,1)S(1)} %get-tuple-element.46), channel_id=1, source_target_pairs={{4,0},{5,1},{6,2},{7,3},{8,4},{9,5},{10,6},{11,7},{12,8},{13,9},{1... | collective-permute-start | bytes 786440 | tf_op jit(solution)/shard_map/ppermute | solution.py:433
  116.9 6.5 %collective-permute-start.17 = (bf16[4,128,256]{2,1,0:T(8,128)(2,1)S(1)}, bf16[4,128,256]{2,1,0:T(8,128)(2,1)S(1)}, u32[]{:S(2)}, u32[]{:S(2)}) collective-permute-start(bf16[4,128,256]{2,1,0:T(8,128)(2,1)S(1)} %get-tuple-element.46), channel_id=1, source_target_pairs={{12,0},{13,1},{14,2},{15,3},{0,4},{1,5},{2,6},{3,7},{4,8},{5,9},{6... | collective-permute-start | bytes 786440 | tf_op jit(solution)/shard_map/ppermute | solution.py:433
  122.2 4.2 %collective-permute-start.16 = (bf16[2,128,256]{2,1,0:T(8,128)(2,1)S(1)}, bf16[2,128,256]{2,1,0:T(8,128)(2,1)S(1)}, u32[]{:S(2)}, u32[]{:S(2)}) collective-permute-start(bf16[2,128,256]{2,1,0:T(8,128)(2,1)S(1)} %slice.24), channel_id=1, source_target_pairs={{4,0},{5,1},{6,2},{7,3},{8,4},{9,5},{10,6},{11,7},{12,8},{13,9},{1... | collective-permute-start | bytes 393224 | tf_op jit(solution)/shard_map/ppermute | solution.py:433
  123.5 5.6 %collective-permute-start.18 = (bf16[2,128,256]{2,1,0:T(8,128)(2,1)S(1)}, bf16[2,128,256]{2,1,0:T(8,128)(2,1)S(1)}, u32[]{:S(2)}, u32[]{:S(2)}) collective-permute-start(bf16[2,128,256]{2,1,0:T(8,128)(2,1)S(1)} %slice.25), channel_id=1, source_target_pairs={{12,0},{13,1},{14,2},{15,3},{0,4},{1,5},{2,6},{3,7},{4,8},{5,9},{6... | collective-permute-start | bytes 393224 | tf_op jit(solution)/shard_map/ppermute | solution.py:433
  129.3 16.0 %collective-permute-start.19 = (bf16[4,4,128,256]{3,2,1,0:T(8,128)(2,1)S(1)}, bf16[4,4,128,256]{3,2,1,0:T(8,128)(2,1)S(1)}, u32[]{:S(2)}, u32[]{:S(2)}) collective-permute-start(bf16[4,4,128,256]{3,2,1,0:T(8,128)(2,1)S(1)} %pad_maximum_fusion.refs_2_), channel_id=1, source_target_pairs={{1,0},{2,1},{3,2},{0,3},{5,4},{6,5},{7,6},{4,7},{9,8},{10,9},{11,1... | collective-permute-start | bytes 3145736 | tf_op jit(solution)/shard_map/ppermute | solution.py:433
  130.8 17.6 %collective-permute-start.20 = (bf16[4,4,128,256]{3,2,1,0:T(8,128)(2,1)S(1)}, bf16[4,4,128,256]{3,2,1,0:T(8,128)(2,1)S(1)}, u32[]{:S(2)}, u32[]{:S(2)}) collective-permute-start(bf16[4,4,128,256]{3,2,1,0:T(8,128)(2,1)S(1)} %pad_maximum_fusion.refs_2_), channel_id=1, source_target_pairs={{3,0},{0,1},{1,2},{2,3},{7,4},{4,5},{5,6},{6,7},{11,8},{8,9},{9,10... | collective-permute-start | bytes 3145736 | tf_op jit(solution)/shard_map/ppermute | solution.py:433
  148.5 13.0 %collective-permute-start.21 = (bf16[2,4,128,256]{3,2,1,0:T(8,128)(2,1)S(1)}, bf16[2,4,128,256]{3,2,1,0:T(8,128)(2,1)S(1)}, u32[]{:S(2)}, u32[]{:S(2)}) collective-permute-start(bf16[2,4,128,256]{3,2,1,0:T(8,128)(2,1)S(1)} %slice.22), channel_id=1, source_target_pairs={{1,0},{2,1},{3,2},{0,3},{5,4},{6,5},{7,6},{4,7},{9,8},{10,9},{11,1... | collective-permute-start | bytes 1572872 | tf_op jit(solution)/shard_map/ppermute | solution.py:433
  148.6 12.9 %collective-permute-start.22 = (bf16[2,4,128,256]{3,2,1,0:T(8,128)(2,1)S(1)}, bf16[2,4,128,256]{3,2,1,0:T(8,128)(2,1)S(1)}, u32[]{:S(2)}, u32[]{:S(2)}) collective-permute-start(bf16[2,4,128,256]{3,2,1,0:T(8,128)(2,1)S(1)} %slice.23), channel_id=1, source_target_pairs={{3,0},{0,1},{1,2},{2,3},{7,4},{4,5},{5,6},{6,7},{11,8},{8,9},{9,10... | collective-permute-start | bytes 1572872 | tf_op jit(solution)/shard_map/ppermute | solution.py:433
  205.9 23.0 %collective-permute-start.26 = (f32[256,768]{1,0:T(8,128)}, f32[256,768]{1,0:T(8,128)S(1)}, u32[]{:S(2)}, u32[]{:S(2)}) collective-permute-start(f32[256,768]{1,0:T(8,128)} %get-tuple-element.43), channel_id=1, source_target_pairs={{0,16},{16,0},{1,17},{17,1},{2,18},{18,2},{3,19},{19,3},{4,20},{20... | collective-permute-start | bytes 2359304 | tf_op jit(solution)/shard_map/ppermute | solution.py:527
  214.4 4.9 %collective-permute-start.29 = (f32[1,512]{1,0:T(1,128)S(1)}, f32[1,512]{1,0:T(1,128)S(1)}, u32[]{:S(2)}, u32[]{:S(2)}) collective-permute-start(f32[1,512]{1,0:T(1,128)S(1)} %log_add_fusion.2), channel_id=1, source_target_pairs={{12,0},{0,4},{4,8},{8,12},{13,1},{1,5},{5,9},{9,13},{14,2},{2,6},{... | collective-permute-start | bytes 6152 | tf_op jit(solution)/shard_map/ppermute | solution.py:422
  (23 other events, 168.2 us)
Sparse Core Ops, SparseCore 0:
  9.0 62.3 all-gather.3
  110.3 70.8 all-gather.5

commit v2 on v1

--- a/solution.py
+++ b/solution.py
@@ -119,14 +119,14 @@
     lax.fori_loop(0, REQ, one, 0, unroll=4)
 
 
-def wait_rows(tables, rows_s, sem):
-    pltpu.make_async_copy(tables[0].at[pl.ds(0, REQ)], rows_s, sem).wait()
-
-
-def own_lanes(rows, lanes, first):
+def wait_rows(table_ref, rows_s, sem):
+    pltpu.make_async_copy(table_ref.at[pl.ds(0, REQ)], rows_s, sem).wait()
+
+
+def own_lanes(rows, lanes, pitch):
     row = lax.broadcasted_iota(jnp.int32, (rows, lanes), 0)
     lane = lax.broadcasted_iota(jnp.int32, (rows, lanes), 1)
-    return row == 2 * (lane // RANK + first)
+    return row == pitch * (lane // RANK)
 
 
 def attended_rows(got_ref):
@@ -167,10 +167,10 @@
 def rank_kernel(idx_ref, got_ref, table_ref, o_ref, rows_s, sem):
     start_rows(idx_ref, [table_ref], rows_s, sem)
     attended = attended_rows(got_ref)
-    wait_rows([table_ref], rows_s, sem)
+    wait_rows(table_ref, rows_s, sem)
     rows = rows_s[...].reshape(REQ * RANK, COLS)
     product = lax.dot_general(attended, rows, LAST, preferred_element_type=F32)
-    mask = own_lanes(128, REQ * RANK, 0)
+    mask = own_lanes(128, REQ * RANK, 2)
     o_ref[...] = jnp.sum(jnp.where(mask, product, 0.0), axis=0, keepdims=True)
 
 
@@ -191,59 +191,64 @@
     )(index, got, table)
 
 
-def hidden_kernel(
-    slot_ref, sums_ref, k0_ref, k1_ref, k2_ref, k3_ref, got_ref, gain_ref, own_ref, sib_ref,
-    oa_ref, ob_ref, rows_s, hid_s, sem,
-):
-    tables = [own_ref, sib_ref]
-    start_rows(slot_ref, tables, rows_s, sem)
+def sum_kernel(sums_ref, got_ref, gain_ref, expert_ref, amateur_ref, hid_s):
     total = sums_ref[0].astype(F32)
     for t in range(1, TEN):
         total = total + sums_ref[t].astype(F32)
+    total = total + got_ref[...].astype(F32)[:, 8:16, :].reshape(128, COLS)
+    for j in range(COLS // HD):
+        lanes = slice(j * HD, (j + 1) * HD)
+        hid_s[j] = total[:, lanes]
+        expert_ref[:, lanes] = hid_s[j, pl.ds(0, REQ, stride=2), :]
+        hidden = hid_s[j, pl.ds(1, REQ, stride=2), :].astype(BF16).astype(F32)
+        amateur_ref[:, lanes] = (hidden * gain_ref[:, lanes].astype(F32)).astype(BF16)
+
+
+def summed_rows(sums, got, gain):
+    near = pl.BlockSpec(memory_space=pltpu.VMEM)
+    return pl.pallas_call(
+        sum_kernel,
+        in_specs=[near] * 3,
+        out_specs=[near, near],
+        out_shape=[
+            jax.ShapeDtypeStruct((REQ, COLS), F32),
+            jax.ShapeDtypeStruct((REQ, COLS), BF16),
+        ],
+        scratch_shapes=[pltpu.VMEM((COLS // HD, 128, HD), F32)],
+        compiler_params=params(16),
+        cost_estimate=pl.CostEstimate(flops=2 * 10**6, bytes_accessed=3 * MIB, transcendentals=0),
+    )(sums, got, gain)
+
+
+def expert_kernel(
+    slot_ref, base_ref, k0_ref, k1_ref, k2_ref, k3_ref, gain_ref, own_ref, sib_ref, o_ref, rows_s, sem
+):
+    start_rows(slot_ref, [own_ref, sib_ref], rows_s, sem)
     rank = (k0_ref[...] + k1_ref[...]) + (k2_ref[...] + k3_ref[...])
-    base = got_ref[...].astype(F32)[:, 8:16, :].reshape(128, COLS)
-    spread = jnp.where(own_lanes(128, REQ * RANK, 0), rank, 0.0)
+    spread = jnp.where(own_lanes(REQ, REQ * RANK, 1), rank, 0.0)
     high = spread.astype(BF16)
     low = (spread - high.astype(F32)).astype(BF16)
-    wait_rows(tables, rows_s, sem)
+    wait_rows(own_ref, rows_s, sem)
     rows = rows_s[...].reshape(REQ * RANK, COLS)
     delta = jnp.dot(high, rows, preferred_element_type=F32)
     delta = delta + jnp.dot(low, rows, preferred_element_type=F32)
-    hidden = (base + (total + LOWRANK_SCALE * delta)).astype(BF16).astype(F32)
-    scaled = hidden * gain_ref[...].astype(F32)
-    for j in range(COLS // HD):
-        lanes = slice(j * HD, (j + 1) * HD)
-        hid_s[j] = scaled[:, lanes]
-        o_ref = oa_ref if j * HD < HALF else ob_ref
-        lanes = slice(j * HD % HALF, j * HD % HALF + HD)
-        for kind in range(2):
-            rows = hid_s[j, pl.ds(kind, REQ, stride=2), :]
-            o_ref[kind * REQ : (kind + 1) * REQ, lanes] = rows.astype(BF16)
-
-
-HALF = COLS // 2
-
-
-def hidden_slice(slots, sums, rank, got, gain, own, sib):
+    hidden = (base_ref[...] + LOWRANK_SCALE * delta).astype(BF16).astype(F32)
+    o_ref[...] = (hidden * gain_ref[...].astype(F32)).astype(BF16)
+
+
+def expert_rows(slots, base, rank, gain, own, sib):
     near = pl.BlockSpec(memory_space=pltpu.VMEM)
-    far = pl.BlockSpec(memory_space=pl.ANY)
-    return pl.pallas_call(
-        hidden_kernel,
-        in_specs=[pl.BlockSpec(memory_space=pltpu.SMEM)] + [near] * 7 + [far] * 2,
-        out_specs=[near, near],
-        out_shape=[jax.ShapeDtypeStruct((128, HALF), BF16)] * 2,
-        scratch_shapes=[
-            pltpu.VMEM((REQ, RANK, COLS), BF16),
-            pltpu.VMEM((COLS // HD, 128, HD), F32),
-            pltpu.SemaphoreType.DMA,
-        ],
-        compiler_params=params(16),
-        cost_estimate=pl.CostEstimate(flops=3 * 10**8, bytes_accessed=4 * MIB, transcendentals=0),
-    )(slots, sums, *rank, got, gain, own, sib)
-
-
-TILE = 256
-TILES = 2 * VOC // TILE
+    return pl.pallas_call(
+        expert_kernel,
+        in_specs=[pl.BlockSpec(memory_space=pltpu.SMEM)]
+        + [near] * 6
+        + [pl.BlockSpec(memory_space=pl.ANY)] * 2,
+        out_specs=near,
+        out_shape=jax.ShapeDtypeStruct((REQ, COLS), BF16),
+        scratch_shapes=[pltpu.VMEM((REQ, RANK, COLS), BF16), pltpu.SemaphoreType.DMA],
+        compiler_params=params(56),
+        cost_estimate=pl.CostEstimate(flops=3 * 10**8, bytes_accessed=2 * MIB, transcendentals=0),
+    )(slots, base, *rank, gain, own, sib)
 
 
 def tensor_index(at, first, second):
@@ -252,131 +257,135 @@
     return lax.rem(at[1] + along_x, 4) * 4 + lax.rem(at[2] + along_z, 4)
 
 
-def head_kernel(pieces, first, last, at_ref, inv_ref, *refs):
+ROWS = NY * REQ
+PAIR = 2 * COLS
+BOTH = 2 * VOC
+
+
+def head_kernel(pieces, first, last, amateur, at_ref, inv_ref, *refs):
     count = 1 + max(piece[0] for piece in pieces)
     x_refs, wo_ref, ws_ref, refs = refs[:count], refs[count], refs[count + 1], refs[count + 2 :]
     if not first:
         sums_ref, square_ref, refs = refs[0], refs[1], refs[2:]
     if last:
-        uo_ref, us_ref, lse_ref, x_s, w_s, acc_s, sq_s, x_sem, w_sem, in_sem, q_sem = refs
+        other_ref, other_lse_ref, uo_ref, us_ref, lse_ref = refs[:5]
+        x_s, w_s, acc_s, sq_s, x_sem, w_sem, in_sem, q_sem, other_s, o_sem = refs[5:]
     else:
-        out_ref, squares_ref, x_s, w_s, acc_s, sq_s, x_sem, w_sem, in_sem, q_sem, out_sem = refs
-
-    for n, (which, block, offsets, absolute) in enumerate(pieces):
-        lanes = pl.ds(n * HALF, HALF)
+        out_ref, squares_ref, x_s, w_s, acc_s, sq_s, x_sem, w_sem, in_sem, q_sem = refs
+
+    starts = []
+    for n, (which, block, offsets) in enumerate(pieces):
+        index = block if offsets is None else tensor_index(at_ref, *offsets)
+        start = pl.multiple_of(index * COLS, COLS)
+        starts.append(start)
+        run, part = n // 2, pl.ds(n % 2 * COLS, COLS)
         for y in range(NY):
-            if absolute:
+            if offsets is None:
                 source = x_refs[which].at[y, block]
                 place = y
             else:
                 source = x_refs[which].at[block, y]
                 place = lax.rem(at_ref[0] + y, NY)
-            pltpu.make_async_copy(source, x_s.at[place, :, lanes], x_sem).start()
-    starts = []
-    for _, block, offsets, absolute in pieces:
-        index = block if absolute else tensor_index(at_ref, *offsets)
-        starts.append(pl.multiple_of(index * COLS + (HALF if absolute else 0), HALF))
-    for tile in range(TILES):
-        w_ref = wo_ref if tile < TILES // 2 else ws_ref
-        columns = pl.ds(tile % (TILES // 2) * TILE, TILE)
-        for n, start in enumerate(starts):
+            pltpu.make_async_copy(source, x_s.at[run, place, :, part], x_sem.at[run]).start()
+        for side, w_ref in enumerate((wo_ref, ws_ref)):
             pltpu.make_async_copy(
-                w_ref.at[pl.ds(start, HALF), columns],
-                w_s.at[tile, pl.ds(n * HALF, HALF), :],
-                w_sem.at[tile],
+                w_ref.at[pl.ds(start, COLS), :],
+                w_s.at[run, part, pl.ds(side * VOC, VOC)],
+                w_sem.at[run],
             ).start()
-        if not first:
-            pltpu.make_async_copy(sums_ref.at[tile], acc_s.at[tile], in_sem.at[tile]).start()
     if not first:
+        pltpu.make_async_copy(sums_ref, acc_s, in_sem).start()
         pltpu.make_async_copy(square_ref, sq_s, q_sem).start()
         pltpu.make_async_copy(square_ref, sq_s, q_sem).wait()
-    pltpu.make_async_copy(x_s, x_s, x_sem).wait()
-
-    def one(tile, carry):
-        pltpu.make_async_copy(w_s.at[tile], w_s.at[tile], w_sem.at[tile]).wait()
-        x = x_s[...].reshape(512, len(pieces) * HALF)
-        part = jnp.dot(x, w_s[tile], preferred_element_type=F32)
-        if first:
-            acc_s[tile] = part
-        else:
-            pltpu.make_async_copy(sums_ref.at[tile], acc_s.at[tile], in_sem.at[tile]).wait()
-            acc_s[tile] += part
-        if not last:
-            pltpu.make_async_copy(acc_s.at[tile], out_ref.at[tile], out_sem.at[tile]).start()
+        pltpu.make_async_copy(sums_ref, acc_s, in_sem).wait()
+    else:
+        acc_s[...] = jnp.zeros((ROWS, BOTH), F32)
+        sq_s[...] = jnp.zeros((ROWS, HD), F32)
+    if last:
+        pltpu.make_async_copy(other_ref, other_s, o_sem).start()
+
+    def one(run, carry):
+        pltpu.make_async_copy(x_s.at[run], x_s.at[run], x_sem.at[run]).wait()
+        pltpu.make_async_copy(w_s.at[run], w_s.at[run], w_sem.at[run]).wait()
+        x = x_s[run].reshape(ROWS, PAIR)
+        acc_s[...] += jnp.dot(x, w_s[run], preferred_element_type=F32)
         return carry
 
-    lax.fori_loop(0, TILES, one, 0)
-
-    square = jnp.zeros((512, HD), F32) if first else sq_s[...]
+    lax.fori_loop(0, len(pieces) // 2, one, 0)
+
+    square = sq_s[...]
     for n, start in enumerate(starts):
-        for j in range(HALF // HD):
-            piece = x_s[:, :, n * HALF + j * HD : n * HALF + (j + 1) * HD].reshape(512, HD).astype(F32)
+        for j in range(COLS // HD):
+            lanes = slice(n % 2 * COLS + j * HD, n % 2 * COLS + (j + 1) * HD)
+            piece = x_s[n // 2, :, :, lanes].reshape(ROWS, HD).astype(F32)
             inverse = inv_ref[:, pl.ds(pl.multiple_of(start + j * HD, HD), HD)]
             square = square + piece * piece * inverse
-    if not last:
+    if not (last or amateur):
         sq_s[...] = square
         pltpu.make_async_copy(sq_s, squares_ref, q_sem).start()
+        pltpu.make_async_copy(acc_s, out_ref, in_sem).start()
         pltpu.make_async_copy(sq_s, squares_ref, q_sem).wait()
-        for tile in range(TILES):
-            pltpu.make_async_copy(acc_s.at[tile], out_ref.at[tile], out_sem.at[tile]).wait()
+        pltpu.make_async_copy(acc_s, out_ref, in_sem).wait()
         return
 
-    mean = jnp.sum(square, axis=1, keepdims=True) * (1.0 / WIDTH)
-    factor = lax.rsqrt(mean + EPS)
-    peak = acc_s[0]
-    for tile in range(1, TILES):
-        peak = jnp.maximum(peak, acc_s[tile])
-    peak = jnp.max(peak, axis=1, keepdims=True) * factor
-    total = jnp.exp(acc_s[0] * factor - peak)
-    for tile in range(1, TILES):
-        total = total + jnp.exp(acc_s[tile] * factor - peak)
-    lse = peak + jnp.log(jnp.sum(total, axis=1, keepdims=True))
-    sq_s[...] = jnp.broadcast_to(lse, (512, HD))
-    lse_ref[...] = jnp.transpose(sq_s[...])[0:1, :]
-    for y in range(NY):
-        a, b, c = y * 128, y * 128 + REQ, y * 128 + 128
-        expert = (1.0 + BETA) * factor[a:b]
-        amateur = BETA * factor[b:c]
-        for tile in range(TILES):
-            u_ref = uo_ref if tile < TILES // 2 else us_ref
-            lanes = slice(tile % (TILES // 2) * TILE, (tile % (TILES // 2) + 1) * TILE)
-            u_ref[y * REQ : (y + 1) * REQ, lanes] = (
-                expert * acc_s[tile, a:b, :] - amateur * acc_s[tile, b:c, :]
-            )
-
-
-def head_part(place, arrays, pieces, inverse, w_own, w_sib, sums=None, last=False):
-    first = sums is None
-    depth = len(pieces) * HALF
+    factor = lax.rsqrt(jnp.sum(square, axis=1, keepdims=True) * (1.0 / WIDTH) + EPS)
+    logits = acc_s[...] * factor
+    peak = jnp.max(logits, axis=1, keepdims=True)
+    lse = peak + jnp.log(jnp.sum(jnp.exp(logits - peak), axis=1, keepdims=True))
+    sq_s[...] = jnp.broadcast_to(lse, (ROWS, HD))
+    lse = jnp.transpose(sq_s[...])[0:1, :]
+    if amateur:
+        acc_s[...] = logits
+        squares_ref[...] = lse
+        pltpu.make_async_copy(acc_s, out_ref, in_sem).start()
+        pltpu.make_async_copy(acc_s, out_ref, in_sem).wait()
+        return
+    lse_ref[:, 0:ROWS] = lse
+    lse_ref[:, ROWS:] = other_lse_ref[...]
+    pltpu.make_async_copy(other_ref, other_s, o_sem).wait()
+    mixed = (1.0 + BETA) * logits - BETA * other_s[...]
+    uo_ref[...] = mixed[:, :VOC]
+    us_ref[...] = mixed[:, VOC:]
+
+
+def head_part(place, arrays, pieces, inverse, w_own, w_sib, sums=None, other=None, amateur=False):
+    first, last = sums is None, other is not None
+    depth = len(pieces) * COLS
+    runs = len(pieces) // 2
     near = pl.BlockSpec(memory_space=pltpu.VMEM)
     far = pl.BlockSpec(memory_space=pl.ANY)
-    partial = [(TILES, 512, TILE), (512, HD)]
-    shapes = [(NY * REQ, VOC), (NY * REQ, VOC), (1, 512)] if last else partial
+    if last:
+        shapes, out_specs = [(ROWS, VOC), (ROWS, VOC), (1, 2 * ROWS)], [near] * 3
+    elif amateur:
+        shapes, out_specs = [(ROWS, BOTH), (1, ROWS)], [far, near]
+    else:
+        shapes, out_specs = [(ROWS, BOTH), (ROWS, HD)], [far, far]
     dma = pltpu.SemaphoreType.DMA
     return pl.pallas_call(
-        lambda *refs: head_kernel(pieces, first, last, *refs),
+        lambda *refs: head_kernel(pieces, first, last, amateur, *refs),
         in_specs=[pl.BlockSpec(memory_space=pltpu.SMEM), near]
-        + [far] * (len(arrays) + 2 + (0 if first else 2)),
-        out_specs=[near] * 3 if last else [far] * 2,
+        + [far] * (len(arrays) + 2 + (0 if first else 2))
+        + ([far, near] if last else []),
+        out_specs=out_specs,
         out_shape=[jax.ShapeDtypeStruct(shape, F32) for shape in shapes],
         scratch_shapes=[
-            pltpu.VMEM((NY, 128, depth), BF16),
-            pltpu.VMEM((TILES, depth, TILE), BF16),
-            pltpu.VMEM((TILES, 512, TILE), F32),
-            pltpu.VMEM((512, HD), F32),
+            pltpu.VMEM((runs, NY, REQ, PAIR), BF16),
+            pltpu.VMEM((runs, PAIR, BOTH), BF16),
+            pltpu.VMEM((ROWS, BOTH), F32),
+            pltpu.VMEM((ROWS, HD), F32),
+            dma((runs,)),
+            dma((runs,)),
             dma,
-            dma((TILES,)),
-            dma((TILES,)),
             dma,
         ]
-        + ([] if last else [dma((TILES,))]),
+        + ([pltpu.VMEM((ROWS, BOTH), F32), dma] if last else []),
         compiler_params=params(56),
         cost_estimate=pl.CostEstimate(
-            flops=2 * 512 * depth * 2 * VOC,
-            bytes_accessed=depth * 4096 + (3 if first else 6) * MIB,
-            transcendentals=786432 if last else 0,
+            flops=ROWS * depth,
+            bytes_accessed=depth * 64,
+            transcendentals=0,
         ),
-    )(place, inverse, *arrays, w_own, w_sib, *(sums or ()))
+    )(place, inverse, *arrays, w_own, w_sib, *(sums or ()), *(other or ()))
 
 
 def contrast_kernel(core_ref, uo_ref, us_ref, no_ref, ns_ref, o_ref):
@@ -384,8 +393,8 @@
     for u_ref, n_ref, parity in ((uo_ref, no_ref, core), (us_ref, ns_ref, 1 - core)):
         column = jnp.transpose(jnp.broadcast_to(n_ref[...], (HD, 512)))
         for y in range(NY):
-            a, b, c = y * 128, y * 128 + REQ, y * 128 + 128
-            shift = (1.0 + BETA) * column[a:b] - BETA * column[b:c]
+            a, b = y * REQ, ROWS + y * REQ
+            shift = (1.0 + BETA) * column[a : a + REQ] - BETA * column[b : b + REQ]
             rows = pl.ds(pl.multiple_of((2 * y + parity) * REQ, REQ), REQ)
             for j in range(VOC // HD):
                 lanes = slice(j * HD, (j + 1) * HD)
@@ -461,12 +470,13 @@
     place = jnp.stack([lax.axis_index(axis) for axis in ("y", "x", "z", "c")]).astype(jnp.int32)
     head_sib = lax.ppermute(vocabulary_head_matrix, "c", SWAP)
     down = lax.all_gather(lowrank_down_factors, ("y", "c"), axis=0, tiled=True)
-    up_after = from_offset(lowrank_up_factors, "y", 1)
-    up_before = from_offset(lowrank_up_factors, "y", 3)
     owner = request_adapter_index // HELD
     slots = ((owner // 2 - place[0]) % NY) * HELD + request_adapter_index % HELD
     slots = slots + jnp.where(owner % 2 == place[3], 0, NY * HELD)
+    up_after = from_offset(lowrank_up_factors, "y", 1)
+    up_before = from_offset(lowrank_up_factors, "y", 3)
     gain = lax.dynamic_slice(final_norm_scale, (lax.axis_index(TENSOR) * COLS,), (COLS,))
+    gain = gain.reshape(1, COLS)
     inverse = 1.0 / final_norm_scale.astype(F32)
     inverse = (inverse * inverse).reshape(1, WIDTH)
 
@@ -483,43 +493,38 @@
     partial = projection(got, output_projection_weight)
     up_after, up_before, partial = lax.optimization_barrier((up_after, up_before, partial))
     sums = lax.all_to_all(partial, TENSOR, split_axis=0, concat_axis=0, tiled=True)
+    rank = rank_sums(request_adapter_index, got, down)
     half = HELD // 2
-    up_own = jnp.concatenate(
-        [
-            lowrank_up_factors,
-            up_after,
-            from_offset(up_after[:half], "y", 1),
-            from_offset(up_before[half:], "y", 3),
-            up_before,
-        ],
-        axis=0,
-    )
+    up_far = (from_offset(up_after[:half], "y", 1), from_offset(up_before[half:], "y", 3))
+    up_own = jnp.concatenate([lowrank_up_factors, up_after, *up_far, up_before], axis=0)
+    up_own, sums = lax.optimization_barrier((up_own, sums))
     up_sib = lax.ppermute(up_own, "c", SWAP)
-    rank = rank_sums(request_adapter_index, got, down)
+    base, amateur = summed_rows(sums, got, gain)
+    gathered = lax.all_gather(amateur, ("y", "x", "z"), axis=0, tiled=False)
+    gathered = gathered.reshape(NY, TEN, REQ, COLS)
+    rank, base = lax.optimization_barrier((rank, base))
     rank = sum([from_offset(rank, "x", d) for d in range(1, 4)], rank)
     rank = [rank] + [from_offset(rank, "z", d) for d in range(1, 4)]
-    own, rest = hidden_slice(slots, sums, rank, got, gain.reshape(1, COLS), up_own, up_sib)
-
-    gathered = lax.all_gather(rest, ("y", "x", "z"), axis=0, tiled=False)
-    gathered = gathered.reshape(NY, TEN, 128, HALF)
-    plane = jnp.stack([own] + [from_offset(own, "y", d) for d in range(1, 4)])
+    expert = expert_rows(slots, base, rank, gain, up_own, up_sib)
+
+    plane = jnp.stack([expert] + [from_offset(expert, "y", d) for d in range(1, 4)])
     after = from_core_offset(plane, FIRST, 1)
     before = from_core_offset(plane, FIRST, 3)
-    far = opposite(after, before, FIRST)
-    mine = jnp.stack([plane, after, jnp.concatenate(far, axis=0), before])
+    mine = jnp.stack([plane, after, from_core_offset(plane, FIRST, 2), before])
     after = from_core_offset(mine, SECOND, 1)
     before = from_core_offset(mine, SECOND, 3)
     weights = (inverse, vocabulary_head_matrix, head_sib)
-    pieces = [(0, n, (n, 0), False) for n in range(4)]
+    pieces = [(0, n, (n, 0)) for n in range(4)]
     partial = head_part(place, [mine], pieces, *weights)
     after, before, *partial = lax.optimization_barrier((after, before, *partial))
     far = opposite(after, before, SECOND)
-    pieces = [(n // 4, n % 4, (n % 4, 1 + 2 * (n // 4)), False) for n in range(8)]
+    pieces = [(n // 4, n % 4, (n % 4, 1 + 2 * (n // 4))) for n in range(8)]
     partial = head_part(place, [after, before], pieces, *weights, sums=partial)
-    pieces = [(n // 2, n % 2, (n, 2), False) for n in range(4)]
-    partial = head_part(place, far, pieces, *weights, sums=partial)
-    pieces = [(0, n, None, True) for n in range(TEN)]
-    u_own, u_send, lse = head_part(place, [gathered], pieces, *weights, sums=partial, last=True)
+    gathered, *partial = lax.optimization_barrier((gathered, *partial))
+    pieces = [(0, n, None) for n in range(TEN)]
+    other = head_part(place, [gathered], pieces, *weights, amateur=True)
+    pieces = [(n // 2, n % 2, (n, 2)) for n in range(4)]
+    u_own, u_send, lse = head_part(place, far, pieces, *weights, sums=partial, other=other)
     for axis in ("y", "x", "z"):
         lse = combine([lse] + [from_offset(lse, axis, d) for d in range(1, 4)])
         if axis == "y":

time: 239 us -> 223 us (0.933)
  waiting for transfers between devices: 87.4 us -> 59 us
  local copies, waits for them, and re-layouts: 6.81 us -> 14.6 us
  starting transfers between devices: 48.8 us -> 53.8 us
    ppermute x22, waiting for transfers between devices: 57.3 us -> 29.8 us  [from_offset(): return lax.ppermute(array, axis, [((i + offset) % 4, i) for i in range(4)])]
    all_gather x1, waiting for transfers between devices: 10.6 us -> 0.02 us  [per_device(): gathered = lax.all_gather(amateur, ('y', 'x', 'z'), axis=0, tiled=False)]
    ppermute x8 -> x7, waiting for transfers between devices: 17.7 us -> 23.4 us  [from_core_offset(): return lax.ppermute(array, ('c', 'x', 'z'), pairs)]
    unnamed x24 -> x36, local copies, waits for them, and re-layouts: 5.58 us -> 10.3 us
    ppermute x1, starting transfers between devices: 8.53 us -> 12.9 us  [per_device(): u_sib = lax.ppermute(u_send, 'c', SWAP)]
    all_to_all x1, waiting for transfers between devices: 0.01 us -> 4.26 us  [per_device(): lax.all_to_all(partial, TENSOR, split_axis=0, concat_axis=0, tiled=True)]
    ppermute x22, starting transfers between devices: 19.5 us -> 17 us  [from_offset(): return lax.ppermute(array, axis, [((i + offset) % 4, i) for i in range(4)])]
    ppermute x1, starting transfers between devices: 3.16 us -> 5.59 us  [per_device(): up_sib = lax.ppermute(up_own, 'c', SWAP)]
  transfers between devices with their start and end apart: 37 -> 36, of which waited for: 26 -> 25; matrix products, arithmetic and copies ran while one was open for 3% -> 7% of each run, Pallas kernels for 18% -> 23%
where the time goes in v2:
time: 223 us; the launch traced here: 222 us
  Pallas kernels  61.2 us (27%)
  waiting for transfers between devices  59 us (26%)
  starting transfers between devices  53.8 us (24%)
  blocking collectives  15.3 us (7%)
  local copies, waits for them, and re-layouts  14.6 us (7%)
  between operations  13.6 us (6%)
  other arithmetic  4.27 us (2%)
    pallas_call x4, Pallas kernels, head_part(): pl.pallas_call(lambda *refs: head_kernel(pieces, first, last, amateur, *r...  41 us
    ppermute x22, waiting for transfers between devices, from_offset(): return lax.ppermute(array, axis, [((i + offset) % 4, i) for i in range(4)])  29.8 us
    ppermute x7, waiting for transfers between devices, from_core_offset(): return lax.ppermute(array, ('c', 'x', 'z'), pairs)  23.4 us
    ppermute x22, starting transfers between devices, from_offset(): return lax.ppermute(array, axis, [((i + offset) % 4, i) for i in range(4)])  17 us
    all_to_all x1, blocking collectives, per_device(): got = lax.all_to_all(sent, TENSOR, split_axis=0, concat_axis=0, tiled=True)  15.3 us
    ppermute x1, starting transfers between devices, per_device(): u_sib = lax.ppermute(u_send, 'c', SWAP)  12.9 us
    unnamed x36, local copies, waits for them, and re-layouts  10.3 us
    all_to_all x1, starting transfers between devices, per_device(): lax.all_to_all(partial, TENSOR, split_axis=0, concat_axis=0, tiled=True)  7.82 us
  transfers between devices with their start and end apart: 36, of which 25 were waited for; matrix products, arithmetic and copies ran while one was open for 7% of the time, Pallas kernels for 23%

profile of v2, /device:TPU:1, one launch (start us, length us, event | category | flops | bytes accessed | tf_op | source)
XLA Modules:
  0.0 221.8 jit_solution(13585996421477853863)
XLA Ops:
  8.8 2.8 %collective-permute-start = (bf16[48,16,512]{2,1,0:T(8,128)(2,1)}, bf16[48,16,512]{2,1,0:T(8,128)(2,1)}, u32[]{:S(2)}, u32[]{:S(2)}) collective-permute-start(bf16[48,16,512]{2,1,0:T(8,128)(2,1)} %param.23), channel_id=1, source_target_pairs={{32,0},{64,32},{96,64},{0,96},{33,1},{65,33},{97,65},{1,97},{34,2}... | collective-permute-start | bytes 2359304 | tf_op jit(solution)/shard_map/ppermute | solution.py:431
  11.6 5.0 %shard_map.127 = bf16[16,16,512]{2,1,0:T(8,128)(2,1)} custom-call(s32[4]{0:T(128)} %len_ref.1, bf16[4,2,8192]{2,1,0:T(2,128)(2,1)} %q_ref.1, bf16[4,2,64,1024]{3,2,1,0:T(8,128)(2,1)} %k_ref.1, bf16[4,2,64,1024]{3,2,1,0:T(8,128)(2,1)} %v_ref.1, bf16[4,2,1024]{2,1,0:T(2,128)(2,1)} %ck_ref.1, bf16[4,2,1024]{2,1,0:T(2,128)(2,1)} %cv_ref.1, ...), custom_call_target="tpu_custom_call" | custom-call | flops 300000000 | bytes 3145728 | tf_op jit(solution)/shard_map/pallas_call | solution.py:81
  16.6 15.3 %all_to_all.10.got_ref = bf16[16,16,512]{2,1,0:T(8,128)(2,1)} all-to-all(bf16[16,16,512]{2,1,0:T(8,128)(2,1)} %shard_map.127), channel_id=1, replica_groups=mesh['y'=4,'c'=2,'x'=4,'z'=4] {'x','z'}, dimensions={0} | all-to-all | bytes 524288 | tf_op jit(solution)/shard_map/all_to_all | solution.py:492
  31.9 6.1 %shard_map.129 = bf16[16,128,512]{2,1,0:T(8,128)(2,1)} custom-call(bf16[16,16,512]{2,1,0:T(8,128)(2,1)} %all_to_all.10.got_ref, bf16[512,8192]{1,0:T(8,128)(2,1)} %w_ref.1), custom_call_target="tpu_custom_call" | custom-call | flops 1100000000 | bytes 11534336 | tf_op jit(solution)/shard_map/pallas_call | solution.py:152
  38.0 7.8 %all-to-all-start.1 = ((bf16[16,128,512]{2,1,0:T(8,128)(2,1)}), bf16[16,128,512]{2,1,0:T(8,128)(2,1)S(1)}, u32[]{:S(2)}, u32[]{:S(2)}) async-start(bf16[16,128,512]{2,1,0:T(8,128)(2,1)} %shard_map.129), calls=%async_computation.1 | async-start | bytes 4194304 | tf_op jit(solution)/shard_map/all_to_all | solution.py:495
  54.9 7.0 %collective-permute-done.2 = bf16[24,16,512]{2,1,0:T(8,128)(2,1)} collective-permute-done((bf16[24,16,512]{2,1,0:T(8,128)(2,1)}, bf16[24,16,512]{2,1,0:T(8,128)(2,1)}, u32[]{:S(2)}, u32[]{:S(2)}) %collective-permute-start.2) | collective-permute-done | bytes 393248 | tf_op jit(solution)/shard_map/ppermute | solution.py:431
  66.9 4.3 %all-to-all-done.1.sums_ref = bf16[16,128,512]{2,1,0:T(8,128)(2,1)S(1)} async-done(((bf16[16,128,512]{2,1,0:T(8,128)(2,1)}), bf16[16,128,512]{2,1,0:T(8,128)(2,1)S(1)}, u32[]{:S(2)}, u32[]{:S(2)}) %all-to-all-start.1) | async-done | bytes 2097184 | tf_op jit(solution)/shard_map/all_to_all | solution.py:495
  72.9 5.6 %collective-permute-start.10 = (bf16[192,16,512]{2,1,0:T(8,128)(2,1)}, bf16[192,16,512]{2,1,0:T(8,128)(2,1)S(1)}, u32[]{:S(2)}, u32[]{:S(2)}) collective-permute-start(bf16[192,16,512]{2,1,0:T(8,128)(2,1)} %constant_dynamic-update-slice_fusion.own_ref), channel_id=1, source_target_pairs={{0,16},{16,0},{1,17},{17,1},{2,18},{18,2},{3,19},{19,3},{4,20},{20... | collective-permute-start | bytes 9437192 | tf_op jit(solution)/shard_map/ppermute | solution.py:501
  78.5 3.2 %shard_map.128 = f32[1,1024]{1,0:T(1,128)} custom-call(s32[64]{0:T(128)} %idx_ref.1, bf16[16,16,512]{2,1,0:T(8,128)(2,1)} %all_to_all.10.got_ref, bf16[384,16,512]{2,1,0:T(8,128)(2,1)} %all-gather.4.cloned.1.call-done.table_ref), custom_call_target="tpu_custom_call" | custom-call | flops 140000000 | bytes 2097152 | tf_op jit(solution)/shard_map/pallas_call | solution.py:179
  94.7 3.4 %shard_map.131 = bf16[64,512]{1,0:T(8,128)(2,1)} custom-call(s32[64]{0:T(128)} %fusion.1.slot_ref, f32[64,512]{1,0:T(8,128)} %copy-done.2, f32[1,1024]{1,0:T(1,128)} %copy-done.11, f32[1,1024]{1,0:T(1,128)} %copy-done.12, f32[1,1024]{1,0:T(1,128)} %copy-done.13, f32[1,1024]{1,0:T(1,128)} %copy-done.14, bf16[1,512]{1,0:T(2,128)(2,1)} %copy-done.3, ...), custom_call_target="tpu_custom_call" | custom-call | flops 300000000 | bytes 2097152 | tf_op jit(solution)/shard_map/pallas_call | solution.py:241
  106.8 3.3 %collective-permute-done.14 = bf16[4,64,512]{2,1,0:T(8,128)(2,1)S(1)} collective-permute-done((bf16[4,64,512]{2,1,0:T(8,128)(2,1)S(1)}, bf16[4,64,512]{2,1,0:T(8,128)(2,1)S(1)}, u32[]{:S(2)}, u32[]{:S(2)}) %collective-permute-start.14) | collective-permute-done | bytes 262176 | tf_op jit(solution)/shard_map/ppermute | solution.py:442
  110.1 2.7 %collective-permute-done.15 = bf16[4,64,512]{2,1,0:T(8,128)(2,1)S(1)} collective-permute-done((bf16[4,64,512]{2,1,0:T(8,128)(2,1)S(1)}, bf16[4,64,512]{2,1,0:T(8,128)(2,1)S(1)}, u32[]{:S(2)}, u32[]{:S(2)}) %collective-permute-start.15) | collective-permute-done | bytes 262176 | tf_op jit(solution)/shard_map/ppermute | solution.py:442
  112.8 4.2 %collective-permute-done.16 = bf16[4,64,512]{2,1,0:T(8,128)(2,1)S(1)} collective-permute-done((bf16[4,64,512]{2,1,0:T(8,128)(2,1)S(1)}, bf16[4,64,512]{2,1,0:T(8,128)(2,1)S(1)}, u32[]{:S(2)}, u32[]{:S(2)}) %collective-permute-start.16) | collective-permute-done | bytes 262176 | tf_op jit(solution)/shard_map/ppermute | solution.py:442
  120.0 6.2 %shard_map.132 = (f32[256,1536]{1,0:T(8,128)}, f32[256,128]{1,0:T(8,128)}) custom-call(s32[4]{0:T(128)} %pad_add_fusion.refs_0_, f32[1,8192]{1,0:T(1,128)} %bitcast.16, bf16[4,4,64,512]{3,2,1,0:T(8,128)(2,1)} %copy-done.4, bf16[8192,768]{1,0:T(8,128)(2,1)} %refs_4_.3, bf16[8192,768]{1,0:T(8,128)(2,1)} %collective-permute-done.19.refs_4_.refs_5_), custom_call_target="tpu_custom_call" | custom-call | flops 524288 | bytes 131072 | tf_op jit(solution)/shard_map/pallas_call | solution.py:364
  126.2 9.0 %collective-permute-done.17.refs_2_ = bf16[4,4,64,512]{3,2,1,0:T(8,128)(2,1)S(1)} collective-permute-done((bf16[4,4,64,512]{3,2,1,0:T(8,128)(2,1)S(1)}, bf16[4,4,64,512]{3,2,1,0:T(8,128)(2,1)S(1)}, u32[]{:S(2)}, u32[]{:S(2)}) %collective-permute-start.17) | collective-permute-done | bytes 1048608 | tf_op jit(solution)/shard_map/ppermute | solution.py:442
  135.2 4.2 %collective-permute-done.18.refs_3_ = bf16[4,4,64,512]{3,2,1,0:T(8,128)(2,1)S(1)} collective-permute-done((bf16[4,4,64,512]{3,2,1,0:T(8,128)(2,1)S(1)}, bf16[4,4,64,512]{3,2,1,0:T(8,128)(2,1)S(1)}, u32[]{:S(2)}, u32[]{:S(2)}) %collective-permute-start.18) | collective-permute-done | bytes 1048608 | tf_op jit(solution)/shard_map/ppermute | solution.py:442
  141.3 11.9 %shard_map.133 = (f32[256,1536]{1,0:T(8,128)}, f32[256,128]{1,0:T(8,128)}) custom-call(s32[4]{0:T(128)} %pad_add_fusion.refs_0_, f32[1,8192]{1,0:T(1,128)} %bitcast.17, bf16[4,4,64,512]{3,2,1,0:T(8,128)(2,1)} %copy-done.6, bf16[4,4,64,512]{3,2,1,0:T(8,128)(2,1)} %copy-done.7, bf16[8192,768]{1,0:T(8,128)(2,1)} %refs_4_.3, ...), custom_call_target="tpu_custom_call" | custom-call | flops 1048576 | bytes 262144 | tf_op jit(solution)/shard_map/pallas_call | solution.py:364
  153.3 14.4 %shard_map.134 = (f32[256,1536]{1,0:T(8,128)}, f32[1,256]{1,0:T(1,128)}) custom-call(s32[4]{0:T(128)} %pad_add_fusion.refs_0_, f32[1,8192]{1,0:T(1,128)} %bitcast.18, bf16[4,16,64,512]{3,2,1,0:T(8,128)(2,1)} %bitcast.15, bf16[8192,768]{1,0:T(8,128)(2,1)} %refs_4_.3, bf16[8192,768]{1,0:T(8,128)(2,1)} %collective-permute-done.19.refs_4_.refs_5_), custom_call_target="tpu_custom_call" | custom-call | flops 2097152 | bytes 524288 | tf_op jit(solution)/shard_map/pallas_call | solution.py:364
  168.6 8.5 %shard_map.135 = (f32[256,768]{1,0:T(8,128)}, f32[256,768]{1,0:T(8,128)}, f32[1,512]{1,0:T(1,128)}) custom-call(s32[4]{0:T(128)} %pad_add_fusion.refs_0_, f32[1,8192]{1,0:T(1,128)} %bitcast.19, bf16[2,4,64,512]{3,2,1,0:T(8,128)(2,1)} %copy-done.8, bf16[2,4,64,512]{3,2,1,0:T(8,128)(2,1)} %copy-done.9, bf16[8192,768]{1,0:T(8,128)(2,1)} %refs_4_.3, ...), custom_call_target="tpu_custom_call" | custom-call | flops 524288 | bytes 131072 | tf_op jit(solution)/shard_map/pallas_call | solution.py:364
  177.2 2.6 %collective-permute-start.22 = (f32[1,512]{1,0:T(1,128)}, f32[1,512]{1,0:T(1,128)S(1)}, u32[]{:S(2)}, u32[]{:S(2)}) collective-permute-start(f32[1,512]{1,0:T(1,128)} %get-tuple-element.56), channel_id=1, source_target_pairs={{32,0},{64,32},{96,64},{0,96},{33,1},{65,33},{97,65},{1,97},{34,2}... | collective-permute-start | bytes 6152 | tf_op jit(solution)/shard_map/ppermute | solution.py:431
  180.7 3.2 %collective-permute-done.23 = f32[1,512]{1,0:T(1,128)S(1)} collective-permute-done((f32[1,512]{1,0:T(1,128)}, f32[1,512]{1,0:T(1,128)S(1)}, u32[]{:S(2)}, u32[]{:S(2)}) %collective-permute-start.23) | collective-permute-done | bytes 2080 | tf_op jit(solution)/shard_map/ppermute | solution.py:431
  185.0 12.9 %collective-permute-start.25 = (f32[256,768]{1,0:T(8,128)}, f32[256,768]{1,0:T(8,128)S(1)}, u32[]{:S(2)}, u32[]{:S(2)}) collective-permute-start(f32[256,768]{1,0:T(8,128)} %get-tuple-element.57), channel_id=1, source_target_pairs={{0,16},{16,0},{1,17},{17,1},{2,18},{18,2},{3,19},{19,3},{4,20},{20... | collective-permute-start | bytes 2359304 | tf_op jit(solution)/shard_map/ppermute | solution.py:532
  205.6 2.4 %collective-permute-done.30 = f32[1,512]{1,0:T(1,128)S(1)} collective-permute-done((f32[1,512]{1,0:T(1,128)S(1)}, f32[1,512]{1,0:T(1,128)S(1)}, u32[]{:S(2)}, u32[]{:S(2)}) %collective-permute-start.30) | collective-permute-done | bytes 2080 | tf_op jit(solution)/shard_map/ppermute | solution.py:431
  208.1 3.5 %collective-permute-start.32 = (f32[1,512]{1,0:T(1,128)S(1)}, f32[1,512]{1,0:T(1,128)S(1)}, u32[]{:S(2)}, u32[]{:S(2)}) collective-permute-start(f32[1,512]{1,0:T(1,128)S(1)} %log_add_fusion.no_ref), channel_id=1, source_target_pairs={{0,16},{16,0},{1,17},{17,1},{2,18},{18,2},{3,19},{19,3},{4,20},{20... | collective-permute-start | bytes 6152 | tf_op jit(solution)/shard_map/ppermute | solution.py:533
  (113 shorter events, 58.6 us)
Async XLA Ops:
  6.5 71.9 %all-gather.4.cloned.1.call-start = ((), (), s32[]{:S(2)}) async-start(), calls=%async_computation.2 | async-start | bytes 7077888 | tf_op jit(solution)/shard_map/all_gather | solution.py:472
  7.3 112.8 %collective-permute-start.19 = (bf16[8192,768]{1,0:T(8,128)(2,1)}, bf16[8192,768]{1,0:T(8,128)(2,1)}, u32[]{:S(2)}, u32[]{:S(2)}) collective-permute-start(bf16[8192,768]{1,0:T(8,128)(2,1)} %refs_4_.3), channel_id=1, source_target_pairs={{0,16},{16,0},{1,17},{17,1},{2,18},{18,2},{3,19},{19,3},{4,20},{20... | collective-permute-start | bytes 37748744 | tf_op jit(solution)/shard_map/ppermute | solution.py:471
  8.8 29.2 %collective-permute-start = (bf16[48,16,512]{2,1,0:T(8,128)(2,1)}, bf16[48,16,512]{2,1,0:T(8,128)(2,1)}, u32[]{:S(2)}, u32[]{:S(2)}) collective-permute-start(bf16[48,16,512]{2,1,0:T(8,128)(2,1)} %param.23), channel_id=1, source_target_pairs={{32,0},{64,32},{96,64},{0,96},{33,1},{65,33},{97,65},{1,97},{34,2}... | collective-permute-start | bytes 2359304 | tf_op jit(solution)/shard_map/ppermute | solution.py:431
  11.6 26.4 %collective-permute-start.1 = (bf16[48,16,512]{2,1,0:T(8,128)(2,1)}, bf16[48,16,512]{2,1,0:T(8,128)(2,1)S(1)}, u32[]{:S(2)}, u32[]{:S(2)}) collective-permute-start(bf16[48,16,512]{2,1,0:T(8,128)(2,1)} %param.23), channel_id=1, source_target_pairs={{96,0},{0,32},{32,64},{64,96},{97,1},{1,33},{33,65},{65,97},{98,2}... | collective-permute-start | bytes 2359304 | tf_op jit(solution)/shard_map/ppermute | solution.py:431
  38.0 33.2 %all-to-all-start.1 = ((bf16[16,128,512]{2,1,0:T(8,128)(2,1)}), bf16[16,128,512]{2,1,0:T(8,128)(2,1)S(1)}, u32[]{:S(2)}, u32[]{:S(2)}) async-start(bf16[16,128,512]{2,1,0:T(8,128)(2,1)} %shard_map.129), calls=%async_computation.1 | async-start | bytes 4194304 | tf_op jit(solution)/shard_map/all_to_all | solution.py:495
  45.8 107.4 %all-gather.6.cloned.1.call-start = ((), (), s32[]{:S(2)}) async-start(), calls=%async_computation.3 | async-start | bytes 4259840 | tf_op jit(solution)/shard_map/all_gather | solution.py:503
  47.7 14.3 %collective-permute-start.2 = (bf16[24,16,512]{2,1,0:T(8,128)(2,1)}, bf16[24,16,512]{2,1,0:T(8,128)(2,1)}, u32[]{:S(2)}, u32[]{:S(2)}) collective-permute-start(bf16[24,16,512]{2,1,0:T(8,128)(2,1)} %slice.12), channel_id=1, source_target_pairs={{32,0},{64,32},{96,64},{0,96},{33,1},{65,33},{97,65},{1,97},{34,2}... | collective-permute-start | bytes 1179656 | tf_op jit(solution)/shard_map/ppermute | solution.py:431
  48.4 16.7 %collective-permute-start.3 = (bf16[24,16,512]{2,1,0:T(8,128)(2,1)}, bf16[24,16,512]{2,1,0:T(8,128)(2,1)S(1)}, u32[]{:S(2)}, u32[]{:S(2)}) collective-permute-start(bf16[24,16,512]{2,1,0:T(8,128)(2,1)} %slice.13), channel_id=1, source_target_pairs={{96,0},{0,32},{32,64},{64,96},{97,1},{1,33},{33,65},{65,97},{98,2}... | collective-permute-start | bytes 1179656 | tf_op jit(solution)/shard_map/ppermute | solution.py:431
  72.9 18.0 %collective-permute-start.10 = (bf16[192,16,512]{2,1,0:T(8,128)(2,1)}, bf16[192,16,512]{2,1,0:T(8,128)(2,1)S(1)}, u32[]{:S(2)}, u32[]{:S(2)}) collective-permute-start(bf16[192,16,512]{2,1,0:T(8,128)(2,1)} %constant_dynamic-update-slice_fusion.own_ref), channel_id=1, source_target_pairs={{0,16},{16,0},{1,17},{17,1},{2,18},{18,2},{3,19},{19,3},{4,20},{20... | collective-permute-start | bytes 9437192 | tf_op jit(solution)/shard_map/ppermute | solution.py:501
  82.2 4.2 %collective-permute-start.5 = (f32[1,1024]{1,0:T(1,128)}, f32[1,1024]{1,0:T(1,128)S(1)}, u32[]{:S(2)}, u32[]{:S(2)}) collective-permute-start(f32[1,1024]{1,0:T(1,128)} %shard_map.128), channel_id=1, source_target_pairs={{8,0},{12,4},{0,8},{4,12},{9,1},{13,5},{1,9},{5,13},{10,2},{14,6},... | collective-permute-start | bytes 12296 | tf_op jit(solution)/shard_map/ppermute | solution.py:431
  82.6 4.6 %collective-permute-start.6 = (f32[1,1024]{1,0:T(1,128)}, f32[1,1024]{1,0:T(1,128)S(1)}, u32[]{:S(2)}, u32[]{:S(2)}) collective-permute-start(f32[1,1024]{1,0:T(1,128)} %shard_map.128), channel_id=1, source_target_pairs={{12,0},{0,4},{4,8},{8,12},{13,1},{1,5},{5,9},{9,13},{14,2},{2,6},{... | collective-permute-start | bytes 12296 | tf_op jit(solution)/shard_map/ppermute | solution.py:431
  90.0 4.1 %collective-permute-start.9 = (f32[1,1024]{1,0:T(1,128)S(1)}, f32[1,1024]{1,0:T(1,128)S(1)}, u32[]{:S(2)}, u32[]{:S(2)}) collective-permute-start(f32[1,1024]{1,0:T(1,128)S(1)} %add_add_fusion.k0_ref), channel_id=1, source_target_pairs={{3,0},{0,1},{1,2},{2,3},{7,4},{4,5},{5,6},{6,7},{11,8},{8,9},{9,10... | collective-permute-start | bytes 12296 | tf_op jit(solution)/shard_map/ppermute | solution.py:431
  98.2 4.9 %collective-permute-start.12 = (bf16[64,512]{1,0:T(8,128)(2,1)}, bf16[64,512]{1,0:T(8,128)(2,1)S(1)}, u32[]{:S(2)}, u32[]{:S(2)}) collective-permute-start(bf16[64,512]{1,0:T(8,128)(2,1)} %shard_map.131), channel_id=1, source_target_pairs={{64,0},{96,32},{0,64},{32,96},{65,1},{97,33},{1,65},{33,97},{66,2}... | collective-permute-start | bytes 196616 | tf_op jit(solution)/shard_map/ppermute | solution.py:431
  98.5 5.4 %collective-permute-start.13 = (bf16[64,512]{1,0:T(8,128)(2,1)}, bf16[64,512]{1,0:T(8,128)(2,1)S(1)}, u32[]{:S(2)}, u32[]{:S(2)}) collective-permute-start(bf16[64,512]{1,0:T(8,128)(2,1)} %shard_map.131), channel_id=1, source_target_pairs={{96,0},{0,32},{32,64},{64,96},{97,1},{1,33},{33,65},{65,97},{98,2}... | collective-permute-start | bytes 196616 | tf_op jit(solution)/shard_map/ppermute | solution.py:431
  104.8 5.3 %collective-permute-start.14 = (bf16[4,64,512]{2,1,0:T(8,128)(2,1)S(1)}, bf16[4,64,512]{2,1,0:T(8,128)(2,1)S(1)}, u32[]{:S(2)}, u32[]{:S(2)}) collective-permute-start(bf16[4,64,512]{2,1,0:T(8,128)(2,1)S(1)} %get-tuple-element.60), channel_id=1, source_target_pairs={{4,0},{5,1},{6,2},{7,3},{8,4},{9,5},{10,6},{11,7},{12,8},{13,9},{1... | collective-permute-start | bytes 786440 | tf_op jit(solution)/shard_map/ppermute | solution.py:442
  105.7 7.1 %collective-permute-start.15 = (bf16[4,64,512]{2,1,0:T(8,128)(2,1)S(1)}, bf16[4,64,512]{2,1,0:T(8,128)(2,1)S(1)}, u32[]{:S(2)}, u32[]{:S(2)}) collective-permute-start(bf16[4,64,512]{2,1,0:T(8,128)(2,1)S(1)} %get-tuple-element.60), channel_id=1, source_target_pairs={{8,0},{9,1},{10,2},{11,3},{12,4},{13,5},{14,6},{15,7},{0,8},{1,9},... | collective-permute-start | bytes 786440 | tf_op jit(solution)/shard_map/ppermute | solution.py:442
  106.5 10.5 %collective-permute-start.16 = (bf16[4,64,512]{2,1,0:T(8,128)(2,1)S(1)}, bf16[4,64,512]{2,1,0:T(8,128)(2,1)S(1)}, u32[]{:S(2)}, u32[]{:S(2)}) collective-permute-start(bf16[4,64,512]{2,1,0:T(8,128)(2,1)S(1)} %get-tuple-element.60), channel_id=1, source_target_pairs={{12,0},{13,1},{14,2},{15,3},{0,4},{1,5},{2,6},{3,7},{4,8},{5,9},{6... | collective-permute-start | bytes 786440 | tf_op jit(solution)/shard_map/ppermute | solution.py:442
  117.2 18.0 %collective-permute-start.17 = (bf16[4,4,64,512]{3,2,1,0:T(8,128)(2,1)S(1)}, bf16[4,4,64,512]{3,2,1,0:T(8,128)(2,1)S(1)}, u32[]{:S(2)}, u32[]{:S(2)}) collective-permute-start(bf16[4,4,64,512]{3,2,1,0:T(8,128)(2,1)S(1)} %pad_maximum_fusion.refs_2_), channel_id=1, source_target_pairs={{1,0},{2,1},{3,2},{0,3},{5,4},{6,5},{7,6},{4,7},{9,8},{10,9},{11,1... | collective-permute-start | bytes 3145736 | tf_op jit(solution)/shard_map/ppermute | solution.py:442
  118.8 20.6 %collective-permute-start.18 = (bf16[4,4,64,512]{3,2,1,0:T(8,128)(2,1)S(1)}, bf16[4,4,64,512]{3,2,1,0:T(8,128)(2,1)S(1)}, u32[]{:S(2)}, u32[]{:S(2)}) collective-permute-start(bf16[4,4,64,512]{3,2,1,0:T(8,128)(2,1)S(1)} %pad_maximum_fusion.refs_2_), channel_id=1, source_target_pairs={{3,0},{0,1},{1,2},{2,3},{7,4},{4,5},{5,6},{6,7},{11,8},{8,9},{9,10... | collective-permute-start | bytes 3145736 | tf_op jit(solution)/shard_map/ppermute | solution.py:442
  139.4 28.2 %collective-permute-start.20 = (bf16[2,4,64,512]{3,2,1,0:T(8,128)(2,1)S(1)}, bf16[2,4,64,512]{3,2,1,0:T(8,128)(2,1)S(1)}, u32[]{:S(2)}, u32[]{:S(2)}) collective-permute-start(bf16[2,4,64,512]{3,2,1,0:T(8,128)(2,1)S(1)} %slice.14), channel_id=1, source_target_pairs={{1,0},{2,1},{3,2},{0,3},{5,4},{6,5},{7,6},{4,7},{9,8},{10,9},{11,1... | collective-permute-start | bytes 1572872 | tf_op jit(solution)/shard_map/ppermute | solution.py:442
  139.7 27.9 %collective-permute-start.21 = (bf16[2,4,64,512]{3,2,1,0:T(8,128)(2,1)S(1)}, bf16[2,4,64,512]{3,2,1,0:T(8,128)(2,1)S(1)}, u32[]{:S(2)}, u32[]{:S(2)}) collective-permute-start(bf16[2,4,64,512]{3,2,1,0:T(8,128)(2,1)S(1)} %slice.15), channel_id=1, source_target_pairs={{3,0},{0,1},{1,2},{2,3},{7,4},{4,5},{5,6},{6,7},{11,8},{8,9},{9,10... | collective-permute-start | bytes 1572872 | tf_op jit(solution)/shard_map/ppermute | solution.py:442
  179.8 4.2 %collective-permute-start.23 = (f32[1,512]{1,0:T(1,128)}, f32[1,512]{1,0:T(1,128)S(1)}, u32[]{:S(2)}, u32[]{:S(2)}) collective-permute-start(f32[1,512]{1,0:T(1,128)} %get-tuple-element.56), channel_id=1, source_target_pairs={{64,0},{96,32},{0,64},{32,96},{65,1},{97,33},{1,65},{33,97},{66,2}... | collective-permute-start | bytes 6152 | tf_op jit(solution)/shard_map/ppermute | solution.py:431
  185.0 27.5 %collective-permute-start.25 = (f32[256,768]{1,0:T(8,128)}, f32[256,768]{1,0:T(8,128)S(1)}, u32[]{:S(2)}, u32[]{:S(2)}) collective-permute-start(f32[256,768]{1,0:T(8,128)} %get-tuple-element.57), channel_id=1, source_target_pairs={{0,16},{16,0},{1,17},{17,1},{2,18},{18,2},{3,19},{19,3},{4,20},{20... | collective-permute-start | bytes 2359304 | tf_op jit(solution)/shard_map/ppermute | solution.py:532
  208.1 4.3 %collective-permute-start.32 = (f32[1,512]{1,0:T(1,128)S(1)}, f32[1,512]{1,0:T(1,128)S(1)}, u32[]{:S(2)}, u32[]{:S(2)}) collective-permute-start(f32[1,512]{1,0:T(1,128)S(1)} %log_add_fusion.no_ref), channel_id=1, source_target_pairs={{0,16},{16,0},{1,17},{17,1},{2,18},{18,2},{3,19},{19,3},{4,20},{20... | collective-permute-start | bytes 6152 | tf_op jit(solution)/shard_map/ppermute | solution.py:533
  (28 other events, 156.7 us)
Sparse Core Ops, SparseCore 0:
  9.0 54.8 all-gather.3
  73.0 76.0 all-gather.5

commit v3 on v2

--- a/solution.py
+++ b/solution.py
@@ -130,22 +130,32 @@
 
 
 def attended_rows(got_ref):
-    return got_ref[...].astype(F32)[:, 0:8, :].reshape(128, COLS).astype(BF16)
+    return got_ref[...].astype(F32)[:, 0:8, :].reshape(128, COLS)
+
+
+def split_kinds(rows, kinds_s):
+    kinds = [[], []]
+    for j in range(COLS // HD):
+        kinds_s[j] = rows[:, j * HD : (j + 1) * HD]
+        for kind in range(2):
+            kinds[kind].append(kinds_s[j, pl.ds(kind, REQ, stride=2), :])
+    return [jnp.concatenate(parts, axis=1) for parts in kinds]
 
 
 WIDE = 4
 
 
-def projection_kernel(got_ref, w_ref, o_ref, att_s):
+def projection_kernel(got_ref, w_ref, expert_ref, amateur_ref, att_s, kinds_s):
     @pl.when(pl.program_id(0) == 0)
     def _():
-        att_s[...] = attended_rows(got_ref)
+        att_s[...] = jnp.concatenate(split_kinds(attended_rows(got_ref), kinds_s), axis=0).astype(BF16)
 
     for t in range(WIDE):
         part = jnp.dot(
             att_s[...], w_ref[:, t * COLS : (t + 1) * COLS], preferred_element_type=F32
         )
-        o_ref[t] = part.astype(BF16)
+        expert_ref[t] = part[:REQ].astype(BF16)
+        amateur_ref[t] = part[REQ:].astype(BF16)
 
 
 def projection(got, weight):
@@ -156,9 +166,12 @@
             pl.BlockSpec((TEN, 16, COLS), lambda j: (0, 0, 0)),
             pl.BlockSpec((COLS, WIDE * COLS), lambda j: (0, j)),
         ],
-        out_specs=pl.BlockSpec((WIDE, 128, COLS), lambda j: (j, 0, 0)),
-        out_shape=jax.ShapeDtypeStruct((TEN, 128, COLS), BF16),
-        scratch_shapes=[pltpu.VMEM((128, COLS), BF16)],
+        out_specs=[pl.BlockSpec((WIDE, REQ, COLS), lambda j: (j, 0, 0))] * 2,
+        out_shape=[jax.ShapeDtypeStruct((TEN, REQ, COLS), BF16)] * 2,
+        scratch_shapes=[
+            pltpu.VMEM((128, COLS), BF16),
+            pltpu.VMEM((COLS // HD, 128, HD), F32),
+        ],
         compiler_params=params(56),
         cost_estimate=pl.CostEstimate(flops=11 * 10**8, bytes_accessed=11 * MIB, transcendentals=0),
     )(got, weight)
@@ -166,7 +179,7 @@
 
 def rank_kernel(idx_ref, got_ref, table_ref, o_ref, rows_s, sem):
     start_rows(idx_ref, [table_ref], rows_s, sem)
-    attended = attended_rows(got_ref)
+    attended = attended_rows(got_ref).astype(BF16)
     wait_rows(table_ref, rows_s, sem)
     rows = rows_s[...].reshape(REQ * RANK, COLS)
     product = lax.dot_general(attended, rows, LAST, preferred_element_type=F32)
@@ -191,39 +204,42 @@
     )(index, got, table)
 
 
-def sum_kernel(sums_ref, got_ref, gain_ref, expert_ref, amateur_ref, hid_s):
+def add_all(sums_ref):
     total = sums_ref[0].astype(F32)
     for t in range(1, TEN):
         total = total + sums_ref[t].astype(F32)
-    total = total + got_ref[...].astype(F32)[:, 8:16, :].reshape(128, COLS)
-    for j in range(COLS // HD):
-        lanes = slice(j * HD, (j + 1) * HD)
-        hid_s[j] = total[:, lanes]
-        expert_ref[:, lanes] = hid_s[j, pl.ds(0, REQ, stride=2), :]
-        hidden = hid_s[j, pl.ds(1, REQ, stride=2), :].astype(BF16).astype(F32)
-        amateur_ref[:, lanes] = (hidden * gain_ref[:, lanes].astype(F32)).astype(BF16)
-
-
-def summed_rows(sums, got, gain):
+    return total
+
+
+def residual_rows(got_ref):
+    return got_ref[...].astype(F32)[:, 8:16, :].reshape(128, COLS)
+
+
+def amateur_kernel(sums_ref, got_ref, gain_ref, o_ref, kinds_s):
+    base = split_kinds(residual_rows(got_ref), kinds_s)[1]
+    hidden = (base + add_all(sums_ref)).astype(BF16).astype(F32)
+    o_ref[...] = (hidden * gain_ref[...].astype(F32)).astype(BF16)
+
+
+def amateur_rows(sums, got, gain):
     near = pl.BlockSpec(memory_space=pltpu.VMEM)
     return pl.pallas_call(
-        sum_kernel,
+        amateur_kernel,
         in_specs=[near] * 3,
-        out_specs=[near, near],
-        out_shape=[
-            jax.ShapeDtypeStruct((REQ, COLS), F32),
-            jax.ShapeDtypeStruct((REQ, COLS), BF16),
-        ],
+        out_specs=near,
+        out_shape=jax.ShapeDtypeStruct((REQ, COLS), BF16),
         scratch_shapes=[pltpu.VMEM((COLS // HD, 128, HD), F32)],
         compiler_params=params(16),
-        cost_estimate=pl.CostEstimate(flops=2 * 10**6, bytes_accessed=3 * MIB, transcendentals=0),
+        cost_estimate=pl.CostEstimate(flops=10**6, bytes_accessed=2 * MIB, transcendentals=0),
     )(sums, got, gain)
 
 
 def expert_kernel(
-    slot_ref, base_ref, k0_ref, k1_ref, k2_ref, k3_ref, gain_ref, own_ref, sib_ref, o_ref, rows_s, sem
+    slot_ref, sums_ref, got_ref, k0_ref, k1_ref, k2_ref, k3_ref, gain_ref, own_ref, sib_ref,
+    o_ref, rows_s, kinds_s, sem,
 ):
     start_rows(slot_ref, [own_ref, sib_ref], rows_s, sem)
+    base = split_kinds(residual_rows(got_ref), kinds_s)[0] + add_all(sums_ref)
     rank = (k0_ref[...] + k1_ref[...]) + (k2_ref[...] + k3_ref[...])
     spread = jnp.where(own_lanes(REQ, REQ * RANK, 1), rank, 0.0)
     high = spread.astype(BF16)
@@ -232,23 +248,27 @@
     rows = rows_s[...].reshape(REQ * RANK, COLS)
     delta = jnp.dot(high, rows, preferred_element_type=F32)
     delta = delta + jnp.dot(low, rows, preferred_element_type=F32)
-    hidden = (base_ref[...] + LOWRANK_SCALE * delta).astype(BF16).astype(F32)
+    hidden = (base + LOWRANK_SCALE * delta).astype(BF16).astype(F32)
     o_ref[...] = (hidden * gain_ref[...].astype(F32)).astype(BF16)
 
 
-def expert_rows(slots, base, rank, gain, own, sib):
+def expert_rows(slots, sums, got, rank, gain, own, sib):
     near = pl.BlockSpec(memory_space=pltpu.VMEM)
     return pl.pallas_call(
         expert_kernel,
         in_specs=[pl.BlockSpec(memory_space=pltpu.SMEM)]
-        + [near] * 6
+        + [near] * 7
         + [pl.BlockSpec(memory_space=pl.ANY)] * 2,
         out_specs=near,
         out_shape=jax.ShapeDtypeStruct((REQ, COLS), BF16),
-        scratch_shapes=[pltpu.VMEM((REQ, RANK, COLS), BF16), pltpu.SemaphoreType.DMA],
+        scratch_shapes=[
+            pltpu.VMEM((REQ, RANK, COLS), BF16),
+            pltpu.VMEM((COLS // HD, 128, HD), F32),
+            pltpu.SemaphoreType.DMA,
+        ],
         compiler_params=params(56),
         cost_estimate=pl.CostEstimate(flops=3 * 10**8, bytes_accessed=2 * MIB, transcendentals=0),
-    )(slots, base, *rank, gain, own, sib)
+    )(slots, sums, got, *rank, gain, own, sib)
 
 
 def tensor_index(at, first, second):
@@ -490,22 +510,23 @@
         residual,
     )
     got = lax.all_to_all(sent, TENSOR, split_axis=0, concat_axis=0, tiled=True)
-    partial = projection(got, output_projection_weight)
-    up_after, up_before, partial = lax.optimization_barrier((up_after, up_before, partial))
-    sums = lax.all_to_all(partial, TENSOR, split_axis=0, concat_axis=0, tiled=True)
-    rank = rank_sums(request_adapter_index, got, down)
+    expert, amateur = projection(got, output_projection_weight)
+    amateur = lax.all_to_all(amateur, TENSOR, split_axis=0, concat_axis=0, tiled=True)
+    sums = lax.all_to_all(expert, TENSOR, split_axis=0, concat_axis=0, tiled=True)
+    amateur = amateur_rows(amateur, got, gain)
+    up_after, up_before, amateur = lax.optimization_barrier((up_after, up_before, amateur))
+    gathered = lax.all_gather(amateur, ("y", "x", "z"), axis=0, tiled=False)
+    gathered = gathered.reshape(NY, TEN, REQ, COLS)
     half = HELD // 2
     up_far = (from_offset(up_after[:half], "y", 1), from_offset(up_before[half:], "y", 3))
     up_own = jnp.concatenate([lowrank_up_factors, up_after, *up_far, up_before], axis=0)
     up_own, sums = lax.optimization_barrier((up_own, sums))
     up_sib = lax.ppermute(up_own, "c", SWAP)
-    base, amateur = summed_rows(sums, got, gain)
-    gathered = lax.all_gather(amateur, ("y", "x", "z"), axis=0, tiled=False)
-    gathered = gathered.reshape(NY, TEN, REQ, COLS)
-    rank, base = lax.optimization_barrier((rank, base))
+    rank = rank_sums(request_adapter_index, got, down)
+    rank, sums = lax.optimization_barrier((rank, sums))
     rank = sum([from_offset(rank, "x", d) for d in range(1, 4)], rank)
     rank = [rank] + [from_offset(rank, "z", d) for d in range(1, 4)]
-    expert = expert_rows(slots, base, rank, gain, up_own, up_sib)
+    expert = expert_rows(slots, sums, got, rank, gain, up_own, up_sib)
 
     plane = jnp.stack([expert] + [from_offset(expert, "y", d) for d in range(1, 4)])
     after = from_core_offset(plane, FIRST, 1)
@@ -516,13 +537,13 @@
     weights = (inverse, vocabulary_head_matrix, head_sib)
     pieces = [(0, n, (n, 0)) for n in range(4)]
     partial = head_part(place, [mine], pieces, *weights)
-    after, before, *partial = lax.optimization_barrier((after, before, *partial))
+    pieces = [(0, n, None) for n in range(TEN)]
+    other = head_part(place, [gathered], pieces, *weights, amateur=True)
+    after, before, *rest = lax.optimization_barrier((after, before, *partial, *other))
+    partial, other = rest[:2], rest[2:]
     far = opposite(after, before, SECOND)
     pieces = [(n // 4, n % 4, (n % 4, 1 + 2 * (n // 4))) for n in range(8)]
     partial = head_part(place, [after, before], pieces, *weights, sums=partial)
-    gathered, *partial = lax.optimization_barrier((gathered, *partial))
-    pieces = [(0, n, None) for n in range(TEN)]
-    other = head_part(place, [gathered], pieces, *weights, amateur=True)
     pieces = [(n // 2, n % 2, (n, 2)) for n in range(4)]
     u_own, u_send, lse = head_part(place, far, pieces, *weights, sums=partial, other=other)
     for axis in ("y", "x", "z"):

time: 223 us -> 227 us (1.018)
  local copies, waits for them, and re-layouts: 14.6 us -> 6.06 us
  starting transfers between devices: 53.8 us -> 59.9 us
  waiting for transfers between devices: 59 us -> 65.1 us
    all_to_all x1 -> x2, waiting for transfers between devices: 4.26 us -> 16 us  [the longest x1 12.1 us: per_device(): lax.all_to_all(amateur, TENSOR, split_axis=0, concat_axis=0, tiled=True)]
    ppermute x22, starting transfers between devices: 17 us -> 25 us  [from_offset(): return lax.ppermute(array, axis, [((i + offset) % 4, i) for i in range(4)])]
    ppermute x7, waiting for transfers between devices: 23.4 us -> 15.7 us  [from_core_offset(): return lax.ppermute(array, ('c', 'x', 'z'), pairs)]
    unnamed x36 -> x40, local copies, waits for them, and re-layouts: 10.3 us -> 5.78 us
    ppermute x1, starting transfers between devices: 12.9 us -> 8.79 us  [per_device(): u_sib = lax.ppermute(u_send, 'c', SWAP)]
    all_to_all x1 -> x2, starting transfers between devices: 7.82 us -> 10.4 us  [the longest x1 6.63 us: per_device(): lax.all_to_all(expert, TENSOR, split_axis=0, concat_axis=0, tiled=True)]
    ppermute x1, starting transfers between devices: 5.59 us -> 3.22 us  [per_device(): up_sib = lax.ppermute(up_own, 'c', SWAP)]
    ppermute x7, starting transfers between devices: 5.35 us -> 7.66 us  [from_core_offset(): return lax.ppermute(array, ('c', 'x', 'z'), pairs)]
  transfers between devices with their start and end apart: 36 -> 37, of which waited for: 25 -> 24; matrix products, arithmetic and copies ran while one was open for 7% -> 3% of each run, Pallas kernels for 23% -> 23%
where the time goes in v3:
time: 227 us; the launch traced here: 226 us
  waiting for transfers between devices  65.1 us (29%)
  Pallas kernels  61.3 us (27%)
  starting transfers between devices  59.9 us (26%)
  blocking collectives  15.6 us (7%)
  between operations  13.7 us (6%)
  local copies, waits for them, and re-layouts  6.06 us (3%)
  other arithmetic  4.33 us (2%)
    pallas_call x4, Pallas kernels, head_part(): pl.pallas_call(lambda *refs: head_kernel(pieces, first, last, amateur, *r...  40.9 us
    ppermute x22, waiting for transfers between devices, from_offset(): return lax.ppermute(array, axis, [((i + offset) % 4, i) for i in range(4)])  31.9 us
    ppermute x22, starting transfers between devices, from_offset(): return lax.ppermute(array, axis, [((i + offset) % 4, i) for i in range(4)])  25 us
    ppermute x7, waiting for transfers between devices, from_core_offset(): return lax.ppermute(array, ('c', 'x', 'z'), pairs)  15.7 us
    all_to_all x1, blocking collectives, per_device(): got = lax.all_to_all(sent, TENSOR, split_axis=0, concat_axis=0, tiled=True)  15.6 us
    all_to_all x1, waiting for transfers between devices, per_device(): lax.all_to_all(amateur, TENSOR, split_axis=0, concat_axis=0, tiled=True)  12.1 us
    ppermute x1, starting transfers between devices, per_device(): u_sib = lax.ppermute(u_send, 'c', SWAP)  8.79 us
    ppermute x7, starting transfers between devices, from_core_offset(): return lax.ppermute(array, ('c', 'x', 'z'), pairs)  7.66 us
  transfers between devices with their start and end apart: 37, of which 24 were waited for; matrix products, arithmetic and copies ran while one was open for 3% of the time, Pallas kernels for 23%

profile of v3, /device:TPU:1, one launch (start us, length us, event | category | flops | bytes accessed | tf_op | source)
XLA Modules:
  0.0 226.0 jit_solution(6535236621520915561)
XLA Ops:
  8.8 5.0 %shard_map.127 = bf16[16,16,512]{2,1,0:T(8,128)(2,1)} custom-call(s32[4]{0:T(128)} %len_ref.1, bf16[4,2,8192]{2,1,0:T(2,128)(2,1)} %q_ref.1, bf16[4,2,64,1024]{3,2,1,0:T(8,128)(2,1)} %k_ref.1, bf16[4,2,64,1024]{3,2,1,0:T(8,128)(2,1)} %v_ref.1, bf16[4,2,1024]{2,1,0:T(2,128)(2,1)} %ck_ref.1, bf16[4,2,1024]{2,1,0:T(2,128)(2,1)} %cv_ref.1, ...), custom_call_target="tpu_custom_call" | custom-call | flops 300000000 | bytes 3145728 | tf_op jit(solution)/shard_map/pallas_call | solution.py:81
  13.7 15.6 %all_to_all.15.got_ref = bf16[16,16,512]{2,1,0:T(8,128)(2,1)} all-to-all(bf16[16,16,512]{2,1,0:T(8,128)(2,1)} %shard_map.127), channel_id=1, replica_groups=mesh['y'=4,'c'=2,'x'=4,'z'=4] {'x','z'}, dimensions={0} | all-to-all | bytes 524288 | tf_op jit(solution)/shard_map/all_to_all | solution.py:512
  29.3 6.2 %shard_map.129 = (bf16[16,64,512]{2,1,0:T(8,128)(2,1)}, bf16[16,64,512]{2,1,0:T(8,128)(2,1)}) custom-call(bf16[16,16,512]{2,1,0:T(8,128)(2,1)} %all_to_all.15.got_ref, bf16[512,8192]{1,0:T(8,128)(2,1)} %w_ref.1), custom_call_target="tpu_custom_call" | custom-call | flops 1100000000 | bytes 11534336 | tf_op jit(solution)/shard_map/pallas_call | solution.py:162
  35.5 3.8 %all-to-all-start.1 = ((bf16[16,64,512]{2,1,0:T(8,128)(2,1)}), bf16[16,64,512]{2,1,0:T(8,128)(2,1)S(1)}, u32[]{:S(2)}, u32[]{:S(2)}) async-start(bf16[16,64,512]{2,1,0:T(8,128)(2,1)} %get-tuple-element.31), calls=%async_computation.1 | async-start | bytes 2097152 | tf_op jit(solution)/shard_map/all_to_all | solution.py:514
  39.3 3.0 %collective-permute-start = (bf16[48,16,512]{2,1,0:T(8,128)(2,1)}, bf16[48,16,512]{2,1,0:T(8,128)(2,1)S(1)}, u32[]{:S(2)}, u32[]{:S(2)}) collective-permute-start(bf16[48,16,512]{2,1,0:T(8,128)(2,1)} %param.23), channel_id=1, source_target_pairs={{32,0},{64,32},{96,64},{0,96},{33,1},{65,33},{97,65},{1,97},{34,2}... | collective-permute-start | bytes 2359304 | tf_op jit(solution)/shard_map/ppermute | solution.py:451
  42.5 12.1 %all-to-all-done.1.sums_ref = bf16[16,64,512]{2,1,0:T(8,128)(2,1)S(1)} async-done(((bf16[16,64,512]{2,1,0:T(8,128)(2,1)}), bf16[16,64,512]{2,1,0:T(8,128)(2,1)S(1)}, u32[]{:S(2)}, u32[]{:S(2)}) %all-to-all-start.1) | async-done | bytes 1048608 | tf_op jit(solution)/shard_map/all_to_all | solution.py:514
  55.3 11.8 %collective-permute-done = bf16[48,16,512]{2,1,0:T(8,128)(2,1)S(1)} collective-permute-done((bf16[48,16,512]{2,1,0:T(8,128)(2,1)}, bf16[48,16,512]{2,1,0:T(8,128)(2,1)S(1)}, u32[]{:S(2)}, u32[]{:S(2)}) %collective-permute-start) | collective-permute-done | bytes 786464 | tf_op jit(solution)/shard_map/ppermute | solution.py:451
  67.9 6.6 %all-to-all-start.2 = ((bf16[16,64,512]{2,1,0:T(8,128)(2,1)}), bf16[16,64,512]{2,1,0:T(8,128)(2,1)}, u32[]{:S(2)}, u32[]{:S(2)}) async-start(bf16[16,64,512]{2,1,0:T(8,128)(2,1)} %get-tuple-element.34), calls=%async_computation.2 | async-start | bytes 2097152 | tf_op jit(solution)/shard_map/all_to_all | solution.py:515
  78.7 5.4 %collective-permute-done.2 = bf16[24,16,512]{2,1,0:T(8,128)(2,1)S(1)} collective-permute-done((bf16[24,16,512]{2,1,0:T(8,128)(2,1)S(1)}, bf16[24,16,512]{2,1,0:T(8,128)(2,1)S(1)}, u32[]{:S(2)}, u32[]{:S(2)}) %collective-permute-start.2) | collective-permute-done | bytes 393248 | tf_op jit(solution)/shard_map/ppermute | solution.py:451
  86.1 3.9 %all-to-all-done.2.sums_ref = bf16[16,64,512]{2,1,0:T(8,128)(2,1)} async-done(((bf16[16,64,512]{2,1,0:T(8,128)(2,1)}), bf16[16,64,512]{2,1,0:T(8,128)(2,1)}, u32[]{:S(2)}, u32[]{:S(2)}) %all-to-all-start.2) | async-done | bytes 1048608 | tf_op jit(solution)/shard_map/all_to_all | solution.py:515
  90.1 3.2 %collective-permute-start.10 = (bf16[192,16,512]{2,1,0:T(8,128)(2,1)S(1)}, bf16[192,16,512]{2,1,0:T(8,128)(2,1)}, u32[]{:S(2)}, u32[]{:S(2)}) collective-permute-start(bf16[192,16,512]{2,1,0:T(8,128)(2,1)S(1)} %constant_dynamic-update-slice_fusion.own_ref), channel_id=1, source_target_pairs={{0,16},{16,0},{1,17},{17,1},{2,18},{18,2},{3,19},{19,3},{4,20},{20... | collective-permute-start | bytes 9437192 | tf_op jit(solution)/shard_map/ppermute | solution.py:524
  93.3 3.2 %shard_map.128 = f32[1,1024]{1,0:T(1,128)} custom-call(s32[64]{0:T(128)} %idx_ref.1, bf16[16,16,512]{2,1,0:T(8,128)(2,1)} %all_to_all.15.got_ref, bf16[384,16,512]{2,1,0:T(8,128)(2,1)} %all-gather.4.cloned.1.call-done.table_ref), custom_call_target="tpu_custom_call" | custom-call | flops 140000000 | bytes 2097152 | tf_op jit(solution)/shard_map/pallas_call | solution.py:192
  107.8 3.7 %shard_map.131 = bf16[64,512]{1,0:T(8,128)(2,1)} custom-call(s32[64]{0:T(128)} %fusion.1.slot_ref, bf16[16,64,512]{2,1,0:T(8,128)(2,1)} %all-to-all-done.2.sums_ref, bf16[16,16,512]{2,1,0:T(8,128)(2,1)} %all_to_all.15.got_ref, f32[1,1024]{1,0:T(1,128)} %copy-done.13, f32[1,1024]{1,0:T(1,128)} %copy-done.16, f32[1,1024]{1,0:T(1,128)} %copy-done.15, ...), custom_call_target="tpu_custom_call" | custom-call | flops 300000000 | bytes 2097152 | tf_op jit(solution)/shard_map/pallas_call | solution.py:257
  121.7 4.7 %collective-permute-done.15 = bf16[4,64,512]{2,1,0:T(8,128)(2,1)S(1)} collective-permute-done((bf16[4,64,512]{2,1,0:T(8,128)(2,1)S(1)}, bf16[4,64,512]{2,1,0:T(8,128)(2,1)S(1)}, u32[]{:S(2)}, u32[]{:S(2)}) %collective-permute-start.15) | collective-permute-done | bytes 262176 | tf_op jit(solution)/shard_map/ppermute | solution.py:462
  126.4 11.0 %collective-permute-done.14 = bf16[4,64,512]{2,1,0:T(8,128)(2,1)S(1)} collective-permute-done((bf16[4,64,512]{2,1,0:T(8,128)(2,1)S(1)}, bf16[4,64,512]{2,1,0:T(8,128)(2,1)S(1)}, u32[]{:S(2)}, u32[]{:S(2)}) %collective-permute-start.14) | collective-permute-done | bytes 262176 | tf_op jit(solution)/shard_map/ppermute | solution.py:462
  141.5 6.2 %shard_map.132 = (f32[256,1536]{1,0:T(8,128)}, f32[256,128]{1,0:T(8,128)}) custom-call(s32[4]{0:T(128)} %pad_add_fusion.refs_0_, f32[1,8192]{1,0:T(1,128)} %bitcast.16, bf16[4,4,64,512]{3,2,1,0:T(8,128)(2,1)} %copy-done.4, bf16[8192,768]{1,0:T(8,128)(2,1)} %refs_4_.3, bf16[8192,768]{1,0:T(8,128)(2,1)} %collective-permute-done.19.refs_4_.refs_5_), custom_call_target="tpu_custom_call" | custom-call | flops 524288 | bytes 131072 | tf_op jit(solution)/shard_map/pallas_call | solution.py:384
  147.7 14.4 %shard_map.133 = (f32[256,1536]{1,0:T(8,128)}, f32[1,256]{1,0:T(1,128)}) custom-call(s32[4]{0:T(128)} %pad_add_fusion.refs_0_, f32[1,8192]{1,0:T(1,128)} %bitcast.17, bf16[4,16,64,512]{3,2,1,0:T(8,128)(2,1)} %bitcast.15, bf16[8192,768]{1,0:T(8,128)(2,1)} %refs_4_.3, bf16[8192,768]{1,0:T(8,128)(2,1)} %collective-permute-done.19.refs_4_.refs_5_), custom_call_target="tpu_custom_call" | custom-call | flops 2097152 | bytes 524288 | tf_op jit(solution)/shard_map/pallas_call | solution.py:384
  163.8 11.8 %shard_map.134 = (f32[256,1536]{1,0:T(8,128)}, f32[256,128]{1,0:T(8,128)}) custom-call(s32[4]{0:T(128)} %pad_add_fusion.refs_0_, f32[1,8192]{1,0:T(1,128)} %bitcast.18, bf16[4,4,64,512]{3,2,1,0:T(8,128)(2,1)} %copy-done.6, bf16[4,4,64,512]{3,2,1,0:T(8,128)(2,1)} %copy-done.5, bf16[8192,768]{1,0:T(8,128)(2,1)} %refs_4_.3, ...), custom_call_target="tpu_custom_call" | custom-call | flops 1048576 | bytes 262144 | tf_op jit(solution)/shard_map/pallas_call | solution.py:384
  176.6 8.5 %shard_map.135 = (f32[256,768]{1,0:T(8,128)}, f32[256,768]{1,0:T(8,128)}, f32[1,512]{1,0:T(1,128)}) custom-call(s32[4]{0:T(128)} %pad_add_fusion.refs_0_, f32[1,8192]{1,0:T(1,128)} %bitcast.19, bf16[2,4,64,512]{3,2,1,0:T(8,128)(2,1)} %copy-done.10, bf16[2,4,64,512]{3,2,1,0:T(8,128)(2,1)} %copy-done.11, bf16[8192,768]{1,0:T(8,128)(2,1)} %refs_4_.3, ...), custom_call_target="tpu_custom_call" | custom-call | flops 524288 | bytes 131072 | tf_op jit(solution)/shard_map/pallas_call | solution.py:384
  185.4 2.6 %collective-permute-start.23 = (f32[1,512]{1,0:T(1,128)}, f32[1,512]{1,0:T(1,128)S(1)}, u32[]{:S(2)}, u32[]{:S(2)}) collective-permute-start(f32[1,512]{1,0:T(1,128)} %get-tuple-element.54), channel_id=1, source_target_pairs={{64,0},{96,32},{0,64},{32,96},{65,1},{97,33},{1,65},{33,97},{66,2}... | collective-permute-start | bytes 6152 | tf_op jit(solution)/shard_map/ppermute | solution.py:451
  191.4 8.8 %collective-permute-start.25 = (f32[256,768]{1,0:T(8,128)}, f32[256,768]{1,0:T(8,128)S(1)}, u32[]{:S(2)}, u32[]{:S(2)}) collective-permute-start(f32[256,768]{1,0:T(8,128)} %get-tuple-element.55), channel_id=1, source_target_pairs={{0,16},{16,0},{1,17},{17,1},{2,18},{18,2},{3,19},{19,3},{4,20},{20... | collective-permute-start | bytes 2359304 | tf_op jit(solution)/shard_map/ppermute | solution.py:553
  200.2 3.2 %collective-permute-start.27 = (f32[1,512]{1,0:T(1,128)S(1)}, f32[1,512]{1,0:T(1,128)S(1)}, u32[]{:S(2)}, u32[]{:S(2)}) collective-permute-start(f32[1,512]{1,0:T(1,128)S(1)} %log_add_fusion.2), channel_id=1, source_target_pairs={{8,0},{12,4},{0,8},{4,12},{9,1},{13,5},{1,9},{5,13},{10,2},{14,6},... | collective-permute-start | bytes 6152 | tf_op jit(solution)/shard_map/ppermute | solution.py:451
  205.9 3.9 %collective-permute-start.30 = (f32[1,512]{1,0:T(1,128)S(1)}, f32[1,512]{1,0:T(1,128)S(1)}, u32[]{:S(2)}, u32[]{:S(2)}) collective-permute-start(f32[1,512]{1,0:T(1,128)S(1)} %log_add_fusion.1), channel_id=1, source_target_pairs={{2,0},{3,1},{0,2},{1,3},{6,4},{7,5},{4,6},{5,7},{10,8},{11,9},{8,1... | collective-permute-start | bytes 6152 | tf_op jit(solution)/shard_map/ppermute | solution.py:451
  212.5 3.3 %collective-permute-start.32 = (f32[1,512]{1,0:T(1,128)S(1)}, f32[1,512]{1,0:T(1,128)S(1)}, u32[]{:S(2)}, u32[]{:S(2)}) collective-permute-start(f32[1,512]{1,0:T(1,128)S(1)} %log_add_fusion.no_ref), channel_id=1, source_target_pairs={{0,16},{16,0},{1,17},{17,1},{2,18},{18,2},{3,19},{19,3},{4,20},{20... | collective-permute-start | bytes 6152 | tf_op jit(solution)/shard_map/ppermute | solution.py:554
  (119 shorter events, 50.3 us)
Async XLA Ops:
  6.5 86.8 %all-gather.4.cloned.1.call-start = ((), (), s32[]{:S(2)}) async-start(), calls=%async_computation.3 | async-start | bytes 7077888 | tf_op jit(solution)/shard_map/all_gather | solution.py:492
  7.3 134.2 %collective-permute-start.19 = (bf16[8192,768]{1,0:T(8,128)(2,1)}, bf16[8192,768]{1,0:T(8,128)(2,1)}, u32[]{:S(2)}, u32[]{:S(2)}) collective-permute-start(bf16[8192,768]{1,0:T(8,128)(2,1)} %refs_4_.3), channel_id=1, source_target_pairs={{0,16},{16,0},{1,17},{17,1},{2,18},{18,2},{3,19},{19,3},{4,20},{20... | collective-permute-start | bytes 37748744 | tf_op jit(solution)/shard_map/ppermute | solution.py:491
  35.5 19.0 %all-to-all-start.1 = ((bf16[16,64,512]{2,1,0:T(8,128)(2,1)}), bf16[16,64,512]{2,1,0:T(8,128)(2,1)S(1)}, u32[]{:S(2)}, u32[]{:S(2)}) async-start(bf16[16,64,512]{2,1,0:T(8,128)(2,1)} %get-tuple-element.31), calls=%async_computation.1 | async-start | bytes 2097152 | tf_op jit(solution)/shard_map/all_to_all | solution.py:514
  39.3 108.4 %all-gather.6.cloned.1.call-start = ((), (), s32[]{:S(2)}) async-start(), calls=%async_computation.4 | async-start | bytes 4259840 | tf_op jit(solution)/shard_map/all_gather | solution.py:518
  39.3 27.8 %collective-permute-start = (bf16[48,16,512]{2,1,0:T(8,128)(2,1)}, bf16[48,16,512]{2,1,0:T(8,128)(2,1)S(1)}, u32[]{:S(2)}, u32[]{:S(2)}) collective-permute-start(bf16[48,16,512]{2,1,0:T(8,128)(2,1)} %param.23), channel_id=1, source_target_pairs={{32,0},{64,32},{96,64},{0,96},{33,1},{65,33},{97,65},{1,97},{34,2}... | collective-permute-start | bytes 2359304 | tf_op jit(solution)/shard_map/ppermute | solution.py:451
  42.4 25.5 %collective-permute-start.1 = (bf16[48,16,512]{2,1,0:T(8,128)(2,1)}, bf16[48,16,512]{2,1,0:T(8,128)(2,1)S(1)}, u32[]{:S(2)}, u32[]{:S(2)}) collective-permute-start(bf16[48,16,512]{2,1,0:T(8,128)(2,1)} %param.23), channel_id=1, source_target_pairs={{96,0},{0,32},{32,64},{64,96},{97,1},{1,33},{33,65},{65,97},{98,2}... | collective-permute-start | bytes 2359304 | tf_op jit(solution)/shard_map/ppermute | solution.py:451
  67.9 22.2 %all-to-all-start.2 = ((bf16[16,64,512]{2,1,0:T(8,128)(2,1)}), bf16[16,64,512]{2,1,0:T(8,128)(2,1)}, u32[]{:S(2)}, u32[]{:S(2)}) async-start(bf16[16,64,512]{2,1,0:T(8,128)(2,1)} %get-tuple-element.34), calls=%async_computation.2 | async-start | bytes 2097152 | tf_op jit(solution)/shard_map/all_to_all | solution.py:515
  74.6 9.5 %collective-permute-start.2 = (bf16[24,16,512]{2,1,0:T(8,128)(2,1)S(1)}, bf16[24,16,512]{2,1,0:T(8,128)(2,1)S(1)}, u32[]{:S(2)}, u32[]{:S(2)}) collective-permute-start(bf16[24,16,512]{2,1,0:T(8,128)(2,1)S(1)} %slice.12), channel_id=1, source_target_pairs={{32,0},{64,32},{96,64},{0,96},{33,1},{65,33},{97,65},{1,97},{34,2}... | collective-permute-start | bytes 1179656 | tf_op jit(solution)/shard_map/ppermute | solution.py:451
  75.5 10.5 %collective-permute-start.3 = (bf16[24,16,512]{2,1,0:T(8,128)(2,1)S(1)}, bf16[24,16,512]{2,1,0:T(8,128)(2,1)S(1)}, u32[]{:S(2)}, u32[]{:S(2)}) collective-permute-start(bf16[24,16,512]{2,1,0:T(8,128)(2,1)S(1)} %slice.13), channel_id=1, source_target_pairs={{96,0},{0,32},{32,64},{64,96},{97,1},{1,33},{33,65},{65,97},{98,2}... | collective-permute-start | bytes 1179656 | tf_op jit(solution)/shard_map/ppermute | solution.py:451
  90.1 15.9 %collective-permute-start.10 = (bf16[192,16,512]{2,1,0:T(8,128)(2,1)S(1)}, bf16[192,16,512]{2,1,0:T(8,128)(2,1)}, u32[]{:S(2)}, u32[]{:S(2)}) collective-permute-start(bf16[192,16,512]{2,1,0:T(8,128)(2,1)S(1)} %constant_dynamic-update-slice_fusion.own_ref), channel_id=1, source_target_pairs={{0,16},{16,0},{1,17},{17,1},{2,18},{18,2},{3,19},{19,3},{4,20},{20... | collective-permute-start | bytes 9437192 | tf_op jit(solution)/shard_map/ppermute | solution.py:524
  96.7 4.3 %collective-permute-start.5 = (f32[1,1024]{1,0:T(1,128)}, f32[1,1024]{1,0:T(1,128)S(1)}, u32[]{:S(2)}, u32[]{:S(2)}) collective-permute-start(f32[1,1024]{1,0:T(1,128)} %shard_map.128), channel_id=1, source_target_pairs={{8,0},{12,4},{0,8},{4,12},{9,1},{13,5},{1,9},{5,13},{10,2},{14,6},... | collective-permute-start | bytes 12296 | tf_op jit(solution)/shard_map/ppermute | solution.py:451
  111.6 4.6 %collective-permute-start.13 = (bf16[64,512]{1,0:T(8,128)(2,1)}, bf16[64,512]{1,0:T(8,128)(2,1)S(1)}, u32[]{:S(2)}, u32[]{:S(2)}) collective-permute-start(bf16[64,512]{1,0:T(8,128)(2,1)} %shard_map.131), channel_id=1, source_target_pairs={{96,0},{0,32},{32,64},{64,96},{97,1},{1,33},{33,65},{65,97},{98,2}... | collective-permute-start | bytes 196616 | tf_op jit(solution)/shard_map/ppermute | solution.py:451
  112.2 4.8 %collective-permute-start.12 = (bf16[64,512]{1,0:T(8,128)(2,1)}, bf16[64,512]{1,0:T(8,128)(2,1)S(1)}, u32[]{:S(2)}, u32[]{:S(2)}) collective-permute-start(bf16[64,512]{1,0:T(8,128)(2,1)} %shard_map.131), channel_id=1, source_target_pairs={{64,0},{96,32},{0,64},{32,96},{65,1},{97,33},{1,65},{33,97},{66,2}... | collective-permute-start | bytes 196616 | tf_op jit(solution)/shard_map/ppermute | solution.py:451
  118.3 8.0 %collective-permute-start.15 = (bf16[4,64,512]{2,1,0:T(8,128)(2,1)S(1)}, bf16[4,64,512]{2,1,0:T(8,128)(2,1)S(1)}, u32[]{:S(2)}, u32[]{:S(2)}) collective-permute-start(bf16[4,64,512]{2,1,0:T(8,128)(2,1)S(1)} %get-tuple-element.58), channel_id=1, source_target_pairs={{8,0},{9,1},{10,2},{11,3},{12,4},{13,5},{14,6},{15,7},{0,8},{1,9},... | collective-permute-start | bytes 786440 | tf_op jit(solution)/shard_map/ppermute | solution.py:462
  119.9 17.5 %collective-permute-start.14 = (bf16[4,64,512]{2,1,0:T(8,128)(2,1)S(1)}, bf16[4,64,512]{2,1,0:T(8,128)(2,1)S(1)}, u32[]{:S(2)}, u32[]{:S(2)}) collective-permute-start(bf16[4,64,512]{2,1,0:T(8,128)(2,1)S(1)} %get-tuple-element.58), channel_id=1, source_target_pairs={{4,0},{5,1},{6,2},{7,3},{8,4},{9,5},{10,6},{11,7},{12,8},{13,9},{1... | collective-permute-start | bytes 786440 | tf_op jit(solution)/shard_map/ppermute | solution.py:462
  121.7 15.6 %collective-permute-start.16 = (bf16[4,64,512]{2,1,0:T(8,128)(2,1)S(1)}, bf16[4,64,512]{2,1,0:T(8,128)(2,1)S(1)}, u32[]{:S(2)}, u32[]{:S(2)}) collective-permute-start(bf16[4,64,512]{2,1,0:T(8,128)(2,1)S(1)} %get-tuple-element.58), channel_id=1, source_target_pairs={{12,0},{13,1},{14,2},{15,3},{0,4},{1,5},{2,6},{3,7},{4,8},{5,9},{6... | collective-permute-start | bytes 786440 | tf_op jit(solution)/shard_map/ppermute | solution.py:462
  137.5 24.6 %collective-permute-start.18 = (bf16[4,4,64,512]{3,2,1,0:T(8,128)(2,1)S(1)}, bf16[4,4,64,512]{3,2,1,0:T(8,128)(2,1)S(1)}, u32[]{:S(2)}, u32[]{:S(2)}) collective-permute-start(bf16[4,4,64,512]{3,2,1,0:T(8,128)(2,1)S(1)} %pad_maximum_fusion.refs_2_), channel_id=1, source_target_pairs={{3,0},{0,1},{1,2},{2,3},{7,4},{4,5},{5,6},{6,7},{11,8},{8,9},{9,10... | collective-permute-start | bytes 3145736 | tf_op jit(solution)/shard_map/ppermute | solution.py:462
  138.0 24.1 %collective-permute-start.17 = (bf16[4,4,64,512]{3,2,1,0:T(8,128)(2,1)S(1)}, bf16[4,4,64,512]{3,2,1,0:T(8,128)(2,1)S(1)}, u32[]{:S(2)}, u32[]{:S(2)}) collective-permute-start(bf16[4,4,64,512]{3,2,1,0:T(8,128)(2,1)S(1)} %pad_maximum_fusion.refs_2_), channel_id=1, source_target_pairs={{1,0},{2,1},{3,2},{0,3},{5,4},{6,5},{7,6},{4,7},{9,8},{10,9},{11,1... | collective-permute-start | bytes 3145736 | tf_op jit(solution)/shard_map/ppermute | solution.py:462
  162.2 13.4 %collective-permute-start.20 = (bf16[2,4,64,512]{3,2,1,0:T(8,128)(2,1)S(1)}, bf16[2,4,64,512]{3,2,1,0:T(8,128)(2,1)S(1)}, u32[]{:S(2)}, u32[]{:S(2)}) collective-permute-start(bf16[2,4,64,512]{3,2,1,0:T(8,128)(2,1)S(1)} %slice.14), channel_id=1, source_target_pairs={{1,0},{2,1},{3,2},{0,3},{5,4},{6,5},{7,6},{4,7},{9,8},{10,9},{11,1... | collective-permute-start | bytes 1572872 | tf_op jit(solution)/shard_map/ppermute | solution.py:462
  162.3 13.3 %collective-permute-start.21 = (bf16[2,4,64,512]{3,2,1,0:T(8,128)(2,1)S(1)}, bf16[2,4,64,512]{3,2,1,0:T(8,128)(2,1)S(1)}, u32[]{:S(2)}, u32[]{:S(2)}) collective-permute-start(bf16[2,4,64,512]{3,2,1,0:T(8,128)(2,1)S(1)} %slice.15), channel_id=1, source_target_pairs={{3,0},{0,1},{1,2},{2,3},{7,4},{4,5},{5,6},{6,7},{11,8},{8,9},{9,10... | collective-permute-start | bytes 1572872 | tf_op jit(solution)/shard_map/ppermute | solution.py:462
  185.4 4.2 %collective-permute-start.23 = (f32[1,512]{1,0:T(1,128)}, f32[1,512]{1,0:T(1,128)S(1)}, u32[]{:S(2)}, u32[]{:S(2)}) collective-permute-start(f32[1,512]{1,0:T(1,128)} %get-tuple-element.54), channel_id=1, source_target_pairs={{64,0},{96,32},{0,64},{32,96},{65,1},{97,33},{1,65},{33,97},{66,2}... | collective-permute-start | bytes 6152 | tf_op jit(solution)/shard_map/ppermute | solution.py:451
  191.4 25.3 %collective-permute-start.25 = (f32[256,768]{1,0:T(8,128)}, f32[256,768]{1,0:T(8,128)S(1)}, u32[]{:S(2)}, u32[]{:S(2)}) collective-permute-start(f32[256,768]{1,0:T(8,128)} %get-tuple-element.55), channel_id=1, source_target_pairs={{0,16},{16,0},{1,17},{17,1},{2,18},{18,2},{3,19},{19,3},{4,20},{20... | collective-permute-start | bytes 2359304 | tf_op jit(solution)/shard_map/ppermute | solution.py:553
  200.2 4.2 %collective-permute-start.27 = (f32[1,512]{1,0:T(1,128)S(1)}, f32[1,512]{1,0:T(1,128)S(1)}, u32[]{:S(2)}, u32[]{:S(2)}) collective-permute-start(f32[1,512]{1,0:T(1,128)S(1)} %log_add_fusion.2), channel_id=1, source_target_pairs={{8,0},{12,4},{0,8},{4,12},{9,1},{13,5},{1,9},{5,13},{10,2},{14,6},... | collective-permute-start | bytes 6152 | tf_op jit(solution)/shard_map/ppermute | solution.py:451
  205.9 4.8 %collective-permute-start.30 = (f32[1,512]{1,0:T(1,128)S(1)}, f32[1,512]{1,0:T(1,128)S(1)}, u32[]{:S(2)}, u32[]{:S(2)}) collective-permute-start(f32[1,512]{1,0:T(1,128)S(1)} %log_add_fusion.1), channel_id=1, source_target_pairs={{2,0},{3,1},{0,2},{1,3},{6,4},{7,5},{4,6},{5,7},{10,8},{11,9},{8,1... | collective-permute-start | bytes 6152 | tf_op jit(solution)/shard_map/ppermute | solution.py:451
  (31 other events, 190.7 us)
Sparse Core Ops, SparseCore 0:
  9.0 51.7 all-gather.3
  68.0 74.5 all-gather.5

commit v4 on v3

--- a/solution.py
+++ b/solution.py
@@ -123,10 +123,10 @@
     pltpu.make_async_copy(table_ref.at[pl.ds(0, REQ)], rows_s, sem).wait()
 
 
-def own_lanes(rows, lanes, pitch):
+def own_lanes(rows, lanes, pitch, first=0):
     row = lax.broadcasted_iota(jnp.int32, (rows, lanes), 0)
     lane = lax.broadcasted_iota(jnp.int32, (rows, lanes), 1)
-    return row == pitch * (lane // RANK)
+    return row == pitch * (lane // RANK + first)
 
 
 def attended_rows(got_ref):
@@ -143,6 +143,7 @@
 
 
 WIDE = 4
+SENT = REQ + 16
 
 
 def projection_kernel(got_ref, w_ref, expert_ref, amateur_ref, att_s, kinds_s):
@@ -154,7 +155,7 @@
         part = jnp.dot(
             att_s[...], w_ref[:, t * COLS : (t + 1) * COLS], preferred_element_type=F32
         )
-        expert_ref[t] = part[:REQ].astype(BF16)
+        expert_ref[t, 0:REQ, :] = part[:REQ].astype(BF16)
         amateur_ref[t] = part[REQ:].astype(BF16)
 
 
@@ -166,8 +167,8 @@
             pl.BlockSpec((TEN, 16, COLS), lambda j: (0, 0, 0)),
             pl.BlockSpec((COLS, WIDE * COLS), lambda j: (0, j)),
         ],
-        out_specs=[pl.BlockSpec((WIDE, REQ, COLS), lambda j: (j, 0, 0))] * 2,
-        out_shape=[jax.ShapeDtypeStruct((TEN, REQ, COLS), BF16)] * 2,
+        out_specs=[pl.BlockSpec((WIDE, rows, COLS), lambda j: (j, 0, 0)) for rows in (SENT, REQ)],
+        out_shape=[jax.ShapeDtypeStruct((TEN, rows, COLS), BF16) for rows in (SENT, REQ)],
         scratch_shapes=[
             pltpu.VMEM((128, COLS), BF16),
             pltpu.VMEM((COLS // HD, 128, HD), F32),
@@ -177,37 +178,60 @@
     )(got, weight)
 
 
-def rank_kernel(idx_ref, got_ref, table_ref, o_ref, rows_s, sem):
+def rank_kernel(idx_ref, got_ref, table_ref, partial_ref, o_ref, rows_s, block_s, sem, out_sem):
     start_rows(idx_ref, [table_ref], rows_s, sem)
     attended = attended_rows(got_ref).astype(BF16)
     wait_rows(table_ref, rows_s, sem)
     rows = rows_s[...].reshape(REQ * RANK, COLS)
     product = lax.dot_general(attended, rows, LAST, preferred_element_type=F32)
     mask = own_lanes(128, REQ * RANK, 2)
-    o_ref[...] = jnp.sum(jnp.where(mask, product, 0.0), axis=0, keepdims=True)
-
-
-def rank_sums(index, got, table):
-    near = pl.BlockSpec(memory_space=pltpu.VMEM)
+    rank = jnp.sum(jnp.where(mask, product, 0.0), axis=0, keepdims=True)
+    place = lax.broadcasted_iota(jnp.int32, (16, COLS), 0)
+    block = jnp.zeros((16, COLS), F32)
+    for n in range(2):
+        half = rank[:, n * COLS : (n + 1) * COLS]
+        high = half.astype(BF16).astype(F32)
+        block = jnp.where(place == n, high, block)
+        block = jnp.where(place == n + 2, half - high, block)
+    block_s[...] = block.astype(BF16)
+    copies = [
+        pltpu.make_async_copy(block_s, o_ref.at[t, pl.ds(REQ, 16), :], out_sem.at[t])
+        for t in range(TEN)
+    ]
+    for copy in copies:
+        copy.start()
+    for copy in copies:
+        copy.wait()
+
+
+def with_rank_sums(index, got, table, partial):
+    far = pl.BlockSpec(memory_space=pl.ANY)
     return pl.pallas_call(
         rank_kernel,
         in_specs=[
             pl.BlockSpec(memory_space=pltpu.SMEM),
-            near,
-            pl.BlockSpec(memory_space=pl.ANY),
+            pl.BlockSpec(memory_space=pltpu.VMEM),
+            far,
+            far,
         ],
-        out_specs=near,
-        out_shape=jax.ShapeDtypeStruct((1, REQ * RANK), F32),
-        scratch_shapes=[pltpu.VMEM((REQ, RANK, COLS), BF16), pltpu.SemaphoreType.DMA],
+        out_specs=far,
+        out_shape=jax.ShapeDtypeStruct(partial.shape, BF16),
+        input_output_aliases={3: 0},
+        scratch_shapes=[
+            pltpu.VMEM((REQ, RANK, COLS), BF16),
+            pltpu.VMEM((16, COLS), BF16),
+            pltpu.SemaphoreType.DMA,
+            pltpu.SemaphoreType.DMA((TEN,)),
+        ],
         compiler_params=params(56),
         cost_estimate=pl.CostEstimate(flops=14 * 10**7, bytes_accessed=2 * MIB, transcendentals=0),
-    )(index, got, table)
-
-
-def add_all(sums_ref):
-    total = sums_ref[0].astype(F32)
+    )(index, got, table, partial)
+
+
+def add_all(sums_ref, first, last):
+    total = sums_ref[0, first:last, :].astype(F32)
     for t in range(1, TEN):
-        total = total + sums_ref[t].astype(F32)
+        total = total + sums_ref[t, first:last, :].astype(F32)
     return total
 
 
@@ -217,7 +241,7 @@
 
 def amateur_kernel(sums_ref, got_ref, gain_ref, o_ref, kinds_s):
     base = split_kinds(residual_rows(got_ref), kinds_s)[1]
-    hidden = (base + add_all(sums_ref)).astype(BF16).astype(F32)
+    hidden = (base + add_all(sums_ref, 0, REQ)).astype(BF16).astype(F32)
     o_ref[...] = (hidden * gain_ref[...].astype(F32)).astype(BF16)
 
 
@@ -235,29 +259,32 @@
 
 
 def expert_kernel(
-    slot_ref, sums_ref, got_ref, k0_ref, k1_ref, k2_ref, k3_ref, gain_ref, own_ref, sib_ref,
-    o_ref, rows_s, kinds_s, sem,
+    slot_ref, sums_ref, got_ref, gain_ref, own_ref, sib_ref, o_ref, rows_s, kinds_s, sem
 ):
     start_rows(slot_ref, [own_ref, sib_ref], rows_s, sem)
-    base = split_kinds(residual_rows(got_ref), kinds_s)[0] + add_all(sums_ref)
-    rank = (k0_ref[...] + k1_ref[...]) + (k2_ref[...] + k3_ref[...])
-    spread = jnp.where(own_lanes(REQ, REQ * RANK, 1), rank, 0.0)
-    high = spread.astype(BF16)
-    low = (spread - high.astype(F32)).astype(BF16)
+    base = split_kinds(residual_rows(got_ref), kinds_s)[0] + add_all(sums_ref, 0, REQ)
+    rank = add_all(sums_ref, REQ, SENT)
     wait_rows(own_ref, rows_s, sem)
     rows = rows_s[...].reshape(REQ * RANK, COLS)
-    delta = jnp.dot(high, rows, preferred_element_type=F32)
-    delta = delta + jnp.dot(low, rows, preferred_element_type=F32)
+    delta = jnp.zeros((REQ, COLS), F32)
+    for n in range(2):
+        vector = rank[n : n + 1, :] + rank[n + 2 : n + 3, :]
+        spread = jnp.where(own_lanes(REQ, COLS, 1, n * (COLS // RANK)), vector, 0.0)
+        high = spread.astype(BF16)
+        low = (spread - high.astype(F32)).astype(BF16)
+        part = rows[n * COLS : (n + 1) * COLS, :]
+        delta = delta + jnp.dot(high, part, preferred_element_type=F32)
+        delta = delta + jnp.dot(low, part, preferred_element_type=F32)
     hidden = (base + LOWRANK_SCALE * delta).astype(BF16).astype(F32)
     o_ref[...] = (hidden * gain_ref[...].astype(F32)).astype(BF16)
 
 
-def expert_rows(slots, sums, got, rank, gain, own, sib):
+def expert_rows(slots, sums, got, gain, own, sib):
     near = pl.BlockSpec(memory_space=pltpu.VMEM)
     return pl.pallas_call(
         expert_kernel,
         in_specs=[pl.BlockSpec(memory_space=pltpu.SMEM)]
-        + [near] * 7
+        + [near] * 3
         + [pl.BlockSpec(memory_space=pl.ANY)] * 2,
         out_specs=near,
         out_shape=jax.ShapeDtypeStruct((REQ, COLS), BF16),
@@ -268,7 +295,7 @@
         ],
         compiler_params=params(56),
         cost_estimate=pl.CostEstimate(flops=3 * 10**8, bytes_accessed=2 * MIB, transcendentals=0),
-    )(slots, sums, got, *rank, gain, own, sib)
+    )(slots, sums, got, gain, own, sib)
 
 
 def tensor_index(at, first, second):
@@ -512,21 +539,18 @@
     got = lax.all_to_all(sent, TENSOR, split_axis=0, concat_axis=0, tiled=True)
     expert, amateur = projection(got, output_projection_weight)
     amateur = lax.all_to_all(amateur, TENSOR, split_axis=0, concat_axis=0, tiled=True)
-    sums = lax.all_to_all(expert, TENSOR, split_axis=0, concat_axis=0, tiled=True)
     amateur = amateur_rows(amateur, got, gain)
-    up_after, up_before, amateur = lax.optimization_barrier((up_after, up_before, amateur))
+    amateur, got = lax.optimization_barrier((amateur, got))
     gathered = lax.all_gather(amateur, ("y", "x", "z"), axis=0, tiled=False)
     gathered = gathered.reshape(NY, TEN, REQ, COLS)
+    expert = with_rank_sums(request_adapter_index, got, down, expert)
+    sums = lax.all_to_all(expert, TENSOR, split_axis=0, concat_axis=0, tiled=True)
+    up_after, up_before, _ = lax.optimization_barrier((up_after, up_before, expert))
     half = HELD // 2
     up_far = (from_offset(up_after[:half], "y", 1), from_offset(up_before[half:], "y", 3))
     up_own = jnp.concatenate([lowrank_up_factors, up_after, *up_far, up_before], axis=0)
-    up_own, sums = lax.optimization_barrier((up_own, sums))
     up_sib = lax.ppermute(up_own, "c", SWAP)
-    rank = rank_sums(request_adapter_index, got, down)
-    rank, sums = lax.optimization_barrier((rank, sums))
-    rank = sum([from_offset(rank, "x", d) for d in range(1, 4)], rank)
-    rank = [rank] + [from_offset(rank, "z", d) for d in range(1, 4)]
-    expert = expert_rows(slots, sums, got, rank, gain, up_own, up_sib)
+    expert = expert_rows(slots, sums, got, gain, up_own, up_sib)
 
     plane = jnp.stack([expert] + [from_offset(expert, "y", d) for d in range(1, 4)])
     after = from_core_offset(plane, FIRST, 1)

time: 227 us -> 226 us (level)
  starting transfers between devices: 59.9 us -> 49.9 us
  waiting for transfers between devices: 65.1 us -> 72.3 us
    all_to_all x1, waiting for transfers between devices: 3.94 us -> 20 us  [per_device(): lax.all_to_all(expert, TENSOR, split_axis=0, concat_axis=0, tiled=True)]
    ppermute x7, waiting for transfers between devices: 15.7 us -> 7.04 us  [from_core_offset(): return lax.ppermute(array, ('c', 'x', 'z'), pairs)]
    ppermute x22 -> x16, starting transfers between devices: 25 us -> 17.9 us  [from_offset(): return lax.ppermute(array, axis, [((i + offset) % 4, i) for i in range(4)])]
    ppermute x22 -> x16, waiting for transfers between devices: 31.9 us -> 28.6 us  [from_offset(): return lax.ppermute(array, axis, [((i + offset) % 4, i) for i in range(4)])]
    all_to_all x1, waiting for transfers between devices: 12.1 us -> 15.1 us  [per_device(): lax.all_to_all(amateur, TENSOR, split_axis=0, concat_axis=0, tiled=True)]
    ppermute x1, starting transfers between devices: 8.79 us -> 5.93 us  [per_device(): u_sib = lax.ppermute(u_send, 'c', SWAP)]
    ppermute x1, starting transfers between devices: 3.22 us -> 5.65 us  [per_device(): up_sib = lax.ppermute(up_own, 'c', SWAP)]
    unnamed x40 -> x28, local copies, waits for them, and re-layouts: 5.78 us -> 6.6 us
  transfers between devices with their start and end apart: 37 -> 31, of which waited for: 24 -> 21; matrix products, arithmetic and copies ran while one was open for 3% -> 3% of each run, Pallas kernels for 23% -> 23%
where the time goes in v4:
time: 226 us; the launch traced here: 225 us
  waiting for transfers between devices  72.3 us (32%)
  Pallas kernels  61.6 us (27%)
  starting transfers between devices  49.9 us (22%)
  blocking collectives  15.6 us (7%)
  between operations  13.7 us (6%)
  local copies, waits for them, and re-layouts  7.78 us (3%)
  other arithmetic  3.63 us (2%)
    pallas_call x4, Pallas kernels, head_part(): pl.pallas_call(lambda *refs: head_kernel(pieces, first, last, amateur, *r...  40.9 us
    ppermute x16, waiting for transfers between devices, from_offset(): return lax.ppermute(array, axis, [((i + offset) % 4, i) for i in range(4)])  28.6 us
    all_to_all x1, waiting for transfers between devices, per_device(): lax.all_to_all(expert, TENSOR, split_axis=0, concat_axis=0, tiled=True)  20 us
    ppermute x16, starting transfers between devices, from_offset(): return lax.ppermute(array, axis, [((i + offset) % 4, i) for i in range(4)])  17.9 us
    all_to_all x1, blocking collectives, per_device(): got = lax.all_to_all(sent, TENSOR, split_axis=0, concat_axis=0, tiled=True)  15.6 us
    all_to_all x1, waiting for transfers between devices, per_device(): lax.all_to_all(amateur, TENSOR, split_axis=0, concat_axis=0, tiled=True)  15.1 us
    ppermute x7, starting transfers between devices, from_core_offset(): return lax.ppermute(array, ('c', 'x', 'z'), pairs)  7.15 us
    ppermute x7, waiting for transfers between devices, from_core_offset(): return lax.ppermute(array, ('c', 'x', 'z'), pairs)  7.04 us
  transfers between devices with their start and end apart: 31, of which 21 were waited for; matrix products, arithmetic and copies ran while one was open for 3% of the time, Pallas kernels for 23%

profile of v4, /device:TPU:1, one launch (start us, length us, event | category | flops | bytes accessed | tf_op | source)
XLA Modules:
  0.0 224.5 jit_solution(3857383527835795212)
XLA Ops:
  8.8 5.0 %shard_map.127 = bf16[16,16,512]{2,1,0:T(8,128)(2,1)} custom-call(s32[4]{0:T(128)} %len_ref.1, bf16[4,2,8192]{2,1,0:T(2,128)(2,1)} %q_ref.1, bf16[4,2,64,1024]{3,2,1,0:T(8,128)(2,1)} %k_ref.1, bf16[4,2,64,1024]{3,2,1,0:T(8,128)(2,1)} %v_ref.1, bf16[4,2,1024]{2,1,0:T(2,128)(2,1)} %ck_ref.1, bf16[4,2,1024]{2,1,0:T(2,128)(2,1)} %cv_ref.1, ...), custom_call_target="tpu_custom_call" | custom-call | flops 300000000 | bytes 3145728 | tf_op jit(solution)/shard_map/pallas_call | solution.py:81
  13.7 15.6 %all_to_all.15.got_ref = bf16[16,16,512]{2,1,0:T(8,128)(2,1)} all-to-all(bf16[16,16,512]{2,1,0:T(8,128)(2,1)} %shard_map.127), channel_id=1, replica_groups=mesh['y'=4,'c'=2,'x'=4,'z'=4] {'x','z'}, dimensions={0} | all-to-all | bytes 524288 | tf_op jit(solution)/shard_map/all_to_all | solution.py:539
  29.3 6.2 %shard_map.128 = (bf16[16,80,512]{2,1,0:T(8,128)(2,1)}, bf16[16,64,512]{2,1,0:T(8,128)(2,1)}) custom-call(bf16[16,16,512]{2,1,0:T(8,128)(2,1)} %all_to_all.15.got_ref, bf16[512,8192]{1,0:T(8,128)(2,1)} %w_ref.1), custom_call_target="tpu_custom_call" | custom-call | flops 1100000000 | bytes 11534336 | tf_op jit(solution)/shard_map/pallas_call | solution.py:163
  35.6 3.9 %all-to-all-start.1 = ((bf16[16,64,512]{2,1,0:T(8,128)(2,1)}), bf16[16,64,512]{2,1,0:T(8,128)(2,1)S(1)}, u32[]{:S(2)}, u32[]{:S(2)}) async-start(bf16[16,64,512]{2,1,0:T(8,128)(2,1)} %get-tuple-element.28), calls=%async_computation.1 | async-start | bytes 2097152 | tf_op jit(solution)/shard_map/all_to_all | solution.py:541
  39.6 15.1 %all-to-all-done.1.sums_ref = bf16[16,64,512]{2,1,0:T(8,128)(2,1)S(1)} async-done(((bf16[16,64,512]{2,1,0:T(8,128)(2,1)}), bf16[16,64,512]{2,1,0:T(8,128)(2,1)S(1)}, u32[]{:S(2)}, u32[]{:S(2)}) %all-to-all-start.1) | async-done | bytes 1048608 | tf_op jit(solution)/shard_map/all_to_all | solution.py:541
  55.6 3.0 %collective-permute-start = (bf16[48,16,512]{2,1,0:T(8,128)(2,1)S(1)}, bf16[48,16,512]{2,1,0:T(8,128)(2,1)S(1)}, u32[]{:S(2)}, u32[]{:S(2)}) collective-permute-start(bf16[48,16,512]{2,1,0:T(8,128)(2,1)S(1)} %copy-done.7), channel_id=1, source_target_pairs={{32,0},{64,32},{96,64},{0,96},{33,1},{65,33},{97,65},{1,97},{34,2}... | collective-permute-start | bytes 2359304 | tf_op jit(solution)/shard_map/ppermute | solution.py:478
  58.6 3.5 %shard_map.130 = bf16[16,80,512]{2,1,0:T(8,128)(2,1)} custom-call(s32[64]{0:T(128)} %idx_ref.1, bf16[16,16,512]{2,1,0:T(8,128)(2,1)} %all_to_all.15.got_ref, bf16[384,16,512]{2,1,0:T(8,128)(2,1)} %all-gather.4.cloned.1.call-done.table_ref, bf16[16,80,512]{2,1,0:T(8,128)(2,1)} %get-tuple-element.30.partial_ref), custom_call_target="tpu_custom_call", output_to_operand_aliasing={{}: (3, {})} | custom-call | flops 140000000 | bytes 2097152 | tf_op jit(solution)/shard_map/pallas_call | solution.py:209
  62.1 10.6 %collective-permute-done = bf16[48,16,512]{2,1,0:T(8,128)(2,1)S(1)} collective-permute-done((bf16[48,16,512]{2,1,0:T(8,128)(2,1)S(1)}, bf16[48,16,512]{2,1,0:T(8,128)(2,1)S(1)}, u32[]{:S(2)}, u32[]{:S(2)}) %collective-permute-start) | collective-permute-done | bytes 786464 | tf_op jit(solution)/shard_map/ppermute | solution.py:478
  72.6 3.1 %collective-permute-done.1 = bf16[48,16,512]{2,1,0:T(8,128)(2,1)S(1)} collective-permute-done((bf16[48,16,512]{2,1,0:T(8,128)(2,1)S(1)}, bf16[48,16,512]{2,1,0:T(8,128)(2,1)S(1)}, u32[]{:S(2)}, u32[]{:S(2)}) %collective-permute-start.1) | collective-permute-done | bytes 786464 | tf_op jit(solution)/shard_map/ppermute | solution.py:478
  79.3 3.3 %collective-permute-done.2 = bf16[24,16,512]{2,1,0:T(8,128)(2,1)S(1)} collective-permute-done((bf16[24,16,512]{2,1,0:T(8,128)(2,1)S(1)}, bf16[24,16,512]{2,1,0:T(8,128)(2,1)S(1)}, u32[]{:S(2)}, u32[]{:S(2)}) %collective-permute-start.2) | collective-permute-done | bytes 393248 | tf_op jit(solution)/shard_map/ppermute | solution.py:478
  85.8 5.7 %collective-permute-start.4 = (bf16[192,16,512]{2,1,0:T(8,128)(2,1)}, bf16[192,16,512]{2,1,0:T(8,128)(2,1)}, u32[]{:S(2)}, u32[]{:S(2)}) collective-permute-start(bf16[192,16,512]{2,1,0:T(8,128)(2,1)} %constant_dynamic-update-slice_fusion.own_ref), channel_id=1, source_target_pairs={{0,16},{16,0},{1,17},{17,1},{2,18},{18,2},{3,19},{19,3},{4,20},{20... | collective-permute-start | bytes 9437192 | tf_op jit(solution)/shard_map/ppermute | solution.py:552
  91.5 4.9 %all-to-all-start.2 = ((bf16[16,80,512]{2,1,0:T(8,128)(2,1)}), bf16[16,80,512]{2,1,0:T(8,128)(2,1)S(1)}, u32[]{:S(2)}, u32[]{:S(2)}) async-start(bf16[16,80,512]{2,1,0:T(8,128)(2,1)} %shard_map.130), calls=%async_computation.2 | async-start | bytes 2621440 | tf_op jit(solution)/shard_map/all_to_all | solution.py:547
  96.9 20.0 %all-to-all-done.2.sums_ref = bf16[16,80,512]{2,1,0:T(8,128)(2,1)S(1)} async-done(((bf16[16,80,512]{2,1,0:T(8,128)(2,1)}), bf16[16,80,512]{2,1,0:T(8,128)(2,1)S(1)}, u32[]{:S(2)}, u32[]{:S(2)}) %all-to-all-start.2) | async-done | bytes 1310752 | tf_op jit(solution)/shard_map/all_to_all | solution.py:547
  118.0 3.8 %shard_map.131 = bf16[64,512]{1,0:T(8,128)(2,1)} custom-call(s32[64]{0:T(128)} %fusion.1.slot_ref, bf16[16,80,512]{2,1,0:T(8,128)(2,1)} %copy-done.3, bf16[16,16,512]{2,1,0:T(8,128)(2,1)} %all_to_all.15.got_ref, bf16[1,512]{1,0:T(2,128)(2,1)} %copy-done.2, bf16[192,16,512]{2,1,0:T(8,128)(2,1)} %constant_dynamic-update-slice_fusion.own_ref, ...), custom_call_target="tpu_custom_call" | custom-call | flops 300000000 | bytes 2097152 | tf_op jit(solution)/shard_map/pallas_call | solution.py:284
  125.2 2.6 %collective-permute-done.7 = bf16[64,512]{1,0:T(8,128)(2,1)S(1)} collective-permute-done((bf16[64,512]{1,0:T(8,128)(2,1)}, bf16[64,512]{1,0:T(8,128)(2,1)S(1)}, u32[]{:S(2)}, u32[]{:S(2)}) %collective-permute-start.7) | collective-permute-done | bytes 65568 | tf_op jit(solution)/shard_map/ppermute | solution.py:478
  127.8 3.1 %collective-permute-done.6 = bf16[64,512]{1,0:T(8,128)(2,1)S(1)} collective-permute-done((bf16[64,512]{1,0:T(8,128)(2,1)}, bf16[64,512]{1,0:T(8,128)(2,1)S(1)}, u32[]{:S(2)}, u32[]{:S(2)}) %collective-permute-start.6) | collective-permute-done | bytes 65568 | tf_op jit(solution)/shard_map/ppermute | solution.py:478
  132.1 2.8 %collective-permute-start.8 = (bf16[4,64,512]{2,1,0:T(8,128)(2,1)S(1)}, bf16[4,64,512]{2,1,0:T(8,128)(2,1)S(1)}, u32[]{:S(2)}, u32[]{:S(2)}) collective-permute-start(bf16[4,64,512]{2,1,0:T(8,128)(2,1)S(1)} %get-tuple-element.52), channel_id=1, source_target_pairs={{4,0},{5,1},{6,2},{7,3},{8,4},{9,5},{10,6},{11,7},{12,8},{13,9},{1... | collective-permute-start | bytes 786440 | tf_op jit(solution)/shard_map/ppermute | solution.py:489
  134.9 4.0 %collective-permute-done.9 = bf16[4,64,512]{2,1,0:T(8,128)(2,1)S(1)} collective-permute-done((bf16[4,64,512]{2,1,0:T(8,128)(2,1)S(1)}, bf16[4,64,512]{2,1,0:T(8,128)(2,1)S(1)}, u32[]{:S(2)}, u32[]{:S(2)}) %collective-permute-start.9) | collective-permute-done | bytes 262176 | tf_op jit(solution)/shard_map/ppermute | solution.py:489
  146.1 14.4 %shard_map.133 = (f32[256,1536]{1,0:T(8,128)}, f32[1,256]{1,0:T(1,128)}) custom-call(s32[4]{0:T(128)} %pad_add_fusion.refs_0_, f32[1,8192]{1,0:T(1,128)} %bitcast.16, bf16[4,16,64,512]{3,2,1,0:T(8,128)(2,1)} %bitcast.15, bf16[8192,768]{1,0:T(8,128)(2,1)} %refs_4_.3, bf16[8192,768]{1,0:T(8,128)(2,1)} %collective-permute-done.13.refs_4_.refs_5_), custom_call_target="tpu_custom_call" | custom-call | flops 2097152 | bytes 524288 | tf_op jit(solution)/shard_map/pallas_call | solution.py:411
  160.5 6.2 %shard_map.132 = (f32[256,1536]{1,0:T(8,128)}, f32[256,128]{1,0:T(8,128)}) custom-call(s32[4]{0:T(128)} %pad_add_fusion.refs_0_, f32[1,8192]{1,0:T(1,128)} %bitcast.17, bf16[4,4,64,512]{3,2,1,0:T(8,128)(2,1)} %copy-done.4, bf16[8192,768]{1,0:T(8,128)(2,1)} %refs_4_.3, bf16[8192,768]{1,0:T(8,128)(2,1)} %collective-permute-done.13.refs_4_.refs_5_), custom_call_target="tpu_custom_call" | custom-call | flops 524288 | bytes 131072 | tf_op jit(solution)/shard_map/pallas_call | solution.py:411
  168.4 11.9 %shard_map.134 = (f32[256,1536]{1,0:T(8,128)}, f32[256,128]{1,0:T(8,128)}) custom-call(s32[4]{0:T(128)} %pad_add_fusion.refs_0_, f32[1,8192]{1,0:T(1,128)} %bitcast.18, bf16[4,4,64,512]{3,2,1,0:T(8,128)(2,1)} %copy-done.6, bf16[4,4,64,512]{3,2,1,0:T(8,128)(2,1)} %copy-done.5, bf16[8192,768]{1,0:T(8,128)(2,1)} %refs_4_.3, ...), custom_call_target="tpu_custom_call" | custom-call | flops 1048576 | bytes 262144 | tf_op jit(solution)/shard_map/pallas_call | solution.py:411
  181.2 8.5 %shard_map.135 = (f32[256,768]{1,0:T(8,128)}, f32[256,768]{1,0:T(8,128)}, f32[1,512]{1,0:T(1,128)}) custom-call(s32[4]{0:T(128)} %pad_add_fusion.refs_0_, f32[1,8192]{1,0:T(1,128)} %bitcast.19, bf16[2,4,64,512]{3,2,1,0:T(8,128)(2,1)} %copy-done.8, bf16[2,4,64,512]{3,2,1,0:T(8,128)(2,1)} %copy-done.9, bf16[8192,768]{1,0:T(8,128)(2,1)} %refs_4_.3, ...), custom_call_target="tpu_custom_call" | custom-call | flops 524288 | bytes 131072 | tf_op jit(solution)/shard_map/pallas_call | solution.py:411
  195.3 5.9 %collective-permute-start.19 = (f32[256,768]{1,0:T(8,128)}, f32[256,768]{1,0:T(8,128)S(1)}, u32[]{:S(2)}, u32[]{:S(2)}) collective-permute-start(f32[256,768]{1,0:T(8,128)} %get-tuple-element.49), channel_id=1, source_target_pairs={{0,16},{16,0},{1,17},{17,1},{2,18},{18,2},{3,19},{19,3},{4,20},{20... | collective-permute-start | bytes 2359304 | tf_op jit(solution)/shard_map/ppermute | solution.py:577
  211.3 3.0 %collective-permute-start.26 = (f32[1,512]{1,0:T(1,128)S(1)}, f32[1,512]{1,0:T(1,128)S(1)}, u32[]{:S(2)}, u32[]{:S(2)}) collective-permute-start(f32[1,512]{1,0:T(1,128)S(1)} %log_add_fusion.no_ref), channel_id=1, source_target_pairs={{0,16},{16,0},{1,17},{17,1},{2,18},{18,2},{3,19},{19,3},{4,20},{20... | collective-permute-start | bytes 6152 | tf_op jit(solution)/shard_map/ppermute | solution.py:578
  (94 shorter events, 45.1 us)
Async XLA Ops:
  6.5 52.0 %all-gather.4.cloned.1.call-start = ((), (), s32[]{:S(2)}) async-start(), calls=%async_computation.3 | async-start | bytes 7077888 | tf_op jit(solution)/shard_map/all_gather | solution.py:519
  7.3 138.8 %collective-permute-start.13 = (bf16[8192,768]{1,0:T(8,128)(2,1)}, bf16[8192,768]{1,0:T(8,128)(2,1)}, u32[]{:S(2)}, u32[]{:S(2)}) collective-permute-start(bf16[8192,768]{1,0:T(8,128)(2,1)} %refs_4_.3), channel_id=1, source_target_pairs={{0,16},{16,0},{1,17},{17,1},{2,18},{18,2},{3,19},{19,3},{4,20},{20... | collective-permute-start | bytes 37748744 | tf_op jit(solution)/shard_map/ppermute | solution.py:518
  35.6 19.2 %all-to-all-start.1 = ((bf16[16,64,512]{2,1,0:T(8,128)(2,1)}), bf16[16,64,512]{2,1,0:T(8,128)(2,1)S(1)}, u32[]{:S(2)}, u32[]{:S(2)}) async-start(bf16[16,64,512]{2,1,0:T(8,128)(2,1)} %get-tuple-element.28), calls=%async_computation.1 | async-start | bytes 2097152 | tf_op jit(solution)/shard_map/all_to_all | solution.py:541
  39.5 106.6 %all-gather.6.cloned.1.call-start = ((), (), s32[]{:S(2)}) async-start(), calls=%async_computation.4 | async-start | bytes 4259840 | tf_op jit(solution)/shard_map/all_gather | solution.py:544
  55.6 17.1 %collective-permute-start = (bf16[48,16,512]{2,1,0:T(8,128)(2,1)S(1)}, bf16[48,16,512]{2,1,0:T(8,128)(2,1)S(1)}, u32[]{:S(2)}, u32[]{:S(2)}) collective-permute-start(bf16[48,16,512]{2,1,0:T(8,128)(2,1)S(1)} %copy-done.7), channel_id=1, source_target_pairs={{32,0},{64,32},{96,64},{0,96},{33,1},{65,33},{97,65},{1,97},{34,2}... | collective-permute-start | bytes 2359304 | tf_op jit(solution)/shard_map/ppermute | solution.py:478
  58.6 17.1 %collective-permute-start.1 = (bf16[48,16,512]{2,1,0:T(8,128)(2,1)S(1)}, bf16[48,16,512]{2,1,0:T(8,128)(2,1)S(1)}, u32[]{:S(2)}, u32[]{:S(2)}) collective-permute-start(bf16[48,16,512]{2,1,0:T(8,128)(2,1)S(1)} %copy-done.7), channel_id=1, source_target_pairs={{96,0},{0,32},{32,64},{64,96},{97,1},{1,33},{33,65},{65,97},{98,2}... | collective-permute-start | bytes 2359304 | tf_op jit(solution)/shard_map/ppermute | solution.py:478
  75.7 6.8 %collective-permute-start.2 = (bf16[24,16,512]{2,1,0:T(8,128)(2,1)S(1)}, bf16[24,16,512]{2,1,0:T(8,128)(2,1)S(1)}, u32[]{:S(2)}, u32[]{:S(2)}) collective-permute-start(bf16[24,16,512]{2,1,0:T(8,128)(2,1)S(1)} %slice.12), channel_id=1, source_target_pairs={{32,0},{64,32},{96,64},{0,96},{33,1},{65,33},{97,65},{1,97},{34,2}... | collective-permute-start | bytes 1179656 | tf_op jit(solution)/shard_map/ppermute | solution.py:478
  76.1 8.0 %collective-permute-start.3 = (bf16[24,16,512]{2,1,0:T(8,128)(2,1)S(1)}, bf16[24,16,512]{2,1,0:T(8,128)(2,1)S(1)}, u32[]{:S(2)}, u32[]{:S(2)}) collective-permute-start(bf16[24,16,512]{2,1,0:T(8,128)(2,1)S(1)} %slice.13), channel_id=1, source_target_pairs={{96,0},{0,32},{32,64},{64,96},{97,1},{1,33},{33,65},{65,97},{98,2}... | collective-permute-start | bytes 1179656 | tf_op jit(solution)/shard_map/ppermute | solution.py:478
  85.8 31.1 %collective-permute-start.4 = (bf16[192,16,512]{2,1,0:T(8,128)(2,1)}, bf16[192,16,512]{2,1,0:T(8,128)(2,1)}, u32[]{:S(2)}, u32[]{:S(2)}) collective-permute-start(bf16[192,16,512]{2,1,0:T(8,128)(2,1)} %constant_dynamic-update-slice_fusion.own_ref), channel_id=1, source_target_pairs={{0,16},{16,0},{1,17},{17,1},{2,18},{18,2},{3,19},{19,3},{4,20},{20... | collective-permute-start | bytes 9437192 | tf_op jit(solution)/shard_map/ppermute | solution.py:552
  91.5 25.4 %all-to-all-start.2 = ((bf16[16,80,512]{2,1,0:T(8,128)(2,1)}), bf16[16,80,512]{2,1,0:T(8,128)(2,1)S(1)}, u32[]{:S(2)}, u32[]{:S(2)}) async-start(bf16[16,80,512]{2,1,0:T(8,128)(2,1)} %shard_map.130), calls=%async_computation.2 | async-start | bytes 2621440 | tf_op jit(solution)/shard_map/all_to_all | solution.py:547
  121.8 6.0 %collective-permute-start.7 = (bf16[64,512]{1,0:T(8,128)(2,1)}, bf16[64,512]{1,0:T(8,128)(2,1)S(1)}, u32[]{:S(2)}, u32[]{:S(2)}) collective-permute-start(bf16[64,512]{1,0:T(8,128)(2,1)} %shard_map.131), channel_id=1, source_target_pairs={{96,0},{0,32},{32,64},{64,96},{97,1},{1,33},{33,65},{65,97},{98,2}... | collective-permute-start | bytes 196616 | tf_op jit(solution)/shard_map/ppermute | solution.py:478
  122.0 8.9 %collective-permute-start.6 = (bf16[64,512]{1,0:T(8,128)(2,1)}, bf16[64,512]{1,0:T(8,128)(2,1)S(1)}, u32[]{:S(2)}, u32[]{:S(2)}) collective-permute-start(bf16[64,512]{1,0:T(8,128)(2,1)} %shard_map.131), channel_id=1, source_target_pairs={{64,0},{96,32},{0,64},{32,96},{65,1},{97,33},{1,65},{33,97},{66,2}... | collective-permute-start | bytes 196616 | tf_op jit(solution)/shard_map/ppermute | solution.py:478
  124.4 6.6 %collective-permute-start.5 = (bf16[64,512]{1,0:T(8,128)(2,1)}, bf16[64,512]{1,0:T(8,128)(2,1)S(1)}, u32[]{:S(2)}, u32[]{:S(2)}) collective-permute-start(bf16[64,512]{1,0:T(8,128)(2,1)} %shard_map.131), channel_id=1, source_target_pairs={{32,0},{64,32},{96,64},{0,96},{33,1},{65,33},{97,65},{1,97},{34,2}... | collective-permute-start | bytes 196616 | tf_op jit(solution)/shard_map/ppermute | solution.py:478
  132.0 6.8 %collective-permute-start.9 = (bf16[4,64,512]{2,1,0:T(8,128)(2,1)S(1)}, bf16[4,64,512]{2,1,0:T(8,128)(2,1)S(1)}, u32[]{:S(2)}, u32[]{:S(2)}) collective-permute-start(bf16[4,64,512]{2,1,0:T(8,128)(2,1)S(1)} %get-tuple-element.52), channel_id=1, source_target_pairs={{8,0},{9,1},{10,2},{11,3},{12,4},{13,5},{14,6},{15,7},{0,8},{1,9},... | collective-permute-start | bytes 786440 | tf_op jit(solution)/shard_map/ppermute | solution.py:489
  132.1 9.1 %collective-permute-start.8 = (bf16[4,64,512]{2,1,0:T(8,128)(2,1)S(1)}, bf16[4,64,512]{2,1,0:T(8,128)(2,1)S(1)}, u32[]{:S(2)}, u32[]{:S(2)}) collective-permute-start(bf16[4,64,512]{2,1,0:T(8,128)(2,1)S(1)} %get-tuple-element.52), channel_id=1, source_target_pairs={{4,0},{5,1},{6,2},{7,3},{8,4},{9,5},{10,6},{11,7},{12,8},{13,9},{1... | collective-permute-start | bytes 786440 | tf_op jit(solution)/shard_map/ppermute | solution.py:489
  134.9 7.0 %collective-permute-start.10 = (bf16[4,64,512]{2,1,0:T(8,128)(2,1)S(1)}, bf16[4,64,512]{2,1,0:T(8,128)(2,1)S(1)}, u32[]{:S(2)}, u32[]{:S(2)}) collective-permute-start(bf16[4,64,512]{2,1,0:T(8,128)(2,1)S(1)} %get-tuple-element.52), channel_id=1, source_target_pairs={{12,0},{13,1},{14,2},{15,3},{0,4},{1,5},{2,6},{3,7},{4,8},{5,9},{6... | collective-permute-start | bytes 786440 | tf_op jit(solution)/shard_map/ppermute | solution.py:489
  142.0 24.7 %collective-permute-start.12 = (bf16[4,4,64,512]{3,2,1,0:T(8,128)(2,1)S(1)}, bf16[4,4,64,512]{3,2,1,0:T(8,128)(2,1)S(1)}, u32[]{:S(2)}, u32[]{:S(2)}) collective-permute-start(bf16[4,4,64,512]{3,2,1,0:T(8,128)(2,1)S(1)} %pad_maximum_fusion.refs_2_), channel_id=1, source_target_pairs={{3,0},{0,1},{1,2},{2,3},{7,4},{4,5},{5,6},{6,7},{11,8},{8,9},{9,10... | collective-permute-start | bytes 3145736 | tf_op jit(solution)/shard_map/ppermute | solution.py:489
  142.4 24.3 %collective-permute-start.11 = (bf16[4,4,64,512]{3,2,1,0:T(8,128)(2,1)S(1)}, bf16[4,4,64,512]{3,2,1,0:T(8,128)(2,1)S(1)}, u32[]{:S(2)}, u32[]{:S(2)}) collective-permute-start(bf16[4,4,64,512]{3,2,1,0:T(8,128)(2,1)S(1)} %pad_maximum_fusion.refs_2_), channel_id=1, source_target_pairs={{1,0},{2,1},{3,2},{0,3},{5,4},{6,5},{7,6},{4,7},{9,8},{10,9},{11,1... | collective-permute-start | bytes 3145736 | tf_op jit(solution)/shard_map/ppermute | solution.py:489
  166.8 13.4 %collective-permute-start.14 = (bf16[2,4,64,512]{3,2,1,0:T(8,128)(2,1)S(1)}, bf16[2,4,64,512]{3,2,1,0:T(8,128)(2,1)S(1)}, u32[]{:S(2)}, u32[]{:S(2)}) collective-permute-start(bf16[2,4,64,512]{3,2,1,0:T(8,128)(2,1)S(1)} %slice.14), channel_id=1, source_target_pairs={{1,0},{2,1},{3,2},{0,3},{5,4},{6,5},{7,6},{4,7},{9,8},{10,9},{11,1... | collective-permute-start | bytes 1572872 | tf_op jit(solution)/shard_map/ppermute | solution.py:489
  166.9 13.3 %collective-permute-start.15 = (bf16[2,4,64,512]{3,2,1,0:T(8,128)(2,1)S(1)}, bf16[2,4,64,512]{3,2,1,0:T(8,128)(2,1)S(1)}, u32[]{:S(2)}, u32[]{:S(2)}) collective-permute-start(bf16[2,4,64,512]{3,2,1,0:T(8,128)(2,1)S(1)} %slice.15), channel_id=1, source_target_pairs={{3,0},{0,1},{1,2},{2,3},{7,4},{4,5},{5,6},{6,7},{11,8},{8,9},{9,10... | collective-permute-start | bytes 1572872 | tf_op jit(solution)/shard_map/ppermute | solution.py:489
  189.9 4.2 %collective-permute-start.17 = (f32[1,512]{1,0:T(1,128)}, f32[1,512]{1,0:T(1,128)S(1)}, u32[]{:S(2)}, u32[]{:S(2)}) collective-permute-start(f32[1,512]{1,0:T(1,128)} %get-tuple-element.48), channel_id=1, source_target_pairs={{64,0},{96,32},{0,64},{32,96},{65,1},{97,33},{1,65},{33,97},{66,2}... | collective-permute-start | bytes 6152 | tf_op jit(solution)/shard_map/ppermute | solution.py:478
  195.3 19.9 %collective-permute-start.19 = (f32[256,768]{1,0:T(8,128)}, f32[256,768]{1,0:T(8,128)S(1)}, u32[]{:S(2)}, u32[]{:S(2)}) collective-permute-start(f32[256,768]{1,0:T(8,128)} %get-tuple-element.49), channel_id=1, source_target_pairs={{0,16},{16,0},{1,17},{17,1},{2,18},{18,2},{3,19},{19,3},{4,20},{20... | collective-permute-start | bytes 2359304 | tf_op jit(solution)/shard_map/ppermute | solution.py:577
  201.3 3.9 %collective-permute-start.21 = (f32[1,512]{1,0:T(1,128)S(1)}, f32[1,512]{1,0:T(1,128)S(1)}, u32[]{:S(2)}, u32[]{:S(2)}) collective-permute-start(f32[1,512]{1,0:T(1,128)S(1)} %log_add_fusion.2), channel_id=1, source_target_pairs={{8,0},{12,4},{0,8},{4,12},{9,1},{13,5},{1,9},{5,13},{10,2},{14,6},... | collective-permute-start | bytes 6152 | tf_op jit(solution)/shard_map/ppermute | solution.py:478
  206.0 4.0 %collective-permute-start.24 = (f32[1,512]{1,0:T(1,128)S(1)}, f32[1,512]{1,0:T(1,128)S(1)}, u32[]{:S(2)}, u32[]{:S(2)}) collective-permute-start(f32[1,512]{1,0:T(1,128)S(1)} %log_add_fusion.1), channel_id=1, source_target_pairs={{2,0},{3,1},{0,2},{1,3},{6,4},{7,5},{4,6},{5,7},{10,8},{11,9},{8,1... | collective-permute-start | bytes 6152 | tf_op jit(solution)/shard_map/ppermute | solution.py:478
  (19 other events, 144.4 us)
Sparse Core Ops, SparseCore 0:
  9.0 44.5 all-gather.3
  56.5 78.6 all-gather.5

commit v5 on v4

--- a/solution.py
+++ b/solution.py
@@ -538,18 +538,19 @@
     )
     got = lax.all_to_all(sent, TENSOR, split_axis=0, concat_axis=0, tiled=True)
     expert, amateur = projection(got, output_projection_weight)
+    up_after, up_before, amateur = lax.optimization_barrier((up_after, up_before, amateur))
     amateur = lax.all_to_all(amateur, TENSOR, split_axis=0, concat_axis=0, tiled=True)
+    half = HELD // 2
+    up_far = (from_offset(up_after[:half], "y", 1), from_offset(up_before[half:], "y", 3))
+    up_own = jnp.concatenate([lowrank_up_factors, up_after, *up_far, up_before], axis=0)
+    up_own, amateur = lax.optimization_barrier((up_own, amateur))
+    up_sib = lax.ppermute(up_own, "c", SWAP)
     amateur = amateur_rows(amateur, got, gain)
     amateur, got = lax.optimization_barrier((amateur, got))
     gathered = lax.all_gather(amateur, ("y", "x", "z"), axis=0, tiled=False)
     gathered = gathered.reshape(NY, TEN, REQ, COLS)
     expert = with_rank_sums(request_adapter_index, got, down, expert)
     sums = lax.all_to_all(expert, TENSOR, split_axis=0, concat_axis=0, tiled=True)
-    up_after, up_before, _ = lax.optimization_barrier((up_after, up_before, expert))
-    half = HELD // 2
-    up_far = (from_offset(up_after[:half], "y", 1), from_offset(up_before[half:], "y", 3))
-    up_own = jnp.concatenate([lowrank_up_factors, up_after, *up_far, up_before], axis=0)
-    up_sib = lax.ppermute(up_own, "c", SWAP)
     expert = expert_rows(slots, sums, got, gain, up_own, up_sib)
 
     plane = jnp.stack([expert] + [from_offset(expert, "y", d) for d in range(1, 4)])

time: 226 us -> 227 us (level)
  local copies, waits for them, and re-layouts: 7.78 us -> 11.5 us
  waiting for transfers between devices: 72.3 us -> 69.3 us
    all_gather x1, waiting for transfers between devices: 0.01 us -> 17.2 us  [per_device(): gathered = lax.all_gather(amateur, ('y', 'x', 'z'), axis=0, tiled=False)]
    all_to_all x1, waiting for transfers between devices: 15.1 us -> 0.01 us  [per_device(): lax.all_to_all(amateur, TENSOR, split_axis=0, concat_axis=0, tiled=True)]
    ppermute x16, waiting for transfers between devices: 28.6 us -> 21.5 us  [from_offset(): return lax.ppermute(array, axis, [((i + offset) % 4, i) for i in range(4)])]
    ppermute x1, starting transfers between devices: 5.93 us -> 1.69 us  [per_device(): u_sib = lax.ppermute(u_send, 'c', SWAP)]
    ppermute x1, starting transfers between devices: 5.65 us -> 1.6 us  [per_device(): up_sib = lax.ppermute(up_own, 'c', SWAP)]
    all_to_all x1, starting transfers between devices: 3.91 us -> 7.79 us  [per_device(): lax.all_to_all(amateur, TENSOR, split_axis=0, concat_axis=0, tiled=True)]
    all_to_all x1, starting transfers between devices: 4.86 us -> 7.6 us  [per_device(): lax.all_to_all(expert, TENSOR, split_axis=0, concat_axis=0, tiled=True)]
    unnamed x28 -> x26, local copies, waits for them, and re-layouts: 6.6 us -> 8.79 us
  transfers between devices with their start and end apart: 31 -> 31, of which waited for: 21 -> 18; matrix products, arithmetic and copies ran while one was open for 3% -> 5% of each run, Pallas kernels for 23% -> 23%
where the time goes in v5:
time: 227 us; the launch traced here: 226 us
  waiting for transfers between devices  69.3 us (31%)
  Pallas kernels  61.8 us (27%)
  starting transfers between devices  50.9 us (22%)
  blocking collectives  15.3 us (7%)
  between operations  13.7 us (6%)
  local copies, waits for them, and re-layouts  11.5 us (5%)
  other arithmetic  3.61 us (2%)
    pallas_call x4, Pallas kernels, head_part(): pl.pallas_call(lambda *refs: head_kernel(pieces, first, last, amateur, *r...  41.2 us
    ppermute x16, waiting for transfers between devices, from_offset(): return lax.ppermute(array, axis, [((i + offset) % 4, i) for i in range(4)])  21.5 us
    all_to_all x1, waiting for transfers between devices, per_device(): lax.all_to_all(expert, TENSOR, split_axis=0, concat_axis=0, tiled=True)  20.9 us
    ppermute x16, starting transfers between devices, from_offset(): return lax.ppermute(array, axis, [((i + offset) % 4, i) for i in range(4)])  19.8 us
    all_gather x1, waiting for transfers between devices, per_device(): gathered = lax.all_gather(amateur, ('y', 'x', 'z'), axis=0, tiled=False)  17.2 us
    all_to_all x1, blocking collectives, per_device(): got = lax.all_to_all(sent, TENSOR, split_axis=0, concat_axis=0, tiled=True)  15.3 us
    unnamed x26, local copies, waits for them, and re-layouts  8.79 us
    ppermute x7, waiting for transfers between devices, from_core_offset(): return lax.ppermute(array, ('c', 'x', 'z'), pairs)  8.21 us
  transfers between devices with their start and end apart: 31, of which 18 were waited for; matrix products, arithmetic and copies ran while one was open for 5% of the time, Pallas kernels for 23%

profile of v5, /device:TPU:1, one launch (start us, length us, event | category | flops | bytes accessed | tf_op | source)
XLA Modules:
  0.0 226.1 jit_solution(18141282314579237308)
XLA Ops:
  8.8 2.8 %collective-permute-start = (bf16[48,16,512]{2,1,0:T(8,128)(2,1)}, bf16[48,16,512]{2,1,0:T(8,128)(2,1)S(1)}, u32[]{:S(2)}, u32[]{:S(2)}) collective-permute-start(bf16[48,16,512]{2,1,0:T(8,128)(2,1)} %param.23), channel_id=1, source_target_pairs={{32,0},{64,32},{96,64},{0,96},{33,1},{65,33},{97,65},{1,97},{34,2}... | collective-permute-start | bytes 2359304 | tf_op jit(solution)/shard_map/ppermute | solution.py:478
  11.6 5.0 %shard_map.127 = bf16[16,16,512]{2,1,0:T(8,128)(2,1)} custom-call(s32[4]{0:T(128)} %len_ref.1, bf16[4,2,8192]{2,1,0:T(2,128)(2,1)} %q_ref.1, bf16[4,2,64,1024]{3,2,1,0:T(8,128)(2,1)} %k_ref.1, bf16[4,2,64,1024]{3,2,1,0:T(8,128)(2,1)} %v_ref.1, bf16[4,2,1024]{2,1,0:T(2,128)(2,1)} %ck_ref.1, bf16[4,2,1024]{2,1,0:T(2,128)(2,1)} %cv_ref.1, ...), custom_call_target="tpu_custom_call" | custom-call | flops 300000000 | bytes 3145728 | tf_op jit(solution)/shard_map/pallas_call | solution.py:81
  16.6 15.3 %all_to_all.15.got_ref = bf16[16,16,512]{2,1,0:T(8,128)(2,1)} all-to-all(bf16[16,16,512]{2,1,0:T(8,128)(2,1)} %shard_map.127), channel_id=1, replica_groups=mesh['y'=4,'c'=2,'x'=4,'z'=4] {'x','z'}, dimensions={0} | all-to-all | bytes 524288 | tf_op jit(solution)/shard_map/all_to_all | solution.py:539
  31.9 6.2 %shard_map.128 = (bf16[16,80,512]{2,1,0:T(8,128)(2,1)}, bf16[16,64,512]{2,1,0:T(8,128)(2,1)}) custom-call(bf16[16,16,512]{2,1,0:T(8,128)(2,1)} %all_to_all.15.got_ref, bf16[512,8192]{1,0:T(8,128)(2,1)} %w_ref.1), custom_call_target="tpu_custom_call" | custom-call | flops 1100000000 | bytes 11534336 | tf_op jit(solution)/shard_map/pallas_call | solution.py:163
  38.0 7.8 %all-to-all-start.1 = ((bf16[16,64,512]{2,1,0:T(8,128)(2,1)}), bf16[16,64,512]{2,1,0:T(8,128)(2,1)S(1)}, u32[]{:S(2)}, u32[]{:S(2)}) async-start(bf16[16,64,512]{2,1,0:T(8,128)(2,1)} %get-tuple-element.34), calls=%async_computation.1 | async-start | bytes 2097152 | tf_op jit(solution)/shard_map/all_to_all | solution.py:542
  52.1 9.9 %collective-permute-done.2 = bf16[24,16,512]{2,1,0:T(8,128)(2,1)} collective-permute-done((bf16[24,16,512]{2,1,0:T(8,128)(2,1)}, bf16[24,16,512]{2,1,0:T(8,128)(2,1)}, u32[]{:S(2)}, u32[]{:S(2)}) %collective-permute-start.2) | collective-permute-done | bytes 393248 | tf_op jit(solution)/shard_map/ppermute | solution.py:478
  69.4 3.5 %shard_map.130 = bf16[16,80,512]{2,1,0:T(8,128)(2,1)} custom-call(s32[64]{0:T(128)} %idx_ref.1, bf16[16,16,512]{2,1,0:T(8,128)(2,1)} %all_to_all.15.got_ref, bf16[384,16,512]{2,1,0:T(8,128)(2,1)} %all-gather.4.cloned.1.call-done.table_ref, bf16[16,80,512]{2,1,0:T(8,128)(2,1)} %get-tuple-element.37.partial_ref), custom_call_target="tpu_custom_call", output_to_operand_aliasing={{}: (3, {})} | custom-call | flops 140000000 | bytes 2097152 | tf_op jit(solution)/shard_map/pallas_call | solution.py:209
  72.9 7.6 %all-to-all-start.2 = ((bf16[16,80,512]{2,1,0:T(8,128)(2,1)}), bf16[16,80,512]{2,1,0:T(8,128)(2,1)S(1)}, u32[]{:S(2)}, u32[]{:S(2)}) async-start(bf16[16,80,512]{2,1,0:T(8,128)(2,1)} %shard_map.130), calls=%async_computation.2 | async-start | bytes 2621440 | tf_op jit(solution)/shard_map/all_to_all | solution.py:553
  81.1 20.9 %all-to-all-done.2.sums_ref = bf16[16,80,512]{2,1,0:T(8,128)(2,1)S(1)} async-done(((bf16[16,80,512]{2,1,0:T(8,128)(2,1)}), bf16[16,80,512]{2,1,0:T(8,128)(2,1)S(1)}, u32[]{:S(2)}, u32[]{:S(2)}) %all-to-all-start.2) | async-done | bytes 1310752 | tf_op jit(solution)/shard_map/all_to_all | solution.py:553
  103.0 3.7 %shard_map.131 = bf16[64,512]{1,0:T(8,128)(2,1)} custom-call(s32[64]{0:T(128)} %fusion.1.slot_ref, bf16[16,80,512]{2,1,0:T(8,128)(2,1)} %copy-done.3, bf16[16,16,512]{2,1,0:T(8,128)(2,1)} %all_to_all.15.got_ref, bf16[1,512]{1,0:T(2,128)(2,1)} %copy-done.2, bf16[192,16,512]{2,1,0:T(8,128)(2,1)} %constant_dynamic-update-slice_fusion.own_ref, ...), custom_call_target="tpu_custom_call" | custom-call | flops 300000000 | bytes 2097152 | tf_op jit(solution)/shard_map/pallas_call | solution.py:284
  106.8 2.7 %collective-permute-start.6 = (bf16[64,512]{1,0:T(8,128)(2,1)}, bf16[64,512]{1,0:T(8,128)(2,1)S(1)}, u32[]{:S(2)}, u32[]{:S(2)}) collective-permute-start(bf16[64,512]{1,0:T(8,128)(2,1)} %shard_map.131), channel_id=1, source_target_pairs={{64,0},{96,32},{0,64},{32,96},{65,1},{97,33},{1,65},{33,97},{66,2}... | collective-permute-start | bytes 196616 | tf_op jit(solution)/shard_map/ppermute | solution.py:478
  115.2 2.6 %collective-permute-start.8 = (bf16[4,64,512]{2,1,0:T(8,128)(2,1)S(1)}, bf16[4,64,512]{2,1,0:T(8,128)(2,1)S(1)}, u32[]{:S(2)}, u32[]{:S(2)}) collective-permute-start(bf16[4,64,512]{2,1,0:T(8,128)(2,1)S(1)} %get-tuple-element.58), channel_id=1, source_target_pairs={{4,0},{5,1},{6,2},{7,3},{8,4},{9,5},{10,6},{11,7},{12,8},{13,9},{1... | collective-permute-start | bytes 786440 | tf_op jit(solution)/shard_map/ppermute | solution.py:489
  117.9 5.0 %collective-permute-done.9 = bf16[4,64,512]{2,1,0:T(8,128)(2,1)S(1)} collective-permute-done((bf16[4,64,512]{2,1,0:T(8,128)(2,1)S(1)}, bf16[4,64,512]{2,1,0:T(8,128)(2,1)S(1)}, u32[]{:S(2)}, u32[]{:S(2)}) %collective-permute-start.9) | collective-permute-done | bytes 262176 | tf_op jit(solution)/shard_map/ppermute | solution.py:489
  126.3 2.7 %collective-permute-start.11 = (bf16[4,4,64,512]{3,2,1,0:T(8,128)(2,1)S(1)}, bf16[4,4,64,512]{3,2,1,0:T(8,128)(2,1)S(1)}, u32[]{:S(2)}, u32[]{:S(2)}) collective-permute-start(bf16[4,4,64,512]{3,2,1,0:T(8,128)(2,1)S(1)} %pad_maximum_fusion.refs_2_), channel_id=1, source_target_pairs={{1,0},{2,1},{3,2},{0,3},{5,4},{6,5},{7,6},{4,7},{9,8},{10,9},{11,1... | collective-permute-start | bytes 3145736 | tf_op jit(solution)/shard_map/ppermute | solution.py:489
  130.2 6.5 %shard_map.132 = (f32[256,1536]{1,0:T(8,128)}, f32[256,128]{1,0:T(8,128)}) custom-call(s32[4]{0:T(128)} %pad_add_fusion.refs_0_, f32[1,8192]{1,0:T(1,128)} %bitcast.16, bf16[4,4,64,512]{3,2,1,0:T(8,128)(2,1)} %copy-done.4, bf16[8192,768]{1,0:T(8,128)(2,1)} %refs_4_.3, bf16[8192,768]{1,0:T(8,128)(2,1)} %collective-permute-done.13.refs_4_.refs_5_), custom_call_target="tpu_custom_call" | custom-call | flops 524288 | bytes 131072 | tf_op jit(solution)/shard_map/pallas_call | solution.py:411
  136.8 17.2 %all-gather.6.cloned.1.call-done = bf16[4096,512]{1,0:T(8,128)(2,1)} async-done(((bf16[64,512]{1,0:T(8,128)(2,1)}), bf16[4096,512]{1,0:T(8,128)(2,1)}) %all-gather.6.cloned.1.call-update) | async-done | bytes 4194320 | tf_op jit(solution)/shard_map/all_gather | solution.py:550
  153.9 14.4 %shard_map.133 = (f32[256,1536]{1,0:T(8,128)}, f32[1,256]{1,0:T(1,128)}) custom-call(s32[4]{0:T(128)} %pad_add_fusion.refs_0_, f32[1,8192]{1,0:T(1,128)} %bitcast.17, bf16[4,16,64,512]{3,2,1,0:T(8,128)(2,1)} %bitcast.15, bf16[8192,768]{1,0:T(8,128)(2,1)} %refs_4_.3, bf16[8192,768]{1,0:T(8,128)(2,1)} %collective-permute-done.13.refs_4_.refs_5_), custom_call_target="tpu_custom_call" | custom-call | flops 2097152 | bytes 524288 | tf_op jit(solution)/shard_map/pallas_call | solution.py:411
  168.4 2.5 %collective-permute-start.14 = (bf16[2,4,64,512]{3,2,1,0:T(8,128)(2,1)S(1)}, bf16[2,4,64,512]{3,2,1,0:T(8,128)(2,1)S(1)}, u32[]{:S(2)}, u32[]{:S(2)}) collective-permute-start(bf16[2,4,64,512]{3,2,1,0:T(8,128)(2,1)S(1)} %slice.14), channel_id=1, source_target_pairs={{1,0},{2,1},{3,2},{0,3},{5,4},{6,5},{7,6},{4,7},{9,8},{10,9},{11,1... | collective-permute-start | bytes 1572872 | tf_op jit(solution)/shard_map/ppermute | solution.py:489
  170.9 11.8 %shard_map.134 = (f32[256,1536]{1,0:T(8,128)}, f32[256,128]{1,0:T(8,128)}) custom-call(s32[4]{0:T(128)} %pad_add_fusion.refs_0_, f32[1,8192]{1,0:T(1,128)} %bitcast.18, bf16[4,4,64,512]{3,2,1,0:T(8,128)(2,1)} %copy-done.6, bf16[4,4,64,512]{3,2,1,0:T(8,128)(2,1)} %copy-done.5, bf16[8192,768]{1,0:T(8,128)(2,1)} %refs_4_.3, ...), custom_call_target="tpu_custom_call" | custom-call | flops 1048576 | bytes 262144 | tf_op jit(solution)/shard_map/pallas_call | solution.py:411
  183.7 8.5 %shard_map.135 = (f32[256,768]{1,0:T(8,128)}, f32[256,768]{1,0:T(8,128)}, f32[1,512]{1,0:T(1,128)}) custom-call(s32[4]{0:T(128)} %pad_add_fusion.refs_0_, f32[1,8192]{1,0:T(1,128)} %bitcast.19, bf16[2,4,64,512]{3,2,1,0:T(8,128)(2,1)} %copy-done.7, bf16[2,4,64,512]{3,2,1,0:T(8,128)(2,1)} %copy-done.8, bf16[8192,768]{1,0:T(8,128)(2,1)} %refs_4_.3, ...), custom_call_target="tpu_custom_call" | custom-call | flops 524288 | bytes 131072 | tf_op jit(solution)/shard_map/pallas_call | solution.py:411
  193.5 2.4 %collective-permute-start.17 = (f32[1,512]{1,0:T(1,128)}, f32[1,512]{1,0:T(1,128)S(1)}, u32[]{:S(2)}, u32[]{:S(2)}) collective-permute-start(f32[1,512]{1,0:T(1,128)} %get-tuple-element.54), channel_id=1, source_target_pairs={{64,0},{96,32},{0,64},{32,96},{65,1},{97,33},{1,65},{33,97},{66,2}... | collective-permute-start | bytes 6152 | tf_op jit(solution)/shard_map/ppermute | solution.py:478
  202.4 2.4 %collective-permute-start.21 = (f32[1,512]{1,0:T(1,128)S(1)}, f32[1,512]{1,0:T(1,128)S(1)}, u32[]{:S(2)}, u32[]{:S(2)}) collective-permute-start(f32[1,512]{1,0:T(1,128)S(1)} %log_add_fusion.2), channel_id=1, source_target_pairs={{8,0},{12,4},{0,8},{4,12},{9,1},{13,5},{1,9},{5,13},{10,2},{14,6},... | collective-permute-start | bytes 6152 | tf_op jit(solution)/shard_map/ppermute | solution.py:478
  207.5 2.6 %collective-permute-start.24 = (f32[1,512]{1,0:T(1,128)S(1)}, f32[1,512]{1,0:T(1,128)S(1)}, u32[]{:S(2)}, u32[]{:S(2)}) collective-permute-start(f32[1,512]{1,0:T(1,128)S(1)} %log_add_fusion.1), channel_id=1, source_target_pairs={{2,0},{3,1},{0,2},{1,3},{6,4},{7,5},{4,6},{5,7},{10,8},{11,9},{8,1... | collective-permute-start | bytes 6152 | tf_op jit(solution)/shard_map/ppermute | solution.py:478
  212.9 3.0 %collective-permute-start.26 = (f32[1,512]{1,0:T(1,128)S(1)}, f32[1,512]{1,0:T(1,128)S(1)}, u32[]{:S(2)}, u32[]{:S(2)}) collective-permute-start(f32[1,512]{1,0:T(1,128)S(1)} %log_add_fusion.no_ref), channel_id=1, source_target_pairs={{0,16},{16,0},{1,17},{17,1},{2,18},{18,2},{3,19},{19,3},{4,20},{20... | collective-permute-start | bytes 6152 | tf_op jit(solution)/shard_map/ppermute | solution.py:579
  (92 shorter events, 45.5 us)
Async XLA Ops:
  6.5 62.8 %all-gather.4.cloned.1.call-start = ((), (), s32[]{:S(2)}) async-start(), calls=%async_computation.3 | async-start | bytes 7077888 | tf_op jit(solution)/shard_map/all_gather | solution.py:519
  7.3 123.0 %collective-permute-start.13 = (bf16[8192,768]{1,0:T(8,128)(2,1)}, bf16[8192,768]{1,0:T(8,128)(2,1)}, u32[]{:S(2)}, u32[]{:S(2)}) collective-permute-start(bf16[8192,768]{1,0:T(8,128)(2,1)} %refs_4_.3), channel_id=1, source_target_pairs={{0,16},{16,0},{1,17},{17,1},{2,18},{18,2},{3,19},{19,3},{4,20},{20... | collective-permute-start | bytes 37748744 | tf_op jit(solution)/shard_map/ppermute | solution.py:518
  8.8 29.3 %collective-permute-start = (bf16[48,16,512]{2,1,0:T(8,128)(2,1)}, bf16[48,16,512]{2,1,0:T(8,128)(2,1)S(1)}, u32[]{:S(2)}, u32[]{:S(2)}) collective-permute-start(bf16[48,16,512]{2,1,0:T(8,128)(2,1)} %param.23), channel_id=1, source_target_pairs={{32,0},{64,32},{96,64},{0,96},{33,1},{65,33},{97,65},{1,97},{34,2}... | collective-permute-start | bytes 2359304 | tf_op jit(solution)/shard_map/ppermute | solution.py:478
  11.6 26.4 %collective-permute-start.1 = (bf16[48,16,512]{2,1,0:T(8,128)(2,1)}, bf16[48,16,512]{2,1,0:T(8,128)(2,1)S(1)}, u32[]{:S(2)}, u32[]{:S(2)}) collective-permute-start(bf16[48,16,512]{2,1,0:T(8,128)(2,1)} %param.23), channel_id=1, source_target_pairs={{96,0},{0,32},{32,64},{64,96},{97,1},{1,33},{33,65},{65,97},{98,2}... | collective-permute-start | bytes 2359304 | tf_op jit(solution)/shard_map/ppermute | solution.py:478
  38.0 28.9 %all-to-all-start.1 = ((bf16[16,64,512]{2,1,0:T(8,128)(2,1)}), bf16[16,64,512]{2,1,0:T(8,128)(2,1)S(1)}, u32[]{:S(2)}, u32[]{:S(2)}) async-start(bf16[16,64,512]{2,1,0:T(8,128)(2,1)} %get-tuple-element.34), calls=%async_computation.1 | async-start | bytes 2097152 | tf_op jit(solution)/shard_map/all_to_all | solution.py:542
  45.8 108.1 %all-gather.6.cloned.1.call-start = ((), (), s32[]{:S(2)}) async-start(), calls=%async_computation.4 | async-start | bytes 4259840 | tf_op jit(solution)/shard_map/all_gather | solution.py:550
  46.7 15.3 %collective-permute-start.2 = (bf16[24,16,512]{2,1,0:T(8,128)(2,1)}, bf16[24,16,512]{2,1,0:T(8,128)(2,1)}, u32[]{:S(2)}, u32[]{:S(2)}) collective-permute-start(bf16[24,16,512]{2,1,0:T(8,128)(2,1)} %slice.12), channel_id=1, source_target_pairs={{32,0},{64,32},{96,64},{0,96},{33,1},{65,33},{97,65},{1,97},{34,2}... | collective-permute-start | bytes 1179656 | tf_op jit(solution)/shard_map/ppermute | solution.py:478
  47.4 17.7 %collective-permute-start.3 = (bf16[24,16,512]{2,1,0:T(8,128)(2,1)}, bf16[24,16,512]{2,1,0:T(8,128)(2,1)S(1)}, u32[]{:S(2)}, u32[]{:S(2)}) collective-permute-start(bf16[24,16,512]{2,1,0:T(8,128)(2,1)} %slice.13), channel_id=1, source_target_pairs={{96,0},{0,32},{32,64},{64,96},{97,1},{1,33},{33,65},{65,97},{98,2}... | collective-permute-start | bytes 1179656 | tf_op jit(solution)/shard_map/ppermute | solution.py:478
  67.8 13.3 %collective-permute-start.4 = (bf16[192,16,512]{2,1,0:T(8,128)(2,1)}, bf16[192,16,512]{2,1,0:T(8,128)(2,1)}, u32[]{:S(2)}, u32[]{:S(2)}) collective-permute-start(bf16[192,16,512]{2,1,0:T(8,128)(2,1)} %constant_dynamic-update-slice_fusion.own_ref), channel_id=1, source_target_pairs={{0,16},{16,0},{1,17},{17,1},{2,18},{18,2},{3,19},{19,3},{4,20},{20... | collective-permute-start | bytes 9437192 | tf_op jit(solution)/shard_map/ppermute | solution.py:547
  72.9 29.1 %all-to-all-start.2 = ((bf16[16,80,512]{2,1,0:T(8,128)(2,1)}), bf16[16,80,512]{2,1,0:T(8,128)(2,1)S(1)}, u32[]{:S(2)}, u32[]{:S(2)}) async-start(bf16[16,80,512]{2,1,0:T(8,128)(2,1)} %shard_map.130), calls=%async_computation.2 | async-start | bytes 2621440 | tf_op jit(solution)/shard_map/all_to_all | solution.py:553
  106.8 4.6 %collective-permute-start.7 = (bf16[64,512]{1,0:T(8,128)(2,1)}, bf16[64,512]{1,0:T(8,128)(2,1)S(1)}, u32[]{:S(2)}, u32[]{:S(2)}) collective-permute-start(bf16[64,512]{1,0:T(8,128)(2,1)} %shard_map.131), channel_id=1, source_target_pairs={{96,0},{0,32},{32,64},{64,96},{97,1},{1,33},{33,65},{65,97},{98,2}... | collective-permute-start | bytes 196616 | tf_op jit(solution)/shard_map/ppermute | solution.py:478
  106.8 5.3 %collective-permute-start.6 = (bf16[64,512]{1,0:T(8,128)(2,1)}, bf16[64,512]{1,0:T(8,128)(2,1)S(1)}, u32[]{:S(2)}, u32[]{:S(2)}) collective-permute-start(bf16[64,512]{1,0:T(8,128)(2,1)} %shard_map.131), channel_id=1, source_target_pairs={{64,0},{96,32},{0,64},{32,96},{65,1},{97,33},{1,65},{33,97},{66,2}... | collective-permute-start | bytes 196616 | tf_op jit(solution)/shard_map/ppermute | solution.py:478
  109.6 4.7 %collective-permute-start.5 = (bf16[64,512]{1,0:T(8,128)(2,1)}, bf16[64,512]{1,0:T(8,128)(2,1)S(1)}, u32[]{:S(2)}, u32[]{:S(2)}) collective-permute-start(bf16[64,512]{1,0:T(8,128)(2,1)} %shard_map.131), channel_id=1, source_target_pairs={{32,0},{64,32},{96,64},{0,96},{33,1},{65,33},{97,65},{1,97},{34,2}... | collective-permute-start | bytes 196616 | tf_op jit(solution)/shard_map/ppermute | solution.py:478
  115.2 7.7 %collective-permute-start.9 = (bf16[4,64,512]{2,1,0:T(8,128)(2,1)S(1)}, bf16[4,64,512]{2,1,0:T(8,128)(2,1)S(1)}, u32[]{:S(2)}, u32[]{:S(2)}) collective-permute-start(bf16[4,64,512]{2,1,0:T(8,128)(2,1)S(1)} %get-tuple-element.58), channel_id=1, source_target_pairs={{8,0},{9,1},{10,2},{11,3},{12,4},{13,5},{14,6},{15,7},{0,8},{1,9},... | collective-permute-start | bytes 786440 | tf_op jit(solution)/shard_map/ppermute | solution.py:489
  115.2 8.9 %collective-permute-start.8 = (bf16[4,64,512]{2,1,0:T(8,128)(2,1)S(1)}, bf16[4,64,512]{2,1,0:T(8,128)(2,1)S(1)}, u32[]{:S(2)}, u32[]{:S(2)}) collective-permute-start(bf16[4,64,512]{2,1,0:T(8,128)(2,1)S(1)} %get-tuple-element.58), channel_id=1, source_target_pairs={{4,0},{5,1},{6,2},{7,3},{8,4},{9,5},{10,6},{11,7},{12,8},{13,9},{1... | collective-permute-start | bytes 786440 | tf_op jit(solution)/shard_map/ppermute | solution.py:489
  117.9 8.2 %collective-permute-start.10 = (bf16[4,64,512]{2,1,0:T(8,128)(2,1)S(1)}, bf16[4,64,512]{2,1,0:T(8,128)(2,1)S(1)}, u32[]{:S(2)}, u32[]{:S(2)}) collective-permute-start(bf16[4,64,512]{2,1,0:T(8,128)(2,1)S(1)} %get-tuple-element.58), channel_id=1, source_target_pairs={{12,0},{13,1},{14,2},{15,3},{0,4},{1,5},{2,6},{3,7},{4,8},{5,9},{6... | collective-permute-start | bytes 786440 | tf_op jit(solution)/shard_map/ppermute | solution.py:489
  126.2 42.0 %collective-permute-start.12 = (bf16[4,4,64,512]{3,2,1,0:T(8,128)(2,1)S(1)}, bf16[4,4,64,512]{3,2,1,0:T(8,128)(2,1)S(1)}, u32[]{:S(2)}, u32[]{:S(2)}) collective-permute-start(bf16[4,4,64,512]{3,2,1,0:T(8,128)(2,1)S(1)} %pad_maximum_fusion.refs_2_), channel_id=1, source_target_pairs={{3,0},{0,1},{1,2},{2,3},{7,4},{4,5},{5,6},{6,7},{11,8},{8,9},{9,10... | collective-permute-start | bytes 3145736 | tf_op jit(solution)/shard_map/ppermute | solution.py:489
  126.3 42.0 %collective-permute-start.11 = (bf16[4,4,64,512]{3,2,1,0:T(8,128)(2,1)S(1)}, bf16[4,4,64,512]{3,2,1,0:T(8,128)(2,1)S(1)}, u32[]{:S(2)}, u32[]{:S(2)}) collective-permute-start(bf16[4,4,64,512]{3,2,1,0:T(8,128)(2,1)S(1)} %pad_maximum_fusion.refs_2_), channel_id=1, source_target_pairs={{1,0},{2,1},{3,2},{0,3},{5,4},{6,5},{7,6},{4,7},{9,8},{10,9},{11,1... | collective-permute-start | bytes 3145736 | tf_op jit(solution)/shard_map/ppermute | solution.py:489
  168.4 14.3 %collective-permute-start.14 = (bf16[2,4,64,512]{3,2,1,0:T(8,128)(2,1)S(1)}, bf16[2,4,64,512]{3,2,1,0:T(8,128)(2,1)S(1)}, u32[]{:S(2)}, u32[]{:S(2)}) collective-permute-start(bf16[2,4,64,512]{3,2,1,0:T(8,128)(2,1)S(1)} %slice.14), channel_id=1, source_target_pairs={{1,0},{2,1},{3,2},{0,3},{5,4},{6,5},{7,6},{4,7},{9,8},{10,9},{11,1... | collective-permute-start | bytes 1572872 | tf_op jit(solution)/shard_map/ppermute | solution.py:489
  170.9 11.9 %collective-permute-start.15 = (bf16[2,4,64,512]{3,2,1,0:T(8,128)(2,1)S(1)}, bf16[2,4,64,512]{3,2,1,0:T(8,128)(2,1)S(1)}, u32[]{:S(2)}, u32[]{:S(2)}) collective-permute-start(bf16[2,4,64,512]{3,2,1,0:T(8,128)(2,1)S(1)} %slice.15), channel_id=1, source_target_pairs={{3,0},{0,1},{1,2},{2,3},{7,4},{4,5},{5,6},{6,7},{11,8},{8,9},{9,10... | collective-permute-start | bytes 1572872 | tf_op jit(solution)/shard_map/ppermute | solution.py:489
  192.3 4.6 %collective-permute-start.18 = (f32[1,512]{1,0:T(1,128)}, f32[1,512]{1,0:T(1,128)S(1)}, u32[]{:S(2)}, u32[]{:S(2)}) collective-permute-start(f32[1,512]{1,0:T(1,128)} %get-tuple-element.54), channel_id=1, source_target_pairs={{96,0},{0,32},{32,64},{64,96},{97,1},{1,33},{33,65},{65,97},{98,2}... | collective-permute-start | bytes 6152 | tf_op jit(solution)/shard_map/ppermute | solution.py:478
  193.5 4.2 %collective-permute-start.17 = (f32[1,512]{1,0:T(1,128)}, f32[1,512]{1,0:T(1,128)S(1)}, u32[]{:S(2)}, u32[]{:S(2)}) collective-permute-start(f32[1,512]{1,0:T(1,128)} %get-tuple-element.54), channel_id=1, source_target_pairs={{64,0},{96,32},{0,64},{32,96},{65,1},{97,33},{1,65},{33,97},{66,2}... | collective-permute-start | bytes 6152 | tf_op jit(solution)/shard_map/ppermute | solution.py:478
  199.5 17.2 %collective-permute-start.19 = (f32[256,768]{1,0:T(8,128)}, f32[256,768]{1,0:T(8,128)S(1)}, u32[]{:S(2)}, u32[]{:S(2)}) collective-permute-start(f32[256,768]{1,0:T(8,128)} %get-tuple-element.55), channel_id=1, source_target_pairs={{0,16},{16,0},{1,17},{17,1},{2,18},{18,2},{3,19},{19,3},{4,20},{20... | collective-permute-start | bytes 2359304 | tf_op jit(solution)/shard_map/ppermute | solution.py:578
  201.2 4.8 %collective-permute-start.22 = (f32[1,512]{1,0:T(1,128)S(1)}, f32[1,512]{1,0:T(1,128)S(1)}, u32[]{:S(2)}, u32[]{:S(2)}) collective-permute-start(f32[1,512]{1,0:T(1,128)S(1)} %log_add_fusion.2), channel_id=1, source_target_pairs={{12,0},{0,4},{4,8},{8,12},{13,1},{1,5},{5,9},{9,13},{14,2},{2,6},{... | collective-permute-start | bytes 6152 | tf_op jit(solution)/shard_map/ppermute | solution.py:478
  (18 other events, 94.7 us)
Sparse Core Ops, SparseCore 0:
  9.0 55.8 all-gather.3
  67.9 85.9 all-gather.5

commit v6 on v4

--- a/solution.py
+++ b/solution.py
@@ -13,7 +13,6 @@
 HD = 128
 CTX = 64
 RANK = 16
-HELD = 48
 REQ = 64
 TEN = 16
 COLS = WIDTH // TEN
@@ -103,20 +102,12 @@
     )(lengths, queries, keys, values, fresh_key, fresh_value, residual)
 
 
-def start_rows(slot_ref, tables, rows_s, sem):
-    held = tables[0].shape[0]
-
+def start_rows(slot_ref, table_ref, rows_s, sem):
     def one(r, carry):
-        slot = slot_ref[r]
-        for n, table_ref in enumerate(tables):
-
-            @pl.when((slot >= n * held) & (slot < (n + 1) * held))
-            def _():
-                pltpu.make_async_copy(table_ref.at[slot - n * held], rows_s.at[r], sem).start()
-
+        pltpu.make_async_copy(table_ref.at[slot_ref[r]], rows_s.at[r], sem).start()
         return carry
 
-    lax.fori_loop(0, REQ, one, 0, unroll=4)
+    lax.fori_loop(0, REQ, one, 0, unroll=8)
 
 
 def wait_rows(table_ref, rows_s, sem):
@@ -179,7 +170,7 @@
 
 
 def rank_kernel(idx_ref, got_ref, table_ref, partial_ref, o_ref, rows_s, block_s, sem, out_sem):
-    start_rows(idx_ref, [table_ref], rows_s, sem)
+    start_rows(idx_ref, table_ref, rows_s, sem)
     attended = attended_rows(got_ref).astype(BF16)
     wait_rows(table_ref, rows_s, sem)
     rows = rows_s[...].reshape(REQ * RANK, COLS)
@@ -258,13 +249,11 @@
     )(sums, got, gain)
 
 
-def expert_kernel(
-    slot_ref, sums_ref, got_ref, gain_ref, own_ref, sib_ref, o_ref, rows_s, kinds_s, sem
-):
-    start_rows(slot_ref, [own_ref, sib_ref], rows_s, sem)
+def expert_kernel(idx_ref, sums_ref, got_ref, gain_ref, table_ref, o_ref, rows_s, kinds_s, sem):
+    start_rows(idx_ref, table_ref, rows_s, sem)
     base = split_kinds(residual_rows(got_ref), kinds_s)[0] + add_all(sums_ref, 0, REQ)
     rank = add_all(sums_ref, REQ, SENT)
-    wait_rows(own_ref, rows_s, sem)
+    wait_rows(table_ref, rows_s, sem)
     rows = rows_s[...].reshape(REQ * RANK, COLS)
     delta = jnp.zeros((REQ, COLS), F32)
     for n in range(2):
@@ -279,13 +268,13 @@
     o_ref[...] = (hidden * gain_ref[...].astype(F32)).astype(BF16)
 
 
-def expert_rows(slots, sums, got, gain, own, sib):
+def expert_rows(index, sums, got, gain, table):
     near = pl.BlockSpec(memory_space=pltpu.VMEM)
     return pl.pallas_call(
         expert_kernel,
         in_specs=[pl.BlockSpec(memory_space=pltpu.SMEM)]
         + [near] * 3
-        + [pl.BlockSpec(memory_space=pl.ANY)] * 2,
+        + [pl.BlockSpec(memory_space=pl.ANY)],
         out_specs=near,
         out_shape=jax.ShapeDtypeStruct((REQ, COLS), BF16),
         scratch_shapes=[
@@ -295,7 +284,7 @@
         ],
         compiler_params=params(56),
         cost_estimate=pl.CostEstimate(flops=3 * 10**8, bytes_accessed=2 * MIB, transcendentals=0),
-    )(slots, sums, got, gain, own, sib)
+    )(index, sums, got, gain, table)
 
 
 def tensor_index(at, first, second):
@@ -322,17 +311,13 @@
 
     starts = []
     for n, (which, block, offsets) in enumerate(pieces):
-        index = block if offsets is None else tensor_index(at_ref, *offsets)
+        index = tensor_index(at_ref, *offsets)
         start = pl.multiple_of(index * COLS, COLS)
         starts.append(start)
         run, part = n // 2, pl.ds(n % 2 * COLS, COLS)
         for y in range(NY):
-            if offsets is None:
-                source = x_refs[which].at[y, block]
-                place = y
-            else:
-                source = x_refs[which].at[block, y]
-                place = lax.rem(at_ref[0] + y, NY)
+            source = x_refs[which].at[block, y]
+            place = lax.rem(at_ref[0] + y, NY)
             pltpu.make_async_copy(source, x_s.at[run, place, :, part], x_sem.at[run]).start()
         for side, w_ref in enumerate((wo_ref, ws_ref)):
             pltpu.make_async_copy(
@@ -493,6 +478,14 @@
 SECOND = ("z", "x")
 
 
+def plane_of(rows):
+    return jnp.stack([rows] + [from_offset(rows, "y", d) for d in range(1, 4)])
+
+
+def block_of(plane):
+    return jnp.stack([plane] + [from_core_offset(plane, FIRST, d) for d in range(1, 4)])
+
+
 def opposite(after, before, axes):
     half = after.shape[0] // 2
     return from_core_offset(after[:half], axes, 1), from_core_offset(before[half:], axes, 3)
@@ -517,11 +510,7 @@
     place = jnp.stack([lax.axis_index(axis) for axis in ("y", "x", "z", "c")]).astype(jnp.int32)
     head_sib = lax.ppermute(vocabulary_head_matrix, "c", SWAP)
     down = lax.all_gather(lowrank_down_factors, ("y", "c"), axis=0, tiled=True)
-    owner = request_adapter_index // HELD
-    slots = ((owner // 2 - place[0]) % NY) * HELD + request_adapter_index % HELD
-    slots = slots + jnp.where(owner % 2 == place[3], 0, NY * HELD)
-    up_after = from_offset(lowrank_up_factors, "y", 1)
-    up_before = from_offset(lowrank_up_factors, "y", 3)
+    up = lax.all_gather(lowrank_up_factors, ("y", "c"), axis=0, tiled=True)
     gain = lax.dynamic_slice(final_norm_scale, (lax.axis_index(TENSOR) * COLS,), (COLS,))
     gain = gain.reshape(1, COLS)
     inverse = 1.0 / final_norm_scale.astype(F32)
@@ -541,35 +530,33 @@
     amateur = lax.all_to_all(amateur, TENSOR, split_axis=0, concat_axis=0, tiled=True)
     amateur = amateur_rows(amateur, got, gain)
     amateur, got = lax.optimization_barrier((amateur, got))
-    gathered = lax.all_gather(amateur, ("y", "x", "z"), axis=0, tiled=False)
-    gathered = gathered.reshape(NY, TEN, REQ, COLS)
     expert = with_rank_sums(request_adapter_index, got, down, expert)
     sums = lax.all_to_all(expert, TENSOR, split_axis=0, concat_axis=0, tiled=True)
-    up_after, up_before, _ = lax.optimization_barrier((up_after, up_before, expert))
-    half = HELD // 2
-    up_far = (from_offset(up_after[:half], "y", 1), from_offset(up_before[half:], "y", 3))
-    up_own = jnp.concatenate([lowrank_up_factors, up_after, *up_far, up_before], axis=0)
-    up_sib = lax.ppermute(up_own, "c", SWAP)
-    expert = expert_rows(slots, sums, got, gain, up_own, up_sib)
-
-    plane = jnp.stack([expert] + [from_offset(expert, "y", d) for d in range(1, 4)])
-    after = from_core_offset(plane, FIRST, 1)
-    before = from_core_offset(plane, FIRST, 3)
-    mine = jnp.stack([plane, after, from_core_offset(plane, FIRST, 2), before])
-    after = from_core_offset(mine, SECOND, 1)
-    before = from_core_offset(mine, SECOND, 3)
+    amateur, _ = lax.optimization_barrier((amateur, expert))
+    amateur, sums = lax.optimization_barrier((plane_of(amateur), sums))
+    amateur, sums = lax.optimization_barrier((block_of(amateur), sums))
+    amateur_after = from_core_offset(amateur, SECOND, 1)
+    amateur_before = from_core_offset(amateur, SECOND, 3)
+    expert = block_of(plane_of(expert_rows(request_adapter_index, sums, got, gain, up)))
+    expert, amateur_after, amateur_before = lax.optimization_barrier(
+        (expert, amateur_after, amateur_before)
+    )
+    after = from_core_offset(expert, SECOND, 1)
+    before = from_core_offset(expert, SECOND, 3)
+    amateur_far = opposite(amateur_after, amateur_before, SECOND)
     weights = (inverse, vocabulary_head_matrix, head_sib)
-    pieces = [(0, n, (n, 0)) for n in range(4)]
-    partial = head_part(place, [mine], pieces, *weights)
-    pieces = [(0, n, None) for n in range(TEN)]
-    other = head_part(place, [gathered], pieces, *weights, amateur=True)
+    own = [(0, n, (n, 0)) for n in range(4)]
+    beside = [(n // 4, n % 4, (n % 4, 1 + 2 * (n // 4))) for n in range(8)]
+    across = [(n // 2, n % 2, (n, 2)) for n in range(4)]
+    partial = head_part(place, [expert], own, *weights)
+    pieces = own + [(1 + n, b, o) for n, b, o in beside] + [(3 + n, b, o) for n, b, o in across]
+    arrays = [amateur, amateur_after, amateur_before, *amateur_far]
+    other = head_part(place, arrays, pieces, *weights, amateur=True)
     after, before, *rest = lax.optimization_barrier((after, before, *partial, *other))
     partial, other = rest[:2], rest[2:]
     far = opposite(after, before, SECOND)
-    pieces = [(n // 4, n % 4, (n % 4, 1 + 2 * (n // 4))) for n in range(8)]
-    partial = head_part(place, [after, before], pieces, *weights, sums=partial)
-    pieces = [(n // 2, n % 2, (n, 2)) for n in range(4)]
-    u_own, u_send, lse = head_part(place, far, pieces, *weights, sums=partial, other=other)
+    partial = head_part(place, [after, before], beside, *weights, sums=partial)
+    u_own, u_send, lse = head_part(place, far, across, *weights, sums=partial, other=other)
     for axis in ("y", "x", "z"):
         lse = combine([lse] + [from_offset(lse, axis, d) for d in range(1, 4)])
         if axis == "y":

time: 226 us -> 231 us (1.022)
  waiting for transfers between devices: 72.3 us -> 83.6 us
  starting transfers between devices: 49.9 us -> 46.2 us
    ppermute x7 -> x14, waiting for transfers between devices: 7.04 us -> 29.6 us  [from_core_offset(): return lax.ppermute(array, ('c', 'x', 'z'), pairs)]
    all_to_all x1, waiting for transfers between devices: 20 us -> 8.59 us  [per_device(): lax.all_to_all(expert, TENSOR, split_axis=0, concat_axis=0, tiled=True)]
    ppermute x7 -> x14, starting transfers between devices: 7.15 us -> 13.6 us  [from_core_offset(): return lax.ppermute(array, ('c', 'x', 'z'), pairs)]
    ppermute x16 -> x15, starting transfers between devices: 17.9 us -> 11.6 us  [from_offset(): return lax.ppermute(array, axis, [((i + offset) % 4, i) for i in range(4)])]
    ppermute x1 -> x0, starting transfers between devices: 5.65 us -> none  [per_device(): up_sib = lax.ppermute(up_own, 'c', SWAP)]
    ppermute x16 -> x15, waiting for transfers between devices: 28.6 us -> 23.4 us  [from_offset(): return lax.ppermute(array, axis, [((i + offset) % 4, i) for i in range(4)])]
    all_gather x1, waiting for transfers between devices: 0.01 us -> 4.63 us  [per_device(): up = lax.all_gather(lowrank_up_factors, ('y', 'c'), axis=0, tiled=True)]
    unnamed x28 -> x22, local copies, waits for them, and re-layouts: 6.6 us -> 2.13 us
  transfers between devices with their start and end apart: 31 -> 36, of which waited for: 21 -> 25; matrix products, arithmetic and copies ran while one was open for 3% -> 3% of each run, Pallas kernels for 23% -> 22%
where the time goes in v6:
time: 231 us; the launch traced here: 229 us
  waiting for transfers between devices  83.6 us (36%)
  Pallas kernels  60.9 us (26%)
  starting transfers between devices  46.2 us (20%)
  blocking collectives  15.6 us (7%)
  between operations  13.7 us (6%)
  local copies, waits for them, and re-layouts  6.34 us (3%)
  other arithmetic  3.18 us (1%)
    pallas_call x4, Pallas kernels, head_part(): pl.pallas_call(lambda *refs: head_kernel(pieces, first, last, amateur, *r...  41 us
    ppermute x14, waiting for transfers between devices, from_core_offset(): return lax.ppermute(array, ('c', 'x', 'z'), pairs)  29.6 us
    ppermute x15, waiting for transfers between devices, from_offset(): return lax.ppermute(array, axis, [((i + offset) % 4, i) for i in range(4)])  23.4 us
    all_to_all x1, blocking collectives, per_device(): got = lax.all_to_all(sent, TENSOR, split_axis=0, concat_axis=0, tiled=True)  15.6 us
    all_to_all x1, waiting for transfers between devices, per_device(): lax.all_to_all(amateur, TENSOR, split_axis=0, concat_axis=0, tiled=True)  15.1 us
    ppermute x14, starting transfers between devices, from_core_offset(): return lax.ppermute(array, ('c', 'x', 'z'), pairs)  13.6 us
    ppermute x15, starting transfers between devices, from_offset(): return lax.ppermute(array, axis, [((i + offset) % 4, i) for i in range(4)])  11.6 us
    all_to_all x1, waiting for transfers between devices, per_device(): lax.all_to_all(expert, TENSOR, split_axis=0, concat_axis=0, tiled=True)  8.59 us
  transfers between devices with their start and end apart: 36, of which 25 were waited for; matrix products, arithmetic and copies ran while one was open for 3% of the time, Pallas kernels for 22%

profile of v6, /device:TPU:1, one launch (start us, length us, event | category | flops | bytes accessed | tf_op | source)
XLA Modules:
  0.0 229.5 jit_solution(8181508114600826335)
XLA Ops:
  9.5 5.0 %shard_map.127 = bf16[16,16,512]{2,1,0:T(8,128)(2,1)} custom-call(s32[4]{0:T(128)} %len_ref.1, bf16[4,2,8192]{2,1,0:T(2,128)(2,1)} %q_ref.1, bf16[4,2,64,1024]{3,2,1,0:T(8,128)(2,1)} %k_ref.1, bf16[4,2,64,1024]{3,2,1,0:T(8,128)(2,1)} %v_ref.1, bf16[4,2,1024]{2,1,0:T(2,128)(2,1)} %ck_ref.1, bf16[4,2,1024]{2,1,0:T(2,128)(2,1)} %cv_ref.1, ...), custom_call_target="tpu_custom_call" | custom-call | flops 300000000 | bytes 3145728 | tf_op jit(solution)/shard_map/pallas_call | solution.py:80
  14.5 15.6 %all_to_all.15.got_ref = bf16[16,16,512]{2,1,0:T(8,128)(2,1)} all-to-all(bf16[16,16,512]{2,1,0:T(8,128)(2,1)} %shard_map.127), channel_id=1, replica_groups=mesh['y'=4,'c'=2,'x'=4,'z'=4] {'x','z'}, dimensions={0} | all-to-all | bytes 524288 | tf_op jit(solution)/shard_map/all_to_all | solution.py:528
  30.1 6.1 %shard_map.128 = (bf16[16,80,512]{2,1,0:T(8,128)(2,1)}, bf16[16,64,512]{2,1,0:T(8,128)(2,1)}) custom-call(bf16[16,16,512]{2,1,0:T(8,128)(2,1)} %all_to_all.15.got_ref, bf16[512,8192]{1,0:T(8,128)(2,1)} %w_ref.1), custom_call_target="tpu_custom_call" | custom-call | flops 1100000000 | bytes 11534336 | tf_op jit(solution)/shard_map/pallas_call | solution.py:154
  36.2 4.0 %all-to-all-start.1 = ((bf16[16,64,512]{2,1,0:T(8,128)(2,1)}), bf16[16,64,512]{2,1,0:T(8,128)(2,1)S(1)}, u32[]{:S(2)}, u32[]{:S(2)}) async-start(bf16[16,64,512]{2,1,0:T(8,128)(2,1)} %get-tuple-element.34), calls=%async_computation.1 | async-start | bytes 2097152 | tf_op jit(solution)/shard_map/all_to_all | solution.py:530
  40.3 15.1 %all-to-all-done.1.sums_ref = bf16[16,64,512]{2,1,0:T(8,128)(2,1)S(1)} async-done(((bf16[16,64,512]{2,1,0:T(8,128)(2,1)}), bf16[16,64,512]{2,1,0:T(8,128)(2,1)S(1)}, u32[]{:S(2)}, u32[]{:S(2)}) %all-to-all-start.1) | async-done | bytes 1048608 | tf_op jit(solution)/shard_map/all_to_all | solution.py:530
  55.7 3.5 %shard_map.130 = bf16[16,80,512]{2,1,0:T(8,128)(2,1)} custom-call(s32[64]{0:T(128)} %idx_ref.3, bf16[16,16,512]{2,1,0:T(8,128)(2,1)} %all_to_all.15.got_ref, bf16[384,16,512]{2,1,0:T(8,128)(2,1)} %all-gather.3.cloned.1.call-done.table_ref, bf16[16,80,512]{2,1,0:T(8,128)(2,1)} %get-tuple-element.37.partial_ref), custom_call_target="tpu_custom_call", output_to_operand_aliasing={{}: (3, {})} | custom-call | flops 140000000 | bytes 2097152 | tf_op jit(solution)/shard_map/pallas_call | solution.py:200
  59.2 4.7 %all-to-all-start.2 = ((bf16[16,80,512]{2,1,0:T(8,128)(2,1)}), bf16[16,80,512]{2,1,0:T(8,128)(2,1)S(1)}, u32[]{:S(2)}, u32[]{:S(2)}) async-start(bf16[16,80,512]{2,1,0:T(8,128)(2,1)} %shard_map.130), calls=%async_computation.2 | async-start | bytes 2621440 | tf_op jit(solution)/shard_map/all_to_all | solution.py:534
  68.4 3.5 %collective-permute-done.1 = bf16[64,512]{1,0:T(8,128)(2,1)S(1)} collective-permute-done((bf16[64,512]{1,0:T(8,128)(2,1)S(1)}, bf16[64,512]{1,0:T(8,128)(2,1)S(1)}, u32[]{:S(2)}, u32[]{:S(2)}) %collective-permute-start.1) | collective-permute-done | bytes 65568 | tf_op jit(solution)/shard_map/ppermute | solution.py:463
  72.9 8.6 %all-to-all-done.2.sums_ref = bf16[16,80,512]{2,1,0:T(8,128)(2,1)S(1)} async-done(((bf16[16,80,512]{2,1,0:T(8,128)(2,1)}), bf16[16,80,512]{2,1,0:T(8,128)(2,1)S(1)}, u32[]{:S(2)}, u32[]{:S(2)}) %all-to-all-start.2) | async-done | bytes 1310752 | tf_op jit(solution)/shard_map/all_to_all | solution.py:534
  83.6 3.4 %collective-permute-done.3 = bf16[4,64,512]{2,1,0:T(8,128)(2,1)S(1)} collective-permute-done((bf16[4,64,512]{2,1,0:T(8,128)(2,1)S(1)}, bf16[4,64,512]{2,1,0:T(8,128)(2,1)S(1)}, u32[]{:S(2)}, u32[]{:S(2)}) %collective-permute-start.3) | collective-permute-done | bytes 262176 | tf_op jit(solution)/shard_map/ppermute | solution.py:474
  94.6 4.6 %all-gather.5.cloned.1.call-done.table_ref = bf16[384,16,512]{2,1,0:T(8,128)(2,1)} async-done(((bf16[48,16,512]{2,1,0:T(8,128)(2,1)}), bf16[384,16,512]{2,1,0:T(8,128)(2,1)}) %all-gather.5.cloned.1.call-update) | async-done | bytes 6291472 | tf_op jit(solution)/shard_map/all_gather | solution.py:513
  99.2 3.7 %shard_map.131 = bf16[64,512]{1,0:T(8,128)(2,1)} custom-call(s32[64]{0:T(128)} %idx_ref.3, bf16[16,80,512]{2,1,0:T(8,128)(2,1)} %copy-done.3, bf16[16,16,512]{2,1,0:T(8,128)(2,1)} %all_to_all.15.got_ref, bf16[1,512]{1,0:T(2,128)(2,1)} %copy-done.2, bf16[384,16,512]{2,1,0:T(8,128)(2,1)} %all-gather.5.cloned.1.call-done.table_ref), custom_call_target="tpu_custom_call" | custom-call | flops 300000000 | bytes 2097152 | tf_op jit(solution)/shard_map/pallas_call | solution.py:273
  108.4 3.3 %collective-permute-done.8 = bf16[64,512]{1,0:T(8,128)(2,1)S(1)} collective-permute-done((bf16[64,512]{1,0:T(8,128)(2,1)}, bf16[64,512]{1,0:T(8,128)(2,1)S(1)}, u32[]{:S(2)}, u32[]{:S(2)}) %collective-permute-start.8) | collective-permute-done | bytes 65568 | tf_op jit(solution)/shard_map/ppermute | solution.py:463
  115.3 5.7 %collective-permute-done.9 = bf16[4,64,512]{2,1,0:T(8,128)(2,1)S(1)} collective-permute-done((bf16[4,64,512]{2,1,0:T(8,128)(2,1)S(1)}, bf16[4,64,512]{2,1,0:T(8,128)(2,1)S(1)}, u32[]{:S(2)}, u32[]{:S(2)}) %collective-permute-start.9) | collective-permute-done | bytes 262176 | tf_op jit(solution)/shard_map/ppermute | solution.py:474
  121.6 6.3 %collective-permute-done.11 = bf16[4,64,512]{2,1,0:T(8,128)(2,1)S(1)} collective-permute-done((bf16[4,64,512]{2,1,0:T(8,128)(2,1)S(1)}, bf16[4,64,512]{2,1,0:T(8,128)(2,1)S(1)}, u32[]{:S(2)}, u32[]{:S(2)}) %collective-permute-start.11) | collective-permute-done | bytes 262176 | tf_op jit(solution)/shard_map/ppermute | solution.py:474
  137.5 6.2 %shard_map.132 = (f32[256,1536]{1,0:T(8,128)}, f32[256,128]{1,0:T(8,128)}) custom-call(s32[4]{0:T(128)} %pad_add_fusion.refs_0_, f32[1,8192]{1,0:T(1,128)} %bitcast.24, bf16[4,4,64,512]{3,2,1,0:T(8,128)(2,1)} %copy-done.5, bf16[8192,768]{1,0:T(8,128)(2,1)} %refs_4_.3, bf16[8192,768]{1,0:T(8,128)(2,1)} %collective-permute-done.16.refs_4_.refs_8_.refs_5_), custom_call_target="tpu_custom_call" | custom-call | flops 524288 | bytes 131072 | tf_op jit(solution)/shard_map/pallas_call | solution.py:396
  143.7 4.6 %collective-permute-done.17.refs_5_ = bf16[2,4,64,512]{3,2,1,0:T(8,128)(2,1)} collective-permute-done((bf16[2,4,64,512]{3,2,1,0:T(8,128)(2,1)}, bf16[2,4,64,512]{3,2,1,0:T(8,128)(2,1)}, u32[]{:S(2)}, u32[]{:S(2)}) %collective-permute-start.17) | collective-permute-done | bytes 524320 | tf_op jit(solution)/shard_map/ppermute | solution.py:474
  148.3 3.4 %collective-permute-done.18.refs_6_ = bf16[2,4,64,512]{3,2,1,0:T(8,128)(2,1)} collective-permute-done((bf16[2,4,64,512]{3,2,1,0:T(8,128)(2,1)}, bf16[2,4,64,512]{3,2,1,0:T(8,128)(2,1)}, u32[]{:S(2)}, u32[]{:S(2)}) %collective-permute-start.18) | collective-permute-done | bytes 524320 | tf_op jit(solution)/shard_map/ppermute | solution.py:474
  151.7 14.4 %shard_map.133 = (f32[256,1536]{1,0:T(8,128)}, f32[1,256]{1,0:T(1,128)}) custom-call(s32[4]{0:T(128)} %pad_add_fusion.refs_0_, f32[1,8192]{1,0:T(1,128)} %bitcast.25, bf16[4,4,64,512]{3,2,1,0:T(8,128)(2,1)} %copy-done.4, bf16[4,4,64,512]{3,2,1,0:T(8,128)(2,1)} %copy-done.6, bf16[4,4,64,512]{3,2,1,0:T(8,128)(2,1)} %collective-permute-done.13.refs_4_, ...), custom_call_target="tpu_custom_call" | custom-call | flops 2097152 | bytes 524288 | tf_op jit(solution)/shard_map/pallas_call | solution.py:396
  169.0 11.8 %shard_map.134 = (f32[256,1536]{1,0:T(8,128)}, f32[256,128]{1,0:T(8,128)}) custom-call(s32[4]{0:T(128)} %pad_add_fusion.refs_0_, f32[1,8192]{1,0:T(1,128)} %bitcast.26, bf16[4,4,64,512]{3,2,1,0:T(8,128)(2,1)} %copy-done.7, bf16[4,4,64,512]{3,2,1,0:T(8,128)(2,1)} %collective-permute-done.15.refs_3_, bf16[8192,768]{1,0:T(8,128)(2,1)} %refs_4_.3, ...), custom_call_target="tpu_custom_call" | custom-call | flops 1048576 | bytes 262144 | tf_op jit(solution)/shard_map/pallas_call | solution.py:396
  181.8 8.5 %shard_map.135 = (f32[256,768]{1,0:T(8,128)}, f32[256,768]{1,0:T(8,128)}, f32[1,512]{1,0:T(1,128)}) custom-call(s32[4]{0:T(128)} %pad_add_fusion.refs_0_, f32[1,8192]{1,0:T(1,128)} %bitcast.27, bf16[2,4,64,512]{3,2,1,0:T(8,128)(2,1)} %copy-done.8, bf16[2,4,64,512]{3,2,1,0:T(8,128)(2,1)} %copy-done.9, bf16[8192,768]{1,0:T(8,128)(2,1)} %refs_4_.3, ...), custom_call_target="tpu_custom_call" | custom-call | flops 524288 | bytes 131072 | tf_op jit(solution)/shard_map/pallas_call | solution.py:396
  196.2 7.8 %collective-permute-start.24 = (f32[256,768]{1,0:T(8,128)}, f32[256,768]{1,0:T(8,128)S(1)}, u32[]{:S(2)}, u32[]{:S(2)}) collective-permute-start(f32[256,768]{1,0:T(8,128)} %get-tuple-element.61), channel_id=1, source_target_pairs={{0,16},{16,0},{1,17},{17,1},{2,18},{18,2},{3,19},{19,3},{4,20},{20... | collective-permute-start | bytes 2359304 | tf_op jit(solution)/shard_map/ppermute | solution.py:564
  207.2 3.2 %collective-permute-done.26 = f32[1,512]{1,0:T(1,128)S(1)} collective-permute-done((f32[1,512]{1,0:T(1,128)S(1)}, f32[1,512]{1,0:T(1,128)S(1)}, u32[]{:S(2)}, u32[]{:S(2)}) %collective-permute-start.26) | collective-permute-done | bytes 2080 | tf_op jit(solution)/shard_map/ppermute | solution.py:463
  213.0 3.2 %collective-permute-done.29 = f32[1,512]{1,0:T(1,128)S(1)} collective-permute-done((f32[1,512]{1,0:T(1,128)S(1)}, f32[1,512]{1,0:T(1,128)S(1)}, u32[]{:S(2)}, u32[]{:S(2)}) %collective-permute-start.29) | collective-permute-done | bytes 2080 | tf_op jit(solution)/shard_map/ppermute | solution.py:463
  (98 shorter events, 59.5 us)
Async XLA Ops:
  6.5 49.1 %all-gather.3.cloned.1.call-start = ((), (), s32[]{:S(2)}) async-start(), calls=%async_computation.3 | async-start | bytes 7077888 | tf_op jit(solution)/shard_map/all_gather | solution.py:512
  7.3 91.9 %all-gather.5.cloned.1.call-start = ((), (), s32[]{:S(2)}) async-start(), calls=%async_computation.4 | async-start | bytes 7077888 | tf_op jit(solution)/shard_map/all_gather | solution.py:513
  8.0 129.5 %collective-permute-start.16 = (bf16[8192,768]{1,0:T(8,128)(2,1)}, bf16[8192,768]{1,0:T(8,128)(2,1)}, u32[]{:S(2)}, u32[]{:S(2)}) collective-permute-start(bf16[8192,768]{1,0:T(8,128)(2,1)} %refs_4_.3), channel_id=1, source_target_pairs={{0,16},{16,0},{1,17},{17,1},{2,18},{18,2},{3,19},{19,3},{4,20},{20... | collective-permute-start | bytes 37748744 | tf_op jit(solution)/shard_map/ppermute | solution.py:511
  36.2 19.3 %all-to-all-start.1 = ((bf16[16,64,512]{2,1,0:T(8,128)(2,1)}), bf16[16,64,512]{2,1,0:T(8,128)(2,1)S(1)}, u32[]{:S(2)}, u32[]{:S(2)}) async-start(bf16[16,64,512]{2,1,0:T(8,128)(2,1)} %get-tuple-element.34), calls=%async_computation.1 | async-start | bytes 2097152 | tf_op jit(solution)/shard_map/all_to_all | solution.py:530
  59.2 22.3 %all-to-all-start.2 = ((bf16[16,80,512]{2,1,0:T(8,128)(2,1)}), bf16[16,80,512]{2,1,0:T(8,128)(2,1)S(1)}, u32[]{:S(2)}, u32[]{:S(2)}) async-start(bf16[16,80,512]{2,1,0:T(8,128)(2,1)} %shard_map.130), calls=%async_computation.2 | async-start | bytes 2621440 | tf_op jit(solution)/shard_map/all_to_all | solution.py:534
  66.0 5.9 %collective-permute-start.1 = (bf16[64,512]{1,0:T(8,128)(2,1)S(1)}, bf16[64,512]{1,0:T(8,128)(2,1)S(1)}, u32[]{:S(2)}, u32[]{:S(2)}) collective-permute-start(bf16[64,512]{1,0:T(8,128)(2,1)S(1)} %shard_map.129), channel_id=1, source_target_pairs={{64,0},{96,32},{0,64},{32,96},{65,1},{97,33},{1,65},{33,97},{66,2}... | collective-permute-start | bytes 196616 | tf_op jit(solution)/shard_map/ppermute | solution.py:463
  66.3 6.5 %collective-permute-start.2 = (bf16[64,512]{1,0:T(8,128)(2,1)S(1)}, bf16[64,512]{1,0:T(8,128)(2,1)S(1)}, u32[]{:S(2)}, u32[]{:S(2)}) collective-permute-start(bf16[64,512]{1,0:T(8,128)(2,1)S(1)} %shard_map.129), channel_id=1, source_target_pairs={{96,0},{0,32},{32,64},{64,96},{97,1},{1,33},{33,65},{65,97},{98,2}... | collective-permute-start | bytes 196616 | tf_op jit(solution)/shard_map/ppermute | solution.py:463
  81.5 5.6 %collective-permute-start.3 = (bf16[4,64,512]{2,1,0:T(8,128)(2,1)S(1)}, bf16[4,64,512]{2,1,0:T(8,128)(2,1)S(1)}, u32[]{:S(2)}, u32[]{:S(2)}) collective-permute-start(bf16[4,64,512]{2,1,0:T(8,128)(2,1)S(1)} %pad_maximum_fusion.2), channel_id=1, source_target_pairs={{4,0},{5,1},{6,2},{7,3},{8,4},{9,5},{10,6},{11,7},{12,8},{13,9},{1... | collective-permute-start | bytes 786440 | tf_op jit(solution)/shard_map/ppermute | solution.py:474
  82.7 6.8 %collective-permute-start.4 = (bf16[4,64,512]{2,1,0:T(8,128)(2,1)S(1)}, bf16[4,64,512]{2,1,0:T(8,128)(2,1)S(1)}, u32[]{:S(2)}, u32[]{:S(2)}) collective-permute-start(bf16[4,64,512]{2,1,0:T(8,128)(2,1)S(1)} %pad_maximum_fusion.2), channel_id=1, source_target_pairs={{8,0},{9,1},{10,2},{11,3},{12,4},{13,5},{14,6},{15,7},{0,8},{1,9},... | collective-permute-start | bytes 786440 | tf_op jit(solution)/shard_map/ppermute | solution.py:474
  83.6 9.0 %collective-permute-start.5 = (bf16[4,64,512]{2,1,0:T(8,128)(2,1)S(1)}, bf16[4,64,512]{2,1,0:T(8,128)(2,1)S(1)}, u32[]{:S(2)}, u32[]{:S(2)}) collective-permute-start(bf16[4,64,512]{2,1,0:T(8,128)(2,1)S(1)} %pad_maximum_fusion.2), channel_id=1, source_target_pairs={{12,0},{13,1},{14,2},{15,3},{0,4},{1,5},{2,6},{3,7},{4,8},{5,9},{6... | collective-permute-start | bytes 786440 | tf_op jit(solution)/shard_map/ppermute | solution.py:474
  92.7 35.3 %collective-permute-start.12 = (bf16[4,4,64,512]{3,2,1,0:T(8,128)(2,1)S(1)}, bf16[4,4,64,512]{3,2,1,0:T(8,128)(2,1)S(1)}, u32[]{:S(2)}, u32[]{:S(2)}) collective-permute-start(bf16[4,4,64,512]{3,2,1,0:T(8,128)(2,1)S(1)} %pad_maximum_fusion.refs_2_), channel_id=1, source_target_pairs={{1,0},{2,1},{3,2},{0,3},{5,4},{6,5},{7,6},{4,7},{9,8},{10,9},{11,1... | collective-permute-start | bytes 3145736 | tf_op jit(solution)/shard_map/ppermute | solution.py:474
  94.6 33.5 %collective-permute-start.13 = (bf16[4,4,64,512]{3,2,1,0:T(8,128)(2,1)S(1)}, bf16[4,4,64,512]{3,2,1,0:T(8,128)(2,1)}, u32[]{:S(2)}, u32[]{:S(2)}) collective-permute-start(bf16[4,4,64,512]{3,2,1,0:T(8,128)(2,1)S(1)} %pad_maximum_fusion.refs_2_), channel_id=1, source_target_pairs={{3,0},{0,1},{1,2},{2,3},{7,4},{4,5},{5,6},{6,7},{11,8},{8,9},{9,10... | collective-permute-start | bytes 3145736 | tf_op jit(solution)/shard_map/ppermute | solution.py:474
  103.6 4.8 %collective-permute-start.7 = (bf16[64,512]{1,0:T(8,128)(2,1)}, bf16[64,512]{1,0:T(8,128)(2,1)S(1)}, u32[]{:S(2)}, u32[]{:S(2)}) collective-permute-start(bf16[64,512]{1,0:T(8,128)(2,1)} %shard_map.131), channel_id=1, source_target_pairs={{64,0},{96,32},{0,64},{32,96},{65,1},{97,33},{1,65},{33,97},{66,2}... | collective-permute-start | bytes 196616 | tf_op jit(solution)/shard_map/ppermute | solution.py:463
  106.7 4.9 %collective-permute-start.8 = (bf16[64,512]{1,0:T(8,128)(2,1)}, bf16[64,512]{1,0:T(8,128)(2,1)S(1)}, u32[]{:S(2)}, u32[]{:S(2)}) collective-permute-start(bf16[64,512]{1,0:T(8,128)(2,1)} %shard_map.131), channel_id=1, source_target_pairs={{96,0},{0,32},{32,64},{64,96},{97,1},{1,33},{33,65},{65,97},{98,2}... | collective-permute-start | bytes 196616 | tf_op jit(solution)/shard_map/ppermute | solution.py:463
  112.6 8.5 %collective-permute-start.9 = (bf16[4,64,512]{2,1,0:T(8,128)(2,1)S(1)}, bf16[4,64,512]{2,1,0:T(8,128)(2,1)S(1)}, u32[]{:S(2)}, u32[]{:S(2)}) collective-permute-start(bf16[4,64,512]{2,1,0:T(8,128)(2,1)S(1)} %get-tuple-element.64), channel_id=1, source_target_pairs={{4,0},{5,1},{6,2},{7,3},{8,4},{9,5},{10,6},{11,7},{12,8},{13,9},{1... | collective-permute-start | bytes 786440 | tf_op jit(solution)/shard_map/ppermute | solution.py:474
  114.9 6.7 %collective-permute-start.10 = (bf16[4,64,512]{2,1,0:T(8,128)(2,1)S(1)}, bf16[4,64,512]{2,1,0:T(8,128)(2,1)S(1)}, u32[]{:S(2)}, u32[]{:S(2)}) collective-permute-start(bf16[4,64,512]{2,1,0:T(8,128)(2,1)S(1)} %get-tuple-element.64), channel_id=1, source_target_pairs={{8,0},{9,1},{10,2},{11,3},{12,4},{13,5},{14,6},{15,7},{0,8},{1,9},... | collective-permute-start | bytes 786440 | tf_op jit(solution)/shard_map/ppermute | solution.py:474
  121.0 6.9 %collective-permute-start.11 = (bf16[4,64,512]{2,1,0:T(8,128)(2,1)S(1)}, bf16[4,64,512]{2,1,0:T(8,128)(2,1)S(1)}, u32[]{:S(2)}, u32[]{:S(2)}) collective-permute-start(bf16[4,64,512]{2,1,0:T(8,128)(2,1)S(1)} %get-tuple-element.64), channel_id=1, source_target_pairs={{12,0},{13,1},{14,2},{15,3},{0,4},{1,5},{2,6},{3,7},{4,8},{5,9},{6... | collective-permute-start | bytes 786440 | tf_op jit(solution)/shard_map/ppermute | solution.py:474
  128.1 38.1 %collective-permute-start.14 = (bf16[4,4,64,512]{3,2,1,0:T(8,128)(2,1)S(1)}, bf16[4,4,64,512]{3,2,1,0:T(8,128)(2,1)S(1)}, u32[]{:S(2)}, u32[]{:S(2)}) collective-permute-start(bf16[4,4,64,512]{3,2,1,0:T(8,128)(2,1)S(1)} %pad_maximum_fusion.1.refs_2_), channel_id=1, source_target_pairs={{1,0},{2,1},{3,2},{0,3},{5,4},{6,5},{7,6},{4,7},{9,8},{10,9},{11,1... | collective-permute-start | bytes 3145736 | tf_op jit(solution)/shard_map/ppermute | solution.py:474
  130.8 35.4 %collective-permute-start.15 = (bf16[4,4,64,512]{3,2,1,0:T(8,128)(2,1)S(1)}, bf16[4,4,64,512]{3,2,1,0:T(8,128)(2,1)}, u32[]{:S(2)}, u32[]{:S(2)}) collective-permute-start(bf16[4,4,64,512]{3,2,1,0:T(8,128)(2,1)S(1)} %pad_maximum_fusion.1.refs_2_), channel_id=1, source_target_pairs={{3,0},{0,1},{1,2},{2,3},{7,4},{4,5},{5,6},{6,7},{11,8},{8,9},{9,10... | collective-permute-start | bytes 3145736 | tf_op jit(solution)/shard_map/ppermute | solution.py:474
  131.7 16.6 %collective-permute-start.17 = (bf16[2,4,64,512]{3,2,1,0:T(8,128)(2,1)}, bf16[2,4,64,512]{3,2,1,0:T(8,128)(2,1)}, u32[]{:S(2)}, u32[]{:S(2)}) collective-permute-start(bf16[2,4,64,512]{3,2,1,0:T(8,128)(2,1)} %slice.12), channel_id=1, source_target_pairs={{1,0},{2,1},{3,2},{0,3},{5,4},{6,5},{7,6},{4,7},{9,8},{10,9},{11,1... | collective-permute-start | bytes 1572872 | tf_op jit(solution)/shard_map/ppermute | solution.py:474
  136.3 15.4 %collective-permute-start.18 = (bf16[2,4,64,512]{3,2,1,0:T(8,128)(2,1)}, bf16[2,4,64,512]{3,2,1,0:T(8,128)(2,1)}, u32[]{:S(2)}, u32[]{:S(2)}) collective-permute-start(bf16[2,4,64,512]{3,2,1,0:T(8,128)(2,1)} %slice.13), channel_id=1, source_target_pairs={{3,0},{0,1},{1,2},{2,3},{7,4},{4,5},{5,6},{6,7},{11,8},{8,9},{9,10... | collective-permute-start | bytes 1572872 | tf_op jit(solution)/shard_map/ppermute | solution.py:474
  166.3 14.5 %collective-permute-start.19 = (bf16[2,4,64,512]{3,2,1,0:T(8,128)(2,1)S(1)}, bf16[2,4,64,512]{3,2,1,0:T(8,128)(2,1)S(1)}, u32[]{:S(2)}, u32[]{:S(2)}) collective-permute-start(bf16[2,4,64,512]{3,2,1,0:T(8,128)(2,1)S(1)} %slice.14), channel_id=1, source_target_pairs={{1,0},{2,1},{3,2},{0,3},{5,4},{6,5},{7,6},{4,7},{9,8},{10,9},{11,1... | collective-permute-start | bytes 1572872 | tf_op jit(solution)/shard_map/ppermute | solution.py:474
  167.7 13.2 %collective-permute-start.20 = (bf16[2,4,64,512]{3,2,1,0:T(8,128)(2,1)S(1)}, bf16[2,4,64,512]{3,2,1,0:T(8,128)(2,1)S(1)}, u32[]{:S(2)}, u32[]{:S(2)}) collective-permute-start(bf16[2,4,64,512]{3,2,1,0:T(8,128)(2,1)S(1)} %slice.15), channel_id=1, source_target_pairs={{3,0},{0,1},{1,2},{2,3},{7,4},{4,5},{5,6},{6,7},{11,8},{8,9},{9,10... | collective-permute-start | bytes 1572872 | tf_op jit(solution)/shard_map/ppermute | solution.py:474
  196.2 23.9 %collective-permute-start.24 = (f32[256,768]{1,0:T(8,128)}, f32[256,768]{1,0:T(8,128)S(1)}, u32[]{:S(2)}, u32[]{:S(2)}) collective-permute-start(f32[256,768]{1,0:T(8,128)} %get-tuple-element.61), channel_id=1, source_target_pairs={{0,16},{16,0},{1,17},{17,1},{2,18},{18,2},{3,19},{19,3},{4,20},{20... | collective-permute-start | bytes 2359304 | tf_op jit(solution)/shard_map/ppermute | solution.py:564
  (23 other events, 145.7 us)
Sparse Core Ops, SparseCore 0:
  9.0 44.5 all-gather.2
  55.4 43.7 all-gather.4

commit v7 on v6

--- a/solution.py
+++ b/solution.py
@@ -537,13 +537,14 @@
     amateur, sums = lax.optimization_barrier((block_of(amateur), sums))
     amateur_after = from_core_offset(amateur, SECOND, 1)
     amateur_before = from_core_offset(amateur, SECOND, 3)
-    expert = block_of(plane_of(expert_rows(request_adapter_index, sums, got, gain, up)))
+    expert = plane_of(expert_rows(request_adapter_index, sums, got, gain, up))
     expert, amateur_after, amateur_before = lax.optimization_barrier(
         (expert, amateur_after, amateur_before)
     )
+    amateur_far = opposite(amateur_after, amateur_before, SECOND)
+    expert, *amateur_far = lax.optimization_barrier((block_of(expert), *amateur_far))
     after = from_core_offset(expert, SECOND, 1)
     before = from_core_offset(expert, SECOND, 3)
-    amateur_far = opposite(amateur_after, amateur_before, SECOND)
     weights = (inverse, vocabulary_head_matrix, head_sib)
     own = [(0, n, (n, 0)) for n in range(4)]
     beside = [(n // 4, n % 4, (n % 4, 1 + 2 * (n // 4))) for n in range(8)]

time: 231 us -> 218 us (0.944)
  waiting for transfers between devices: 83.6 us -> 73.8 us
  local copies, waits for them, and re-layouts: 6.34 us -> 3.43 us
    ppermute x14, waiting for transfers between devices: 29.6 us -> 20.7 us  [from_core_offset(): return lax.ppermute(array, ('c', 'x', 'z'), pairs)]
    ppermute x1, starting transfers between devices: 7.78 us -> 4.49 us  [per_device(): u_sib = lax.ppermute(u_send, 'c', SWAP)]
    slice x2, local copies, waits for them, and re-layouts: 3.21 us -> 0.08 us  [opposite(): before[half:]]
    ppermute x14, starting transfers between devices: 13.6 us -> 16.3 us  [from_core_offset(): return lax.ppermute(array, ('c', 'x', 'z'), pairs)]
  transfers between devices with their start and end apart: 36 -> 36, of which waited for: 25 -> 22; matrix products, arithmetic and copies ran while one was open for 3% -> 2% of each run, Pallas kernels for 22% -> 24%
where the time goes in v7:
time: 218 us; the launch traced here: 217 us
  waiting for transfers between devices  73.8 us (34%)
  Pallas kernels  60.9 us (28%)
  starting transfers between devices  46 us (21%)
  blocking collectives  15.6 us (7%)
  between operations  13.8 us (6%)
  local copies, waits for them, and re-layouts  3.43 us (2%)
  other arithmetic  3.11 us (1%)
    pallas_call x4, Pallas kernels, head_part(): pl.pallas_call(lambda *refs: head_kernel(pieces, first, last, amateur, *r...  41 us
    ppermute x15, waiting for transfers between devices, from_offset(): return lax.ppermute(array, axis, [((i + offset) % 4, i) for i in range(4)])  23.4 us
    ppermute x14, waiting for transfers between devices, from_core_offset(): return lax.ppermute(array, ('c', 'x', 'z'), pairs)  20.7 us
    ppermute x14, starting transfers between devices, from_core_offset(): return lax.ppermute(array, ('c', 'x', 'z'), pairs)  16.3 us
    all_to_all x1, blocking collectives, per_device(): got = lax.all_to_all(sent, TENSOR, split_axis=0, concat_axis=0, tiled=True)  15.6 us
    all_to_all x1, waiting for transfers between devices, per_device(): lax.all_to_all(amateur, TENSOR, split_axis=0, concat_axis=0, tiled=True)  15.1 us
    ppermute x15, starting transfers between devices, from_offset(): return lax.ppermute(array, axis, [((i + offset) % 4, i) for i in range(4)])  11.9 us
    all_to_all x1, waiting for transfers between devices, per_device(): lax.all_to_all(expert, TENSOR, split_axis=0, concat_axis=0, tiled=True)  8.57 us
  transfers between devices with their start and end apart: 36, of which 22 were waited for; matrix products, arithmetic and copies ran while one was open for 2% of the time, Pallas kernels for 24%

profile of v7, /device:TPU:1, one launch (start us, length us, event | category | flops | bytes accessed | tf_op | source)
XLA Modules:
  0.0 216.5 jit_solution(15560098541637964202)
XLA Ops:
  9.5 5.0 %shard_map.127 = bf16[16,16,512]{2,1,0:T(8,128)(2,1)} custom-call(s32[4]{0:T(128)} %len_ref.1, bf16[4,2,8192]{2,1,0:T(2,128)(2,1)} %q_ref.1, bf16[4,2,64,1024]{3,2,1,0:T(8,128)(2,1)} %k_ref.1, bf16[4,2,64,1024]{3,2,1,0:T(8,128)(2,1)} %v_ref.1, bf16[4,2,1024]{2,1,0:T(2,128)(2,1)} %ck_ref.1, bf16[4,2,1024]{2,1,0:T(2,128)(2,1)} %cv_ref.1, ...), custom_call_target="tpu_custom_call" | custom-call | flops 300000000 | bytes 3145728 | tf_op jit(solution)/shard_map/pallas_call | solution.py:80
  14.5 15.6 %all_to_all.15.got_ref = bf16[16,16,512]{2,1,0:T(8,128)(2,1)} all-to-all(bf16[16,16,512]{2,1,0:T(8,128)(2,1)} %shard_map.127), channel_id=1, replica_groups=mesh['y'=4,'c'=2,'x'=4,'z'=4] {'x','z'}, dimensions={0} | all-to-all | bytes 524288 | tf_op jit(solution)/shard_map/all_to_all | solution.py:528
  30.1 6.1 %shard_map.128 = (bf16[16,80,512]{2,1,0:T(8,128)(2,1)}, bf16[16,64,512]{2,1,0:T(8,128)(2,1)}) custom-call(bf16[16,16,512]{2,1,0:T(8,128)(2,1)} %all_to_all.15.got_ref, bf16[512,8192]{1,0:T(8,128)(2,1)} %w_ref.1), custom_call_target="tpu_custom_call" | custom-call | flops 1100000000 | bytes 11534336 | tf_op jit(solution)/shard_map/pallas_call | solution.py:154
  36.2 4.0 %all-to-all-start.1 = ((bf16[16,64,512]{2,1,0:T(8,128)(2,1)}), bf16[16,64,512]{2,1,0:T(8,128)(2,1)S(1)}, u32[]{:S(2)}, u32[]{:S(2)}) async-start(bf16[16,64,512]{2,1,0:T(8,128)(2,1)} %get-tuple-element.37), calls=%async_computation.1 | async-start | bytes 2097152 | tf_op jit(solution)/shard_map/all_to_all | solution.py:530
  40.3 15.1 %all-to-all-done.1.sums_ref = bf16[16,64,512]{2,1,0:T(8,128)(2,1)S(1)} async-done(((bf16[16,64,512]{2,1,0:T(8,128)(2,1)}), bf16[16,64,512]{2,1,0:T(8,128)(2,1)S(1)}, u32[]{:S(2)}, u32[]{:S(2)}) %all-to-all-start.1) | async-done | bytes 1048608 | tf_op jit(solution)/shard_map/all_to_all | solution.py:530
  55.7 3.5 %shard_map.130 = bf16[16,80,512]{2,1,0:T(8,128)(2,1)} custom-call(s32[64]{0:T(128)} %idx_ref.3, bf16[16,16,512]{2,1,0:T(8,128)(2,1)} %all_to_all.15.got_ref, bf16[384,16,512]{2,1,0:T(8,128)(2,1)} %all-gather.3.cloned.1.call-done.table_ref, bf16[16,80,512]{2,1,0:T(8,128)(2,1)} %get-tuple-element.40.partial_ref), custom_call_target="tpu_custom_call", output_to_operand_aliasing={{}: (3, {})} | custom-call | flops 140000000 | bytes 2097152 | tf_op jit(solution)/shard_map/pallas_call | solution.py:200
  59.2 4.7 %all-to-all-start.2 = ((bf16[16,80,512]{2,1,0:T(8,128)(2,1)}), bf16[16,80,512]{2,1,0:T(8,128)(2,1)S(1)}, u32[]{:S(2)}, u32[]{:S(2)}) async-start(bf16[16,80,512]{2,1,0:T(8,128)(2,1)} %shard_map.130), calls=%async_computation.2 | async-start | bytes 2621440 | tf_op jit(solution)/shard_map/all_to_all | solution.py:534
  68.4 3.4 %collective-permute-done.1 = bf16[64,512]{1,0:T(8,128)(2,1)S(1)} collective-permute-done((bf16[64,512]{1,0:T(8,128)(2,1)S(1)}, bf16[64,512]{1,0:T(8,128)(2,1)S(1)}, u32[]{:S(2)}, u32[]{:S(2)}) %collective-permute-start.1) | collective-permute-done | bytes 65568 | tf_op jit(solution)/shard_map/ppermute | solution.py:463
  72.9 8.6 %all-to-all-done.2.sums_ref = bf16[16,80,512]{2,1,0:T(8,128)(2,1)S(1)} async-done(((bf16[16,80,512]{2,1,0:T(8,128)(2,1)}), bf16[16,80,512]{2,1,0:T(8,128)(2,1)S(1)}, u32[]{:S(2)}, u32[]{:S(2)}) %all-to-all-start.2) | async-done | bytes 1310752 | tf_op jit(solution)/shard_map/all_to_all | solution.py:534
  83.6 3.4 %collective-permute-done.3 = bf16[4,64,512]{2,1,0:T(8,128)(2,1)S(1)} collective-permute-done((bf16[4,64,512]{2,1,0:T(8,128)(2,1)S(1)}, bf16[4,64,512]{2,1,0:T(8,128)(2,1)S(1)}, u32[]{:S(2)}, u32[]{:S(2)}) %collective-permute-start.3) | collective-permute-done | bytes 262176 | tf_op jit(solution)/shard_map/ppermute | solution.py:474
  89.5 3.1 %collective-permute-done.5 = bf16[4,64,512]{2,1,0:T(8,128)(2,1)S(1)} collective-permute-done((bf16[4,64,512]{2,1,0:T(8,128)(2,1)S(1)}, bf16[4,64,512]{2,1,0:T(8,128)(2,1)S(1)}, u32[]{:S(2)}, u32[]{:S(2)}) %collective-permute-start.5) | collective-permute-done | bytes 262176 | tf_op jit(solution)/shard_map/ppermute | solution.py:474
  95.5 3.7 %all-gather.5.cloned.1.call-done.table_ref = bf16[384,16,512]{2,1,0:T(8,128)(2,1)} async-done(((bf16[48,16,512]{2,1,0:T(8,128)(2,1)}), bf16[384,16,512]{2,1,0:T(8,128)(2,1)}) %all-gather.5.cloned.1.call-update) | async-done | bytes 6291472 | tf_op jit(solution)/shard_map/all_gather | solution.py:513
  99.2 3.7 %shard_map.131 = bf16[64,512]{1,0:T(8,128)(2,1)} custom-call(s32[64]{0:T(128)} %idx_ref.3, bf16[16,80,512]{2,1,0:T(8,128)(2,1)} %copy-done.3, bf16[16,16,512]{2,1,0:T(8,128)(2,1)} %all_to_all.15.got_ref, bf16[1,512]{1,0:T(2,128)(2,1)} %copy-done.2, bf16[384,16,512]{2,1,0:T(8,128)(2,1)} %all-gather.5.cloned.1.call-done.table_ref), custom_call_target="tpu_custom_call" | custom-call | flops 300000000 | bytes 2097152 | tf_op jit(solution)/shard_map/pallas_call | solution.py:273
  108.4 3.4 %collective-permute-done.8 = bf16[64,512]{1,0:T(8,128)(2,1)S(1)} collective-permute-done((bf16[64,512]{1,0:T(8,128)(2,1)}, bf16[64,512]{1,0:T(8,128)(2,1)S(1)}, u32[]{:S(2)}, u32[]{:S(2)}) %collective-permute-start.8) | collective-permute-done | bytes 65568 | tf_op jit(solution)/shard_map/ppermute | solution.py:463
  119.7 6.1 %collective-permute-done.12 = bf16[4,64,512]{2,1,0:T(8,128)(2,1)S(1)} collective-permute-done((bf16[4,64,512]{2,1,0:T(8,128)(2,1)S(1)}, bf16[4,64,512]{2,1,0:T(8,128)(2,1)S(1)}, u32[]{:S(2)}, u32[]{:S(2)}) %collective-permute-start.12) | collective-permute-done | bytes 262176 | tf_op jit(solution)/shard_map/ppermute | solution.py:474
  125.8 4.8 %collective-permute-done.13 = bf16[4,64,512]{2,1,0:T(8,128)(2,1)S(1)} collective-permute-done((bf16[4,64,512]{2,1,0:T(8,128)(2,1)S(1)}, bf16[4,64,512]{2,1,0:T(8,128)(2,1)S(1)}, u32[]{:S(2)}, u32[]{:S(2)}) %collective-permute-start.13) | collective-permute-done | bytes 262176 | tf_op jit(solution)/shard_map/ppermute | solution.py:474
  135.6 6.2 %shard_map.132 = (f32[256,1536]{1,0:T(8,128)}, f32[256,128]{1,0:T(8,128)}) custom-call(s32[4]{0:T(128)} %pad_add_fusion.refs_0_, f32[1,8192]{1,0:T(1,128)} %bitcast.24, bf16[4,4,64,512]{3,2,1,0:T(8,128)(2,1)} %copy-done.5, bf16[8192,768]{1,0:T(8,128)(2,1)} %refs_4_.3, bf16[8192,768]{1,0:T(8,128)(2,1)} %collective-permute-done.18.refs_4_.refs_8_.refs_5_), custom_call_target="tpu_custom_call" | custom-call | flops 524288 | bytes 131072 | tf_op jit(solution)/shard_map/pallas_call | solution.py:396
  141.7 14.4 %shard_map.133 = (f32[256,1536]{1,0:T(8,128)}, f32[1,256]{1,0:T(1,128)}) custom-call(s32[4]{0:T(128)} %pad_add_fusion.refs_0_, f32[1,8192]{1,0:T(1,128)} %bitcast.25, bf16[4,4,64,512]{3,2,1,0:T(8,128)(2,1)} %copy-done.4, bf16[4,4,64,512]{3,2,1,0:T(8,128)(2,1)} %collective-permute-done.9.refs_3_, bf16[4,4,64,512]{3,2,1,0:T(8,128)(2,1)} %copy-done.6, ...), custom_call_target="tpu_custom_call" | custom-call | flops 2097152 | bytes 524288 | tf_op jit(solution)/shard_map/pallas_call | solution.py:396
  159.2 11.9 %shard_map.134 = (f32[256,1536]{1,0:T(8,128)}, f32[256,128]{1,0:T(8,128)}) custom-call(s32[4]{0:T(128)} %pad_add_fusion.refs_0_, f32[1,8192]{1,0:T(1,128)} %bitcast.26, bf16[4,4,64,512]{3,2,1,0:T(8,128)(2,1)} %copy-done.7, bf16[4,4,64,512]{3,2,1,0:T(8,128)(2,1)} %copy-done.8, bf16[8192,768]{1,0:T(8,128)(2,1)} %refs_4_.3, ...), custom_call_target="tpu_custom_call" | custom-call | flops 1048576 | bytes 262144 | tf_op jit(solution)/shard_map/pallas_call | solution.py:396
  172.1 8.5 %shard_map.135 = (f32[256,768]{1,0:T(8,128)}, f32[256,768]{1,0:T(8,128)}, f32[1,512]{1,0:T(1,128)}) custom-call(s32[4]{0:T(128)} %pad_add_fusion.refs_0_, f32[1,8192]{1,0:T(1,128)} %bitcast.27, bf16[2,4,64,512]{3,2,1,0:T(8,128)(2,1)} %copy-done.11, bf16[2,4,64,512]{3,2,1,0:T(8,128)(2,1)} %copy-done.12, bf16[8192,768]{1,0:T(8,128)(2,1)} %refs_4_.3, ...), custom_call_target="tpu_custom_call" | custom-call | flops 524288 | bytes 131072 | tf_op jit(solution)/shard_map/pallas_call | solution.py:396
  186.6 4.5 %collective-permute-start.24 = (f32[256,768]{1,0:T(8,128)}, f32[256,768]{1,0:T(8,128)S(1)}, u32[]{:S(2)}, u32[]{:S(2)}) collective-permute-start(f32[256,768]{1,0:T(8,128)} %get-tuple-element.67), channel_id=1, source_target_pairs={{0,16},{16,0},{1,17},{17,1},{2,18},{18,2},{3,19},{19,3},{4,20},{20... | collective-permute-start | bytes 2359304 | tf_op jit(solution)/shard_map/ppermute | solution.py:565
  196.4 3.0 %collective-permute-start.28 = (f32[1,512]{1,0:T(1,128)S(1)}, f32[1,512]{1,0:T(1,128)S(1)}, u32[]{:S(2)}, u32[]{:S(2)}) collective-permute-start(f32[1,512]{1,0:T(1,128)S(1)} %log_add_fusion.1), channel_id=1, source_target_pairs={{1,0},{2,1},{3,2},{0,3},{5,4},{6,5},{7,6},{4,7},{9,8},{10,9},{11,1... | collective-permute-start | bytes 6152 | tf_op jit(solution)/shard_map/ppermute | solution.py:463
  200.1 3.2 %collective-permute-done.29 = f32[1,512]{1,0:T(1,128)S(1)} collective-permute-done((f32[1,512]{1,0:T(1,128)S(1)}, f32[1,512]{1,0:T(1,128)S(1)}, u32[]{:S(2)}, u32[]{:S(2)}) %collective-permute-start.29) | collective-permute-done | bytes 2080 | tf_op jit(solution)/shard_map/ppermute | solution.py:463
  203.3 3.0 %collective-permute-start.31 = (f32[1,512]{1,0:T(1,128)S(1)}, f32[1,512]{1,0:T(1,128)S(1)}, u32[]{:S(2)}, u32[]{:S(2)}) collective-permute-start(f32[1,512]{1,0:T(1,128)S(1)} %log_add_fusion.no_ref), channel_id=1, source_target_pairs={{0,16},{16,0},{1,17},{17,1},{2,18},{18,2},{3,19},{19,3},{4,20},{20... | collective-permute-start | bytes 6152 | tf_op jit(solution)/shard_map/ppermute | solution.py:566
  (104 shorter events, 53.9 us)
Async XLA Ops:
  6.5 49.1 %all-gather.3.cloned.1.call-start = ((), (), s32[]{:S(2)}) async-start(), calls=%async_computation.3 | async-start | bytes 7077888 | tf_op jit(solution)/shard_map/all_gather | solution.py:512
  7.3 91.9 %all-gather.5.cloned.1.call-start = ((), (), s32[]{:S(2)}) async-start(), calls=%async_computation.4 | async-start | bytes 7077888 | tf_op jit(solution)/shard_map/all_gather | solution.py:513
  8.0 127.5 %collective-permute-start.18 = (bf16[8192,768]{1,0:T(8,128)(2,1)}, bf16[8192,768]{1,0:T(8,128)(2,1)}, u32[]{:S(2)}, u32[]{:S(2)}) collective-permute-start(bf16[8192,768]{1,0:T(8,128)(2,1)} %refs_4_.3), channel_id=1, source_target_pairs={{0,16},{16,0},{1,17},{17,1},{2,18},{18,2},{3,19},{19,3},{4,20},{20... | collective-permute-start | bytes 37748744 | tf_op jit(solution)/shard_map/ppermute | solution.py:511
  36.2 19.3 %all-to-all-start.1 = ((bf16[16,64,512]{2,1,0:T(8,128)(2,1)}), bf16[16,64,512]{2,1,0:T(8,128)(2,1)S(1)}, u32[]{:S(2)}, u32[]{:S(2)}) async-start(bf16[16,64,512]{2,1,0:T(8,128)(2,1)} %get-tuple-element.37), calls=%async_computation.1 | async-start | bytes 2097152 | tf_op jit(solution)/shard_map/all_to_all | solution.py:530
  59.2 22.3 %all-to-all-start.2 = ((bf16[16,80,512]{2,1,0:T(8,128)(2,1)}), bf16[16,80,512]{2,1,0:T(8,128)(2,1)S(1)}, u32[]{:S(2)}, u32[]{:S(2)}) async-start(bf16[16,80,512]{2,1,0:T(8,128)(2,1)} %shard_map.130), calls=%async_computation.2 | async-start | bytes 2621440 | tf_op jit(solution)/shard_map/all_to_all | solution.py:534
  66.0 5.9 %collective-permute-start.1 = (bf16[64,512]{1,0:T(8,128)(2,1)S(1)}, bf16[64,512]{1,0:T(8,128)(2,1)S(1)}, u32[]{:S(2)}, u32[]{:S(2)}) collective-permute-start(bf16[64,512]{1,0:T(8,128)(2,1)S(1)} %shard_map.129), channel_id=1, source_target_pairs={{64,0},{96,32},{0,64},{32,96},{65,1},{97,33},{1,65},{33,97},{66,2}... | collective-permute-start | bytes 196616 | tf_op jit(solution)/shard_map/ppermute | solution.py:463
  66.3 6.5 %collective-permute-start.2 = (bf16[64,512]{1,0:T(8,128)(2,1)S(1)}, bf16[64,512]{1,0:T(8,128)(2,1)S(1)}, u32[]{:S(2)}, u32[]{:S(2)}) collective-permute-start(bf16[64,512]{1,0:T(8,128)(2,1)S(1)} %shard_map.129), channel_id=1, source_target_pairs={{96,0},{0,32},{32,64},{64,96},{97,1},{1,33},{33,65},{65,97},{98,2}... | collective-permute-start | bytes 196616 | tf_op jit(solution)/shard_map/ppermute | solution.py:463
  81.4 5.6 %collective-permute-start.3 = (bf16[4,64,512]{2,1,0:T(8,128)(2,1)S(1)}, bf16[4,64,512]{2,1,0:T(8,128)(2,1)S(1)}, u32[]{:S(2)}, u32[]{:S(2)}) collective-permute-start(bf16[4,64,512]{2,1,0:T(8,128)(2,1)S(1)} %pad_maximum_fusion.2), channel_id=1, source_target_pairs={{4,0},{5,1},{6,2},{7,3},{8,4},{9,5},{10,6},{11,7},{12,8},{13,9},{1... | collective-permute-start | bytes 786440 | tf_op jit(solution)/shard_map/ppermute | solution.py:474
  82.7 6.8 %collective-permute-start.4 = (bf16[4,64,512]{2,1,0:T(8,128)(2,1)S(1)}, bf16[4,64,512]{2,1,0:T(8,128)(2,1)S(1)}, u32[]{:S(2)}, u32[]{:S(2)}) collective-permute-start(bf16[4,64,512]{2,1,0:T(8,128)(2,1)S(1)} %pad_maximum_fusion.2), channel_id=1, source_target_pairs={{8,0},{9,1},{10,2},{11,3},{12,4},{13,5},{14,6},{15,7},{0,8},{1,9},... | collective-permute-start | bytes 786440 | tf_op jit(solution)/shard_map/ppermute | solution.py:474
  83.6 9.0 %collective-permute-start.5 = (bf16[4,64,512]{2,1,0:T(8,128)(2,1)S(1)}, bf16[4,64,512]{2,1,0:T(8,128)(2,1)S(1)}, u32[]{:S(2)}, u32[]{:S(2)}) collective-permute-start(bf16[4,64,512]{2,1,0:T(8,128)(2,1)S(1)} %pad_maximum_fusion.2), channel_id=1, source_target_pairs={{12,0},{13,1},{14,2},{15,3},{0,4},{1,5},{2,6},{3,7},{4,8},{5,9},{6... | collective-permute-start | bytes 786440 | tf_op jit(solution)/shard_map/ppermute | solution.py:474
  92.8 19.9 %collective-permute-start.10 = (bf16[4,4,64,512]{3,2,1,0:T(8,128)(2,1)S(1)}, bf16[4,4,64,512]{3,2,1,0:T(8,128)(2,1)S(1)}, u32[]{:S(2)}, u32[]{:S(2)}) collective-permute-start(bf16[4,4,64,512]{3,2,1,0:T(8,128)(2,1)S(1)} %pad_maximum_fusion.refs_2_), channel_id=1, source_target_pairs={{3,0},{0,1},{1,2},{2,3},{7,4},{4,5},{5,6},{6,7},{11,8},{8,9},{9,10... | collective-permute-start | bytes 3145736 | tf_op jit(solution)/shard_map/ppermute | solution.py:474
  94.2 18.5 %collective-permute-start.9 = (bf16[4,4,64,512]{3,2,1,0:T(8,128)(2,1)S(1)}, bf16[4,4,64,512]{3,2,1,0:T(8,128)(2,1)}, u32[]{:S(2)}, u32[]{:S(2)}) collective-permute-start(bf16[4,4,64,512]{3,2,1,0:T(8,128)(2,1)S(1)} %pad_maximum_fusion.refs_2_), channel_id=1, source_target_pairs={{1,0},{2,1},{3,2},{0,3},{5,4},{6,5},{7,6},{4,7},{9,8},{10,9},{11,1... | collective-permute-start | bytes 3145736 | tf_op jit(solution)/shard_map/ppermute | solution.py:474
  103.6 4.8 %collective-permute-start.7 = (bf16[64,512]{1,0:T(8,128)(2,1)}, bf16[64,512]{1,0:T(8,128)(2,1)S(1)}, u32[]{:S(2)}, u32[]{:S(2)}) collective-permute-start(bf16[64,512]{1,0:T(8,128)(2,1)} %shard_map.131), channel_id=1, source_target_pairs={{64,0},{96,32},{0,64},{32,96},{65,1},{97,33},{1,65},{33,97},{66,2}... | collective-permute-start | bytes 196616 | tf_op jit(solution)/shard_map/ppermute | solution.py:463
  106.7 5.1 %collective-permute-start.8 = (bf16[64,512]{1,0:T(8,128)(2,1)}, bf16[64,512]{1,0:T(8,128)(2,1)S(1)}, u32[]{:S(2)}, u32[]{:S(2)}) collective-permute-start(bf16[64,512]{1,0:T(8,128)(2,1)} %shard_map.131), channel_id=1, source_target_pairs={{96,0},{0,32},{32,64},{64,96},{97,1},{1,33},{33,65},{65,97},{98,2}... | collective-permute-start | bytes 196616 | tf_op jit(solution)/shard_map/ppermute | solution.py:463
  112.7 6.5 %collective-permute-start.11 = (bf16[4,64,512]{2,1,0:T(8,128)(2,1)S(1)}, bf16[4,64,512]{2,1,0:T(8,128)(2,1)S(1)}, u32[]{:S(2)}, u32[]{:S(2)}) collective-permute-start(bf16[4,64,512]{2,1,0:T(8,128)(2,1)S(1)} %pad_maximum_fusion.3), channel_id=1, source_target_pairs={{4,0},{5,1},{6,2},{7,3},{8,4},{9,5},{10,6},{11,7},{12,8},{13,9},{1... | collective-permute-start | bytes 786440 | tf_op jit(solution)/shard_map/ppermute | solution.py:474
  116.4 14.4 %collective-permute-start.14 = (bf16[2,4,64,512]{3,2,1,0:T(8,128)(2,1)S(1)}, bf16[2,4,64,512]{3,2,1,0:T(8,128)(2,1)S(1)}, u32[]{:S(2)}, u32[]{:S(2)}) collective-permute-start(bf16[2,4,64,512]{3,2,1,0:T(8,128)(2,1)S(1)} %slice.12), channel_id=1, source_target_pairs={{1,0},{2,1},{3,2},{0,3},{5,4},{6,5},{7,6},{4,7},{9,8},{10,9},{11,1... | collective-permute-start | bytes 1572872 | tf_op jit(solution)/shard_map/ppermute | solution.py:474
  118.5 13.2 %collective-permute-start.15 = (bf16[2,4,64,512]{3,2,1,0:T(8,128)(2,1)S(1)}, bf16[2,4,64,512]{3,2,1,0:T(8,128)(2,1)S(1)}, u32[]{:S(2)}, u32[]{:S(2)}) collective-permute-start(bf16[2,4,64,512]{3,2,1,0:T(8,128)(2,1)S(1)} %slice.13), channel_id=1, source_target_pairs={{3,0},{0,1},{1,2},{2,3},{7,4},{4,5},{5,6},{6,7},{11,8},{8,9},{9,10... | collective-permute-start | bytes 1572872 | tf_op jit(solution)/shard_map/ppermute | solution.py:474
  118.6 7.2 %collective-permute-start.12 = (bf16[4,64,512]{2,1,0:T(8,128)(2,1)S(1)}, bf16[4,64,512]{2,1,0:T(8,128)(2,1)S(1)}, u32[]{:S(2)}, u32[]{:S(2)}) collective-permute-start(bf16[4,64,512]{2,1,0:T(8,128)(2,1)S(1)} %pad_maximum_fusion.3), channel_id=1, source_target_pairs={{8,0},{9,1},{10,2},{11,3},{12,4},{13,5},{14,6},{15,7},{0,8},{1,9},... | collective-permute-start | bytes 786440 | tf_op jit(solution)/shard_map/ppermute | solution.py:474
  119.2 11.4 %collective-permute-start.13 = (bf16[4,64,512]{2,1,0:T(8,128)(2,1)S(1)}, bf16[4,64,512]{2,1,0:T(8,128)(2,1)S(1)}, u32[]{:S(2)}, u32[]{:S(2)}) collective-permute-start(bf16[4,64,512]{2,1,0:T(8,128)(2,1)S(1)} %pad_maximum_fusion.3), channel_id=1, source_target_pairs={{12,0},{13,1},{14,2},{15,3},{0,4},{1,5},{2,6},{3,7},{4,8},{5,9},{6... | collective-permute-start | bytes 786440 | tf_op jit(solution)/shard_map/ppermute | solution.py:474
  131.7 24.5 %collective-permute-start.16 = (bf16[4,4,64,512]{3,2,1,0:T(8,128)(2,1)S(1)}, bf16[4,4,64,512]{3,2,1,0:T(8,128)(2,1)S(1)}, u32[]{:S(2)}, u32[]{:S(2)}) collective-permute-start(bf16[4,4,64,512]{3,2,1,0:T(8,128)(2,1)S(1)} %pad_maximum_fusion.1.refs_2_), channel_id=1, source_target_pairs={{1,0},{2,1},{3,2},{0,3},{5,4},{6,5},{7,6},{4,7},{9,8},{10,9},{11,1... | collective-permute-start | bytes 3145736 | tf_op jit(solution)/shard_map/ppermute | solution.py:474
  134.4 21.9 %collective-permute-start.17 = (bf16[4,4,64,512]{3,2,1,0:T(8,128)(2,1)S(1)}, bf16[4,4,64,512]{3,2,1,0:T(8,128)(2,1)S(1)}, u32[]{:S(2)}, u32[]{:S(2)}) collective-permute-start(bf16[4,4,64,512]{3,2,1,0:T(8,128)(2,1)S(1)} %pad_maximum_fusion.1.refs_2_), channel_id=1, source_target_pairs={{3,0},{0,1},{1,2},{2,3},{7,4},{4,5},{5,6},{6,7},{11,8},{8,9},{9,10... | collective-permute-start | bytes 3145736 | tf_op jit(solution)/shard_map/ppermute | solution.py:474
  156.3 14.8 %collective-permute-start.19 = (bf16[2,4,64,512]{3,2,1,0:T(8,128)(2,1)S(1)}, bf16[2,4,64,512]{3,2,1,0:T(8,128)(2,1)S(1)}, u32[]{:S(2)}, u32[]{:S(2)}) collective-permute-start(bf16[2,4,64,512]{3,2,1,0:T(8,128)(2,1)S(1)} %slice.14), channel_id=1, source_target_pairs={{1,0},{2,1},{3,2},{0,3},{5,4},{6,5},{7,6},{4,7},{9,8},{10,9},{11,1... | collective-permute-start | bytes 1572872 | tf_op jit(solution)/shard_map/ppermute | solution.py:474
  159.1 12.0 %collective-permute-start.20 = (bf16[2,4,64,512]{3,2,1,0:T(8,128)(2,1)S(1)}, bf16[2,4,64,512]{3,2,1,0:T(8,128)(2,1)S(1)}, u32[]{:S(2)}, u32[]{:S(2)}) collective-permute-start(bf16[2,4,64,512]{3,2,1,0:T(8,128)(2,1)S(1)} %slice.15), channel_id=1, source_target_pairs={{3,0},{0,1},{1,2},{2,3},{7,4},{4,5},{5,6},{6,7},{11,8},{8,9},{9,10... | collective-permute-start | bytes 1572872 | tf_op jit(solution)/shard_map/ppermute | solution.py:474
  186.6 20.6 %collective-permute-start.24 = (f32[256,768]{1,0:T(8,128)}, f32[256,768]{1,0:T(8,128)S(1)}, u32[]{:S(2)}, u32[]{:S(2)}) collective-permute-start(f32[256,768]{1,0:T(8,128)} %get-tuple-element.67), channel_id=1, source_target_pairs={{0,16},{16,0},{1,17},{17,1},{2,18},{18,2},{3,19},{19,3},{4,20},{20... | collective-permute-start | bytes 2359304 | tf_op jit(solution)/shard_map/ppermute | solution.py:565
  (26 other events, 150.3 us)
Sparse Core Ops, SparseCore 0:
  9.0 44.5 all-gather.2
  55.4 43.7 all-gather.4

commit v8 on v7

--- a/solution.py
+++ b/solution.py
@@ -309,6 +309,9 @@
     else:
         out_ref, squares_ref, x_s, w_s, acc_s, sq_s, x_sem, w_sem, in_sem, q_sem = refs
 
+    if not first:
+        pltpu.make_async_copy(square_ref, sq_s, q_sem).start()
+        pltpu.make_async_copy(sums_ref, acc_s, in_sem).start()
     starts = []
     for n, (which, block, offsets) in enumerate(pieces):
         index = tensor_index(at_ref, *offsets)
@@ -326,8 +329,6 @@
                 w_sem.at[run],
             ).start()
     if not first:
-        pltpu.make_async_copy(sums_ref, acc_s, in_sem).start()
-        pltpu.make_async_copy(square_ref, sq_s, q_sem).start()
         pltpu.make_async_copy(square_ref, sq_s, q_sem).wait()
         pltpu.make_async_copy(sums_ref, acc_s, in_sem).wait()
     else:
@@ -549,14 +550,13 @@
     own = [(0, n, (n, 0)) for n in range(4)]
     beside = [(n // 4, n % 4, (n % 4, 1 + 2 * (n // 4))) for n in range(8)]
     across = [(n // 2, n % 2, (n, 2)) for n in range(4)]
-    partial = head_part(place, [expert], own, *weights)
     pieces = own + [(1 + n, b, o) for n, b, o in beside] + [(3 + n, b, o) for n, b, o in across]
     arrays = [amateur, amateur_after, amateur_before, *amateur_far]
     other = head_part(place, arrays, pieces, *weights, amateur=True)
-    after, before, *rest = lax.optimization_barrier((after, before, *partial, *other))
-    partial, other = rest[:2], rest[2:]
+    after, before, *other = lax.optimization_barrier((after, before, *other))
     far = opposite(after, before, SECOND)
-    partial = head_part(place, [after, before], beside, *weights, sums=partial)
+    pieces = own + [(1 + n, b, o) for n, b, o in beside]
+    partial = head_part(place, [expert, after, before], pieces, *weights)
     u_own, u_send, lse = head_part(place, far, across, *weights, sums=partial, other=other)
     for axis in ("y", "x", "z"):
         lse = combine([lse] + [from_offset(lse, axis, d) for d in range(1, 4)])

time: 218 us -> 211 us (0.968)
  Pallas kernels: 60.9 us -> 53.9 us
    pallas_call x4 -> x3, Pallas kernels: 41 us -> 34 us  [head_part(): pl.pallas_call(lambda *refs: head_kernel(pieces, first, last, amateur, *r...]
  transfers between devices with their start and end apart: 36 -> 36, of which waited for: 22 -> 22; matrix products, arithmetic and copies ran while one was open for 2% -> 2% of each run, Pallas kernels for 24% -> 21%
where the time goes in v8:
time: 211 us; the launch traced here: 210 us
  waiting for transfers between devices  73.8 us (35%)
  Pallas kernels  53.9 us (26%)
  starting transfers between devices  46.1 us (22%)
  blocking collectives  15.6 us (7%)
  between operations  13.8 us (7%)
  local copies, waits for them, and re-layouts  3.43 us (2%)
  other arithmetic  3.21 us (2%)
    pallas_call x3, Pallas kernels, head_part(): pl.pallas_call(lambda *refs: head_kernel(pieces, first, last, amateur, *r...  34 us
    ppermute x15, waiting for transfers between devices, from_offset(): return lax.ppermute(array, axis, [((i + offset) % 4, i) for i in range(4)])  23.4 us
    ppermute x14, waiting for transfers between devices, from_core_offset(): return lax.ppermute(array, ('c', 'x', 'z'), pairs)  20.7 us
    ppermute x14, starting transfers between devices, from_core_offset(): return lax.ppermute(array, ('c', 'x', 'z'), pairs)  16.3 us
    all_to_all x1, blocking collectives, per_device(): got = lax.all_to_all(sent, TENSOR, split_axis=0, concat_axis=0, tiled=True)  15.6 us
    all_to_all x1, waiting for transfers between devices, per_device(): lax.all_to_all(amateur, TENSOR, split_axis=0, concat_axis=0, tiled=True)  15.1 us
    ppermute x15, starting transfers between devices, from_offset(): return lax.ppermute(array, axis, [((i + offset) % 4, i) for i in range(4)])  11.9 us
    all_to_all x1, waiting for transfers between devices, per_device(): lax.all_to_all(expert, TENSOR, split_axis=0, concat_axis=0, tiled=True)  8.6 us
  transfers between devices with their start and end apart: 36, of which 22 were waited for; matrix products, arithmetic and copies ran while one was open for 2% of the time, Pallas kernels for 21%

profile of v8, /device:TPU:1, one launch (start us, length us, event | category | flops | bytes accessed | tf_op | source)
XLA Modules:
  0.0 209.7 jit_solution(17044972565507402045)
XLA Ops:
  9.5 5.0 %shard_map.127 = bf16[16,16,512]{2,1,0:T(8,128)(2,1)} custom-call(s32[4]{0:T(128)} %len_ref.1, bf16[4,2,8192]{2,1,0:T(2,128)(2,1)} %q_ref.1, bf16[4,2,64,1024]{3,2,1,0:T(8,128)(2,1)} %k_ref.1, bf16[4,2,64,1024]{3,2,1,0:T(8,128)(2,1)} %v_ref.1, bf16[4,2,1024]{2,1,0:T(2,128)(2,1)} %ck_ref.1, bf16[4,2,1024]{2,1,0:T(2,128)(2,1)} %cv_ref.1, ...), custom_call_target="tpu_custom_call" | custom-call | flops 300000000 | bytes 3145728 | tf_op jit(solution)/shard_map/pallas_call | solution.py:80
  14.5 15.6 %all_to_all.15.got_ref = bf16[16,16,512]{2,1,0:T(8,128)(2,1)} all-to-all(bf16[16,16,512]{2,1,0:T(8,128)(2,1)} %shard_map.127), channel_id=1, replica_groups=mesh['y'=4,'c'=2,'x'=4,'z'=4] {'x','z'}, dimensions={0} | all-to-all | bytes 524288 | tf_op jit(solution)/shard_map/all_to_all | solution.py:529
  30.1 6.1 %shard_map.128 = (bf16[16,80,512]{2,1,0:T(8,128)(2,1)}, bf16[16,64,512]{2,1,0:T(8,128)(2,1)}) custom-call(bf16[16,16,512]{2,1,0:T(8,128)(2,1)} %all_to_all.15.got_ref, bf16[512,8192]{1,0:T(8,128)(2,1)} %w_ref.1), custom_call_target="tpu_custom_call" | custom-call | flops 1100000000 | bytes 11534336 | tf_op jit(solution)/shard_map/pallas_call | solution.py:154
  36.2 4.0 %all-to-all-start.1 = ((bf16[16,64,512]{2,1,0:T(8,128)(2,1)}), bf16[16,64,512]{2,1,0:T(8,128)(2,1)S(1)}, u32[]{:S(2)}, u32[]{:S(2)}) async-start(bf16[16,64,512]{2,1,0:T(8,128)(2,1)} %get-tuple-element.33), calls=%async_computation.1 | async-start | bytes 2097152 | tf_op jit(solution)/shard_map/all_to_all | solution.py:531
  40.3 15.1 %all-to-all-done.1.sums_ref = bf16[16,64,512]{2,1,0:T(8,128)(2,1)S(1)} async-done(((bf16[16,64,512]{2,1,0:T(8,128)(2,1)}), bf16[16,64,512]{2,1,0:T(8,128)(2,1)S(1)}, u32[]{:S(2)}, u32[]{:S(2)}) %all-to-all-start.1) | async-done | bytes 1048608 | tf_op jit(solution)/shard_map/all_to_all | solution.py:531
  55.7 3.5 %shard_map.130 = bf16[16,80,512]{2,1,0:T(8,128)(2,1)} custom-call(s32[64]{0:T(128)} %idx_ref.3, bf16[16,16,512]{2,1,0:T(8,128)(2,1)} %all_to_all.15.got_ref, bf16[384,16,512]{2,1,0:T(8,128)(2,1)} %all-gather.3.cloned.1.call-done.table_ref, bf16[16,80,512]{2,1,0:T(8,128)(2,1)} %get-tuple-element.36.partial_ref), custom_call_target="tpu_custom_call", output_to_operand_aliasing={{}: (3, {})} | custom-call | flops 140000000 | bytes 2097152 | tf_op jit(solution)/shard_map/pallas_call | solution.py:200
  59.2 4.7 %all-to-all-start.2 = ((bf16[16,80,512]{2,1,0:T(8,128)(2,1)}), bf16[16,80,512]{2,1,0:T(8,128)(2,1)S(1)}, u32[]{:S(2)}, u32[]{:S(2)}) async-start(bf16[16,80,512]{2,1,0:T(8,128)(2,1)} %shard_map.130), calls=%async_computation.2 | async-start | bytes 2621440 | tf_op jit(solution)/shard_map/all_to_all | solution.py:535
  68.4 3.5 %collective-permute-done.1 = bf16[64,512]{1,0:T(8,128)(2,1)S(1)} collective-permute-done((bf16[64,512]{1,0:T(8,128)(2,1)S(1)}, bf16[64,512]{1,0:T(8,128)(2,1)S(1)}, u32[]{:S(2)}, u32[]{:S(2)}) %collective-permute-start.1) | collective-permute-done | bytes 65568 | tf_op jit(solution)/shard_map/ppermute | solution.py:464
  72.9 8.6 %all-to-all-done.2.sums_ref = bf16[16,80,512]{2,1,0:T(8,128)(2,1)S(1)} async-done(((bf16[16,80,512]{2,1,0:T(8,128)(2,1)}), bf16[16,80,512]{2,1,0:T(8,128)(2,1)S(1)}, u32[]{:S(2)}, u32[]{:S(2)}) %all-to-all-start.2) | async-done | bytes 1310752 | tf_op jit(solution)/shard_map/all_to_all | solution.py:535
  83.7 3.4 %collective-permute-done.3 = bf16[4,64,512]{2,1,0:T(8,128)(2,1)S(1)} collective-permute-done((bf16[4,64,512]{2,1,0:T(8,128)(2,1)S(1)}, bf16[4,64,512]{2,1,0:T(8,128)(2,1)S(1)}, u32[]{:S(2)}, u32[]{:S(2)}) %collective-permute-start.3) | collective-permute-done | bytes 262176 | tf_op jit(solution)/shard_map/ppermute | solution.py:475
  89.5 3.1 %collective-permute-done.5 = bf16[4,64,512]{2,1,0:T(8,128)(2,1)S(1)} collective-permute-done((bf16[4,64,512]{2,1,0:T(8,128)(2,1)S(1)}, bf16[4,64,512]{2,1,0:T(8,128)(2,1)S(1)}, u32[]{:S(2)}, u32[]{:S(2)}) %collective-permute-start.5) | collective-permute-done | bytes 262176 | tf_op jit(solution)/shard_map/ppermute | solution.py:475
  95.5 3.7 %all-gather.5.cloned.1.call-done.table_ref = bf16[384,16,512]{2,1,0:T(8,128)(2,1)} async-done(((bf16[48,16,512]{2,1,0:T(8,128)(2,1)}), bf16[384,16,512]{2,1,0:T(8,128)(2,1)}) %all-gather.5.cloned.1.call-update) | async-done | bytes 6291472 | tf_op jit(solution)/shard_map/all_gather | solution.py:514
  99.2 3.7 %shard_map.131 = bf16[64,512]{1,0:T(8,128)(2,1)} custom-call(s32[64]{0:T(128)} %idx_ref.3, bf16[16,80,512]{2,1,0:T(8,128)(2,1)} %copy-done.3, bf16[16,16,512]{2,1,0:T(8,128)(2,1)} %all_to_all.15.got_ref, bf16[1,512]{1,0:T(2,128)(2,1)} %copy-done.2, bf16[384,16,512]{2,1,0:T(8,128)(2,1)} %all-gather.5.cloned.1.call-done.table_ref), custom_call_target="tpu_custom_call" | custom-call | flops 300000000 | bytes 2097152 | tf_op jit(solution)/shard_map/pallas_call | solution.py:273
  108.4 3.4 %collective-permute-done.8 = bf16[64,512]{1,0:T(8,128)(2,1)S(1)} collective-permute-done((bf16[64,512]{1,0:T(8,128)(2,1)}, bf16[64,512]{1,0:T(8,128)(2,1)S(1)}, u32[]{:S(2)}, u32[]{:S(2)}) %collective-permute-start.8) | collective-permute-done | bytes 65568 | tf_op jit(solution)/shard_map/ppermute | solution.py:464
  119.7 6.0 %collective-permute-done.12 = bf16[4,64,512]{2,1,0:T(8,128)(2,1)S(1)} collective-permute-done((bf16[4,64,512]{2,1,0:T(8,128)(2,1)S(1)}, bf16[4,64,512]{2,1,0:T(8,128)(2,1)S(1)}, u32[]{:S(2)}, u32[]{:S(2)}) %collective-permute-start.12) | collective-permute-done | bytes 262176 | tf_op jit(solution)/shard_map/ppermute | solution.py:475
  125.8 4.8 %collective-permute-done.13 = bf16[4,64,512]{2,1,0:T(8,128)(2,1)S(1)} collective-permute-done((bf16[4,64,512]{2,1,0:T(8,128)(2,1)S(1)}, bf16[4,64,512]{2,1,0:T(8,128)(2,1)S(1)}, u32[]{:S(2)}, u32[]{:S(2)}) %collective-permute-start.13) | collective-permute-done | bytes 262176 | tf_op jit(solution)/shard_map/ppermute | solution.py:475
  135.6 14.5 %shard_map.132 = (f32[256,1536]{1,0:T(8,128)}, f32[1,256]{1,0:T(1,128)}) custom-call(s32[4]{0:T(128)} %pad_add_fusion.refs_0_, f32[1,8192]{1,0:T(1,128)} %bitcast.24, bf16[4,4,64,512]{3,2,1,0:T(8,128)(2,1)} %copy-done.4, bf16[4,4,64,512]{3,2,1,0:T(8,128)(2,1)} %collective-permute-done.9.refs_3_, bf16[4,4,64,512]{3,2,1,0:T(8,128)(2,1)} %copy-done.6, ...), custom_call_target="tpu_custom_call" | custom-call | flops 2097152 | bytes 524288 | tf_op jit(solution)/shard_map/pallas_call | solution.py:397
  153.1 11.2 %shard_map.133 = (f32[256,1536]{1,0:T(8,128)}, f32[256,128]{1,0:T(8,128)}) custom-call(s32[4]{0:T(128)} %pad_add_fusion.refs_0_, f32[1,8192]{1,0:T(1,128)} %bitcast.25, bf16[4,4,64,512]{3,2,1,0:T(8,128)(2,1)} %copy-done.5, bf16[4,4,64,512]{3,2,1,0:T(8,128)(2,1)} %copy-done.7, bf16[4,4,64,512]{3,2,1,0:T(8,128)(2,1)} %copy-done.8, bf16[8192,768]{1,0:T(8,128)(2,1)} %refs_4_.1, ...), custom_call_target="tpu_custom_call" | custom-call | flops 1572864 | bytes 393216 | tf_op jit(solution)/shard_map/pallas_call | solution.py:397
  165.3 8.3 %shard_map.134 = (f32[256,768]{1,0:T(8,128)}, f32[256,768]{1,0:T(8,128)}, f32[1,512]{1,0:T(1,128)}) custom-call(s32[4]{0:T(128)} %pad_add_fusion.refs_0_, f32[1,8192]{1,0:T(1,128)} %bitcast.26, bf16[2,4,64,512]{3,2,1,0:T(8,128)(2,1)} %copy-done.11, bf16[2,4,64,512]{3,2,1,0:T(8,128)(2,1)} %copy-done.12, bf16[8192,768]{1,0:T(8,128)(2,1)} %refs_4_.1, ...), custom_call_target="tpu_custom_call" | custom-call | flops 524288 | bytes 131072 | tf_op jit(solution)/shard_map/pallas_call | solution.py:397
  179.6 4.5 %collective-permute-start.24 = (f32[256,768]{1,0:T(8,128)}, f32[256,768]{1,0:T(8,128)S(1)}, u32[]{:S(2)}, u32[]{:S(2)}) collective-permute-start(f32[256,768]{1,0:T(8,128)} %get-tuple-element.59), channel_id=1, source_target_pairs={{0,16},{16,0},{1,17},{17,1},{2,18},{18,2},{3,19},{19,3},{4,20},{20... | collective-permute-start | bytes 2359304 | tf_op jit(solution)/shard_map/ppermute | solution.py:565
  186.6 2.8 %collective-permute-done.26 = f32[1,512]{1,0:T(1,128)S(1)} collective-permute-done((f32[1,512]{1,0:T(1,128)S(1)}, f32[1,512]{1,0:T(1,128)S(1)}, u32[]{:S(2)}, u32[]{:S(2)}) %collective-permute-start.26) | collective-permute-done | bytes 2080 | tf_op jit(solution)/shard_map/ppermute | solution.py:464
  189.5 3.0 %collective-permute-start.28 = (f32[1,512]{1,0:T(1,128)S(1)}, f32[1,512]{1,0:T(1,128)S(1)}, u32[]{:S(2)}, u32[]{:S(2)}) collective-permute-start(f32[1,512]{1,0:T(1,128)S(1)} %log_add_fusion.1), channel_id=1, source_target_pairs={{1,0},{2,1},{3,2},{0,3},{5,4},{6,5},{7,6},{4,7},{9,8},{10,9},{11,1... | collective-permute-start | bytes 6152 | tf_op jit(solution)/shard_map/ppermute | solution.py:464
  193.3 3.2 %collective-permute-done.29 = f32[1,512]{1,0:T(1,128)S(1)} collective-permute-done((f32[1,512]{1,0:T(1,128)S(1)}, f32[1,512]{1,0:T(1,128)S(1)}, u32[]{:S(2)}, u32[]{:S(2)}) %collective-permute-start.29) | collective-permute-done | bytes 2080 | tf_op jit(solution)/shard_map/ppermute | solution.py:464
  196.5 3.0 %collective-permute-start.31 = (f32[1,512]{1,0:T(1,128)S(1)}, f32[1,512]{1,0:T(1,128)S(1)}, u32[]{:S(2)}, u32[]{:S(2)}) collective-permute-start(f32[1,512]{1,0:T(1,128)S(1)} %log_add_fusion.no_ref), channel_id=1, source_target_pairs={{0,16},{16,0},{1,17},{17,1},{2,18},{18,2},{3,19},{19,3},{4,20},{20... | collective-permute-start | bytes 6152 | tf_op jit(solution)/shard_map/ppermute | solution.py:566
  (103 shorter events, 51.1 us)
Async XLA Ops:
  6.5 49.1 %all-gather.3.cloned.1.call-start = ((), (), s32[]{:S(2)}) async-start(), calls=%async_computation.3 | async-start | bytes 7077888 | tf_op jit(solution)/shard_map/all_gather | solution.py:513
  7.3 91.9 %all-gather.5.cloned.1.call-start = ((), (), s32[]{:S(2)}) async-start(), calls=%async_computation.4 | async-start | bytes 7077888 | tf_op jit(solution)/shard_map/all_gather | solution.py:514
  8.0 127.6 %collective-permute-start.18 = (bf16[8192,768]{1,0:T(8,128)(2,1)}, bf16[8192,768]{1,0:T(8,128)(2,1)}, u32[]{:S(2)}, u32[]{:S(2)}) collective-permute-start(bf16[8192,768]{1,0:T(8,128)(2,1)} %refs_4_.1), channel_id=1, source_target_pairs={{0,16},{16,0},{1,17},{17,1},{2,18},{18,2},{3,19},{19,3},{4,20},{20... | collective-permute-start | bytes 37748744 | tf_op jit(solution)/shard_map/ppermute | solution.py:512
  36.2 19.3 %all-to-all-start.1 = ((bf16[16,64,512]{2,1,0:T(8,128)(2,1)}), bf16[16,64,512]{2,1,0:T(8,128)(2,1)S(1)}, u32[]{:S(2)}, u32[]{:S(2)}) async-start(bf16[16,64,512]{2,1,0:T(8,128)(2,1)} %get-tuple-element.33), calls=%async_computation.1 | async-start | bytes 2097152 | tf_op jit(solution)/shard_map/all_to_all | solution.py:531
  59.2 22.3 %all-to-all-start.2 = ((bf16[16,80,512]{2,1,0:T(8,128)(2,1)}), bf16[16,80,512]{2,1,0:T(8,128)(2,1)S(1)}, u32[]{:S(2)}, u32[]{:S(2)}) async-start(bf16[16,80,512]{2,1,0:T(8,128)(2,1)} %shard_map.130), calls=%async_computation.2 | async-start | bytes 2621440 | tf_op jit(solution)/shard_map/all_to_all | solution.py:535
  66.0 5.9 %collective-permute-start.1 = (bf16[64,512]{1,0:T(8,128)(2,1)S(1)}, bf16[64,512]{1,0:T(8,128)(2,1)S(1)}, u32[]{:S(2)}, u32[]{:S(2)}) collective-permute-start(bf16[64,512]{1,0:T(8,128)(2,1)S(1)} %shard_map.129), channel_id=1, source_target_pairs={{64,0},{96,32},{0,64},{32,96},{65,1},{97,33},{1,65},{33,97},{66,2}... | collective-permute-start | bytes 196616 | tf_op jit(solution)/shard_map/ppermute | solution.py:464
  66.3 6.5 %collective-permute-start.2 = (bf16[64,512]{1,0:T(8,128)(2,1)S(1)}, bf16[64,512]{1,0:T(8,128)(2,1)S(1)}, u32[]{:S(2)}, u32[]{:S(2)}) collective-permute-start(bf16[64,512]{1,0:T(8,128)(2,1)S(1)} %shard_map.129), channel_id=1, source_target_pairs={{96,0},{0,32},{32,64},{64,96},{97,1},{1,33},{33,65},{65,97},{98,2}... | collective-permute-start | bytes 196616 | tf_op jit(solution)/shard_map/ppermute | solution.py:464
  81.5 5.6 %collective-permute-start.3 = (bf16[4,64,512]{2,1,0:T(8,128)(2,1)S(1)}, bf16[4,64,512]{2,1,0:T(8,128)(2,1)S(1)}, u32[]{:S(2)}, u32[]{:S(2)}) collective-permute-start(bf16[4,64,512]{2,1,0:T(8,128)(2,1)S(1)} %pad_maximum_fusion.2), channel_id=1, source_target_pairs={{4,0},{5,1},{6,2},{7,3},{8,4},{9,5},{10,6},{11,7},{12,8},{13,9},{1... | collective-permute-start | bytes 786440 | tf_op jit(solution)/shard_map/ppermute | solution.py:475
  82.7 6.8 %collective-permute-start.4 = (bf16[4,64,512]{2,1,0:T(8,128)(2,1)S(1)}, bf16[4,64,512]{2,1,0:T(8,128)(2,1)S(1)}, u32[]{:S(2)}, u32[]{:S(2)}) collective-permute-start(bf16[4,64,512]{2,1,0:T(8,128)(2,1)S(1)} %pad_maximum_fusion.2), channel_id=1, source_target_pairs={{8,0},{9,1},{10,2},{11,3},{12,4},{13,5},{14,6},{15,7},{0,8},{1,9},... | collective-permute-start | bytes 786440 | tf_op jit(solution)/shard_map/ppermute | solution.py:475
  83.6 8.9 %collective-permute-start.5 = (bf16[4,64,512]{2,1,0:T(8,128)(2,1)S(1)}, bf16[4,64,512]{2,1,0:T(8,128)(2,1)S(1)}, u32[]{:S(2)}, u32[]{:S(2)}) collective-permute-start(bf16[4,64,512]{2,1,0:T(8,128)(2,1)S(1)} %pad_maximum_fusion.2), channel_id=1, source_target_pairs={{12,0},{13,1},{14,2},{15,3},{0,4},{1,5},{2,6},{3,7},{4,8},{5,9},{6... | collective-permute-start | bytes 786440 | tf_op jit(solution)/shard_map/ppermute | solution.py:475
  92.7 19.9 %collective-permute-start.10 = (bf16[4,4,64,512]{3,2,1,0:T(8,128)(2,1)S(1)}, bf16[4,4,64,512]{3,2,1,0:T(8,128)(2,1)S(1)}, u32[]{:S(2)}, u32[]{:S(2)}) collective-permute-start(bf16[4,4,64,512]{3,2,1,0:T(8,128)(2,1)S(1)} %pad_maximum_fusion.refs_2_), channel_id=1, source_target_pairs={{3,0},{0,1},{1,2},{2,3},{7,4},{4,5},{5,6},{6,7},{11,8},{8,9},{9,10... | collective-permute-start | bytes 3145736 | tf_op jit(solution)/shard_map/ppermute | solution.py:475
  94.2 18.5 %collective-permute-start.9 = (bf16[4,4,64,512]{3,2,1,0:T(8,128)(2,1)S(1)}, bf16[4,4,64,512]{3,2,1,0:T(8,128)(2,1)}, u32[]{:S(2)}, u32[]{:S(2)}) collective-permute-start(bf16[4,4,64,512]{3,2,1,0:T(8,128)(2,1)S(1)} %pad_maximum_fusion.refs_2_), channel_id=1, source_target_pairs={{1,0},{2,1},{3,2},{0,3},{5,4},{6,5},{7,6},{4,7},{9,8},{10,9},{11,1... | collective-permute-start | bytes 3145736 | tf_op jit(solution)/shard_map/ppermute | solution.py:475
  103.5 4.8 %collective-permute-start.7 = (bf16[64,512]{1,0:T(8,128)(2,1)}, bf16[64,512]{1,0:T(8,128)(2,1)S(1)}, u32[]{:S(2)}, u32[]{:S(2)}) collective-permute-start(bf16[64,512]{1,0:T(8,128)(2,1)} %shard_map.131), channel_id=1, source_target_pairs={{64,0},{96,32},{0,64},{32,96},{65,1},{97,33},{1,65},{33,97},{66,2}... | collective-permute-start | bytes 196616 | tf_op jit(solution)/shard_map/ppermute | solution.py:464
  106.7 5.0 %collective-permute-start.8 = (bf16[64,512]{1,0:T(8,128)(2,1)}, bf16[64,512]{1,0:T(8,128)(2,1)S(1)}, u32[]{:S(2)}, u32[]{:S(2)}) collective-permute-start(bf16[64,512]{1,0:T(8,128)(2,1)} %shard_map.131), channel_id=1, source_target_pairs={{96,0},{0,32},{32,64},{64,96},{97,1},{1,33},{33,65},{65,97},{98,2}... | collective-permute-start | bytes 196616 | tf_op jit(solution)/shard_map/ppermute | solution.py:464
  112.7 6.5 %collective-permute-start.11 = (bf16[4,64,512]{2,1,0:T(8,128)(2,1)S(1)}, bf16[4,64,512]{2,1,0:T(8,128)(2,1)S(1)}, u32[]{:S(2)}, u32[]{:S(2)}) collective-permute-start(bf16[4,64,512]{2,1,0:T(8,128)(2,1)S(1)} %pad_maximum_fusion.3), channel_id=1, source_target_pairs={{4,0},{5,1},{6,2},{7,3},{8,4},{9,5},{10,6},{11,7},{12,8},{13,9},{1... | collective-permute-start | bytes 786440 | tf_op jit(solution)/shard_map/ppermute | solution.py:475
  116.4 14.4 %collective-permute-start.14 = (bf16[2,4,64,512]{3,2,1,0:T(8,128)(2,1)S(1)}, bf16[2,4,64,512]{3,2,1,0:T(8,128)(2,1)S(1)}, u32[]{:S(2)}, u32[]{:S(2)}) collective-permute-start(bf16[2,4,64,512]{3,2,1,0:T(8,128)(2,1)S(1)} %slice.12), channel_id=1, source_target_pairs={{1,0},{2,1},{3,2},{0,3},{5,4},{6,5},{7,6},{4,7},{9,8},{10,9},{11,1... | collective-permute-start | bytes 1572872 | tf_op jit(solution)/shard_map/ppermute | solution.py:475
  118.5 13.2 %collective-permute-start.15 = (bf16[2,4,64,512]{3,2,1,0:T(8,128)(2,1)S(1)}, bf16[2,4,64,512]{3,2,1,0:T(8,128)(2,1)S(1)}, u32[]{:S(2)}, u32[]{:S(2)}) collective-permute-start(bf16[2,4,64,512]{3,2,1,0:T(8,128)(2,1)S(1)} %slice.13), channel_id=1, source_target_pairs={{3,0},{0,1},{1,2},{2,3},{7,4},{4,5},{5,6},{6,7},{11,8},{8,9},{9,10... | collective-permute-start | bytes 1572872 | tf_op jit(solution)/shard_map/ppermute | solution.py:475
  118.6 7.2 %collective-permute-start.12 = (bf16[4,64,512]{2,1,0:T(8,128)(2,1)S(1)}, bf16[4,64,512]{2,1,0:T(8,128)(2,1)S(1)}, u32[]{:S(2)}, u32[]{:S(2)}) collective-permute-start(bf16[4,64,512]{2,1,0:T(8,128)(2,1)S(1)} %pad_maximum_fusion.3), channel_id=1, source_target_pairs={{8,0},{9,1},{10,2},{11,3},{12,4},{13,5},{14,6},{15,7},{0,8},{1,9},... | collective-permute-start | bytes 786440 | tf_op jit(solution)/shard_map/ppermute | solution.py:475
  119.2 11.4 %collective-permute-start.13 = (bf16[4,64,512]{2,1,0:T(8,128)(2,1)S(1)}, bf16[4,64,512]{2,1,0:T(8,128)(2,1)S(1)}, u32[]{:S(2)}, u32[]{:S(2)}) collective-permute-start(bf16[4,64,512]{2,1,0:T(8,128)(2,1)S(1)} %pad_maximum_fusion.3), channel_id=1, source_target_pairs={{12,0},{13,1},{14,2},{15,3},{0,4},{1,5},{2,6},{3,7},{4,8},{5,9},{6... | collective-permute-start | bytes 786440 | tf_op jit(solution)/shard_map/ppermute | solution.py:475
  131.7 18.4 %collective-permute-start.16 = (bf16[4,4,64,512]{3,2,1,0:T(8,128)(2,1)S(1)}, bf16[4,4,64,512]{3,2,1,0:T(8,128)(2,1)S(1)}, u32[]{:S(2)}, u32[]{:S(2)}) collective-permute-start(bf16[4,4,64,512]{3,2,1,0:T(8,128)(2,1)S(1)} %pad_maximum_fusion.1.refs_2_), channel_id=1, source_target_pairs={{1,0},{2,1},{3,2},{0,3},{5,4},{6,5},{7,6},{4,7},{9,8},{10,9},{11,1... | collective-permute-start | bytes 3145736 | tf_op jit(solution)/shard_map/ppermute | solution.py:475
  134.3 15.8 %collective-permute-start.17 = (bf16[4,4,64,512]{3,2,1,0:T(8,128)(2,1)S(1)}, bf16[4,4,64,512]{3,2,1,0:T(8,128)(2,1)S(1)}, u32[]{:S(2)}, u32[]{:S(2)}) collective-permute-start(bf16[4,4,64,512]{3,2,1,0:T(8,128)(2,1)S(1)} %pad_maximum_fusion.1.refs_2_), channel_id=1, source_target_pairs={{3,0},{0,1},{1,2},{2,3},{7,4},{4,5},{5,6},{6,7},{11,8},{8,9},{9,10... | collective-permute-start | bytes 3145736 | tf_op jit(solution)/shard_map/ppermute | solution.py:475
  150.2 14.1 %collective-permute-start.19 = (bf16[2,4,64,512]{3,2,1,0:T(8,128)(2,1)S(1)}, bf16[2,4,64,512]{3,2,1,0:T(8,128)(2,1)S(1)}, u32[]{:S(2)}, u32[]{:S(2)}) collective-permute-start(bf16[2,4,64,512]{3,2,1,0:T(8,128)(2,1)S(1)} %slice.14), channel_id=1, source_target_pairs={{1,0},{2,1},{3,2},{0,3},{5,4},{6,5},{7,6},{4,7},{9,8},{10,9},{11,1... | collective-permute-start | bytes 1572872 | tf_op jit(solution)/shard_map/ppermute | solution.py:475
  153.0 11.4 %collective-permute-start.20 = (bf16[2,4,64,512]{3,2,1,0:T(8,128)(2,1)S(1)}, bf16[2,4,64,512]{3,2,1,0:T(8,128)(2,1)S(1)}, u32[]{:S(2)}, u32[]{:S(2)}) collective-permute-start(bf16[2,4,64,512]{3,2,1,0:T(8,128)(2,1)S(1)} %slice.15), channel_id=1, source_target_pairs={{3,0},{0,1},{1,2},{2,3},{7,4},{4,5},{5,6},{6,7},{11,8},{8,9},{9,10... | collective-permute-start | bytes 1572872 | tf_op jit(solution)/shard_map/ppermute | solution.py:475
  179.6 20.7 %collective-permute-start.24 = (f32[256,768]{1,0:T(8,128)}, f32[256,768]{1,0:T(8,128)S(1)}, u32[]{:S(2)}, u32[]{:S(2)}) collective-permute-start(f32[256,768]{1,0:T(8,128)} %get-tuple-element.59), channel_id=1, source_target_pairs={{0,16},{16,0},{1,17},{17,1},{2,18},{18,2},{3,19},{19,3},{4,20},{20... | collective-permute-start | bytes 2359304 | tf_op jit(solution)/shard_map/ppermute | solution.py:565
  (26 other events, 164.8 us)
Sparse Core Ops, SparseCore 0:
  9.0 44.5 all-gather.2
  55.4 43.7 all-gather.4

commit v9 on v8

--- a/solution.py
+++ b/solution.py
@@ -530,7 +530,6 @@
     expert, amateur = projection(got, output_projection_weight)
     amateur = lax.all_to_all(amateur, TENSOR, split_axis=0, concat_axis=0, tiled=True)
     amateur = amateur_rows(amateur, got, gain)
-    amateur, got = lax.optimization_barrier((amateur, got))
     expert = with_rank_sums(request_adapter_index, got, down, expert)
     sums = lax.all_to_all(expert, TENSOR, split_axis=0, concat_axis=0, tiled=True)
     amateur, _ = lax.optimization_barrier((amateur, expert))

time: 211 us -> 212 us (level)
    all_to_all x1, waiting for transfers between devices: 15.1 us -> 0.01 us  [per_device(): lax.all_to_all(amateur, TENSOR, split_axis=0, concat_axis=0, tiled=True)]
    all_gather x1, waiting for transfers between devices: 0.02 us -> 13.6 us  [per_device(): down = lax.all_gather(lowrank_down_factors, ('y', 'c'), axis=0, tiled=True)]
    all_to_all x1, starting transfers between devices: 4.67 us -> 6.81 us  [per_device(): lax.all_to_all(expert, TENSOR, split_axis=0, concat_axis=0, tiled=True)]
  transfers between devices with their start and end apart: 36 -> 36, of which waited for: 22 -> 23; matrix products, arithmetic and copies ran while one was open for 2% -> 2% of each run, Pallas kernels for 21% -> 21%
where the time goes in v9:
time: 212 us; the launch traced here: 211 us
  waiting for transfers between devices  73.8 us (35%)
  Pallas kernels  53.9 us (25%)
  starting transfers between devices  47 us (22%)
  blocking collectives  15.6 us (7%)
  between operations  13.8 us (7%)
  local copies, waits for them, and re-layouts  3.43 us (2%)
  other arithmetic  3.21 us (2%)
    pallas_call x3, Pallas kernels, head_part(): pl.pallas_call(lambda *refs: head_kernel(pieces, first, last, amateur, *r...  34 us
    ppermute x15, waiting for transfers between devices, from_offset(): return lax.ppermute(array, axis, [((i + offset) % 4, i) for i in range(4)])  24.9 us
    ppermute x14, waiting for transfers between devices, from_core_offset(): return lax.ppermute(array, ('c', 'x', 'z'), pairs)  20.8 us
    ppermute x14, starting transfers between devices, from_core_offset(): return lax.ppermute(array, ('c', 'x', 'z'), pairs)  15.8 us
    all_to_all x1, blocking collectives, per_device(): got = lax.all_to_all(sent, TENSOR, split_axis=0, concat_axis=0, tiled=True)  15.6 us
    all_gather x1, waiting for transfers between devices, per_device(): down = lax.all_gather(lowrank_down_factors, ('y', 'c'), axis=0, tiled=True)  13.6 us
    ppermute x15, starting transfers between devices, from_offset(): return lax.ppermute(array, axis, [((i + offset) % 4, i) for i in range(4)])  11.1 us
    all_to_all x1, waiting for transfers between devices, per_device(): lax.all_to_all(expert, TENSOR, split_axis=0, concat_axis=0, tiled=True)  9.78 us
  transfers between devices with their start and end apart: 36, of which 23 were waited for; matrix products, arithmetic and copies ran while one was open for 2% of the time, Pallas kernels for 21%

profile of v9, /device:TPU:1, one launch (start us, length us, event | category | flops | bytes accessed | tf_op | source)
XLA Modules:
  0.0 210.6 jit_solution(10326407004651893260)
XLA Ops:
  9.5 5.0 %shard_map.127 = bf16[16,16,512]{2,1,0:T(8,128)(2,1)} custom-call(s32[4]{0:T(128)} %len_ref.1, bf16[4,2,8192]{2,1,0:T(2,128)(2,1)} %q_ref.1, bf16[4,2,64,1024]{3,2,1,0:T(8,128)(2,1)} %k_ref.1, bf16[4,2,64,1024]{3,2,1,0:T(8,128)(2,1)} %v_ref.1, bf16[4,2,1024]{2,1,0:T(2,128)(2,1)} %ck_ref.1, bf16[4,2,1024]{2,1,0:T(2,128)(2,1)} %cv_ref.1, ...), custom_call_target="tpu_custom_call" | custom-call | flops 300000000 | bytes 3145728 | tf_op jit(solution)/shard_map/pallas_call | solution.py:80
  14.5 15.6 %all_to_all.15.got_ref = bf16[16,16,512]{2,1,0:T(8,128)(2,1)} all-to-all(bf16[16,16,512]{2,1,0:T(8,128)(2,1)} %shard_map.127), channel_id=1, replica_groups=mesh['y'=4,'c'=2,'x'=4,'z'=4] {'x','z'}, dimensions={0} | all-to-all | bytes 524288 | tf_op jit(solution)/shard_map/all_to_all | solution.py:529
  30.1 6.1 %shard_map.128 = (bf16[16,80,512]{2,1,0:T(8,128)(2,1)}, bf16[16,64,512]{2,1,0:T(8,128)(2,1)}) custom-call(bf16[16,16,512]{2,1,0:T(8,128)(2,1)} %all_to_all.15.got_ref, bf16[512,8192]{1,0:T(8,128)(2,1)} %w_ref.1), custom_call_target="tpu_custom_call" | custom-call | flops 1100000000 | bytes 11534336 | tf_op jit(solution)/shard_map/pallas_call | solution.py:154
  36.2 3.9 %all-to-all-start.1 = ((bf16[16,64,512]{2,1,0:T(8,128)(2,1)}), bf16[16,64,512]{2,1,0:T(8,128)(2,1)S(1)}, u32[]{:S(2)}, u32[]{:S(2)}) async-start(bf16[16,64,512]{2,1,0:T(8,128)(2,1)} %get-tuple-element.31), calls=%async_computation.1 | async-start | bytes 2097152 | tf_op jit(solution)/shard_map/all_to_all | solution.py:531
  40.1 13.6 %all-gather.3.cloned.1.call-done.table_ref = bf16[384,16,512]{2,1,0:T(8,128)(2,1)} async-done(((bf16[48,16,512]{2,1,0:T(8,128)(2,1)}), bf16[384,16,512]{2,1,0:T(8,128)(2,1)}) %all-gather.3.cloned.1.call-update) | async-done | bytes 6291472 | tf_op jit(solution)/shard_map/all_gather | solution.py:513
  53.7 3.5 %shard_map.130 = bf16[16,80,512]{2,1,0:T(8,128)(2,1)} custom-call(s32[64]{0:T(128)} %idx_ref.3, bf16[16,16,512]{2,1,0:T(8,128)(2,1)} %all_to_all.15.got_ref, bf16[384,16,512]{2,1,0:T(8,128)(2,1)} %all-gather.3.cloned.1.call-done.table_ref, bf16[16,80,512]{2,1,0:T(8,128)(2,1)} %get-tuple-element.32.partial_ref), custom_call_target="tpu_custom_call", output_to_operand_aliasing={{}: (3, {})} | custom-call | flops 140000000 | bytes 2097152 | tf_op jit(solution)/shard_map/pallas_call | solution.py:200
  57.2 6.8 %all-to-all-start.2 = ((bf16[16,80,512]{2,1,0:T(8,128)(2,1)}), bf16[16,80,512]{2,1,0:T(8,128)(2,1)S(1)}, u32[]{:S(2)}, u32[]{:S(2)}) async-start(bf16[16,80,512]{2,1,0:T(8,128)(2,1)} %shard_map.130), calls=%async_computation.2 | async-start | bytes 2621440 | tf_op jit(solution)/shard_map/all_to_all | solution.py:534
  67.5 3.2 %collective-permute-done.1 = bf16[64,512]{1,0:T(8,128)(2,1)S(1)} collective-permute-done((bf16[64,512]{1,0:T(8,128)(2,1)S(1)}, bf16[64,512]{1,0:T(8,128)(2,1)S(1)}, u32[]{:S(2)}, u32[]{:S(2)}) %collective-permute-start.1) | collective-permute-done | bytes 65568 | tf_op jit(solution)/shard_map/ppermute | solution.py:464
  73.4 9.8 %all-to-all-done.2.sums_ref = bf16[16,80,512]{2,1,0:T(8,128)(2,1)S(1)} async-done(((bf16[16,80,512]{2,1,0:T(8,128)(2,1)}), bf16[16,80,512]{2,1,0:T(8,128)(2,1)S(1)}, u32[]{:S(2)}, u32[]{:S(2)}) %all-to-all-start.2) | async-done | bytes 1310752 | tf_op jit(solution)/shard_map/all_to_all | solution.py:534
  85.2 3.5 %collective-permute-done.3 = bf16[4,64,512]{2,1,0:T(8,128)(2,1)S(1)} collective-permute-done((bf16[4,64,512]{2,1,0:T(8,128)(2,1)S(1)}, bf16[4,64,512]{2,1,0:T(8,128)(2,1)S(1)}, u32[]{:S(2)}, u32[]{:S(2)}) %collective-permute-start.3) | collective-permute-done | bytes 262176 | tf_op jit(solution)/shard_map/ppermute | solution.py:475
  90.5 3.1 %collective-permute-done.5 = bf16[4,64,512]{2,1,0:T(8,128)(2,1)S(1)} collective-permute-done((bf16[4,64,512]{2,1,0:T(8,128)(2,1)S(1)}, bf16[4,64,512]{2,1,0:T(8,128)(2,1)S(1)}, u32[]{:S(2)}, u32[]{:S(2)}) %collective-permute-start.5) | collective-permute-done | bytes 262176 | tf_op jit(solution)/shard_map/ppermute | solution.py:475
  99.1 3.7 %shard_map.131 = bf16[64,512]{1,0:T(8,128)(2,1)} custom-call(s32[64]{0:T(128)} %idx_ref.3, bf16[16,80,512]{2,1,0:T(8,128)(2,1)} %copy-done.3, bf16[16,16,512]{2,1,0:T(8,128)(2,1)} %all_to_all.15.got_ref, bf16[1,512]{1,0:T(2,128)(2,1)} %copy-done.2, bf16[384,16,512]{2,1,0:T(8,128)(2,1)} %all-gather.5.cloned.1.call-done.table_ref), custom_call_target="tpu_custom_call" | custom-call | flops 300000000 | bytes 2097152 | tf_op jit(solution)/shard_map/pallas_call | solution.py:273
  103.6 3.0 %collective-permute-done.6 = bf16[64,512]{1,0:T(8,128)(2,1)S(1)} collective-permute-done((bf16[64,512]{1,0:T(8,128)(2,1)}, bf16[64,512]{1,0:T(8,128)(2,1)S(1)}, u32[]{:S(2)}, u32[]{:S(2)}) %collective-permute-start.6) | collective-permute-done | bytes 65568 | tf_op jit(solution)/shard_map/ppermute | solution.py:464
  108.0 3.7 %collective-permute-done.8 = bf16[64,512]{1,0:T(8,128)(2,1)S(1)} collective-permute-done((bf16[64,512]{1,0:T(8,128)(2,1)}, bf16[64,512]{1,0:T(8,128)(2,1)S(1)}, u32[]{:S(2)}, u32[]{:S(2)}) %collective-permute-start.8) | collective-permute-done | bytes 65568 | tf_op jit(solution)/shard_map/ppermute | solution.py:464
  119.7 6.5 %collective-permute-done.12 = bf16[4,64,512]{2,1,0:T(8,128)(2,1)S(1)} collective-permute-done((bf16[4,64,512]{2,1,0:T(8,128)(2,1)S(1)}, bf16[4,64,512]{2,1,0:T(8,128)(2,1)S(1)}, u32[]{:S(2)}, u32[]{:S(2)}) %collective-permute-start.12) | collective-permute-done | bytes 262176 | tf_op jit(solution)/shard_map/ppermute | solution.py:475
  126.2 4.6 %collective-permute-done.13 = bf16[4,64,512]{2,1,0:T(8,128)(2,1)S(1)} collective-permute-done((bf16[4,64,512]{2,1,0:T(8,128)(2,1)S(1)}, bf16[4,64,512]{2,1,0:T(8,128)(2,1)S(1)}, u32[]{:S(2)}, u32[]{:S(2)}) %collective-permute-start.13) | collective-permute-done | bytes 262176 | tf_op jit(solution)/shard_map/ppermute | solution.py:475
  135.7 14.4 %shard_map.132 = (f32[256,1536]{1,0:T(8,128)}, f32[1,256]{1,0:T(1,128)}) custom-call(s32[4]{0:T(128)} %pad_add_fusion.refs_0_, f32[1,8192]{1,0:T(1,128)} %bitcast.24, bf16[4,4,64,512]{3,2,1,0:T(8,128)(2,1)} %copy-done.4, bf16[4,4,64,512]{3,2,1,0:T(8,128)(2,1)} %collective-permute-done.9.refs_3_, bf16[4,4,64,512]{3,2,1,0:T(8,128)(2,1)} %copy-done.6, ...), custom_call_target="tpu_custom_call" | custom-call | flops 2097152 | bytes 524288 | tf_op jit(solution)/shard_map/pallas_call | solution.py:397
  153.2 11.2 %shard_map.133 = (f32[256,1536]{1,0:T(8,128)}, f32[256,128]{1,0:T(8,128)}) custom-call(s32[4]{0:T(128)} %pad_add_fusion.refs_0_, f32[1,8192]{1,0:T(1,128)} %bitcast.25, bf16[4,4,64,512]{3,2,1,0:T(8,128)(2,1)} %copy-done.5, bf16[4,4,64,512]{3,2,1,0:T(8,128)(2,1)} %copy-done.7, bf16[4,4,64,512]{3,2,1,0:T(8,128)(2,1)} %copy-done.8, bf16[8192,768]{1,0:T(8,128)(2,1)} %refs_4_.1, ...), custom_call_target="tpu_custom_call" | custom-call | flops 1572864 | bytes 393216 | tf_op jit(solution)/shard_map/pallas_call | solution.py:397
  165.4 8.3 %shard_map.134 = (f32[256,768]{1,0:T(8,128)}, f32[256,768]{1,0:T(8,128)}, f32[1,512]{1,0:T(1,128)}) custom-call(s32[4]{0:T(128)} %pad_add_fusion.refs_0_, f32[1,8192]{1,0:T(1,128)} %bitcast.26, bf16[2,4,64,512]{3,2,1,0:T(8,128)(2,1)} %copy-done.11, bf16[2,4,64,512]{3,2,1,0:T(8,128)(2,1)} %copy-done.12, bf16[8192,768]{1,0:T(8,128)(2,1)} %refs_4_.1, ...), custom_call_target="tpu_custom_call" | custom-call | flops 524288 | bytes 131072 | tf_op jit(solution)/shard_map/pallas_call | solution.py:397
  179.6 4.5 %collective-permute-start.24 = (f32[256,768]{1,0:T(8,128)}, f32[256,768]{1,0:T(8,128)S(1)}, u32[]{:S(2)}, u32[]{:S(2)}) collective-permute-start(f32[256,768]{1,0:T(8,128)} %get-tuple-element.55), channel_id=1, source_target_pairs={{0,16},{16,0},{1,17},{17,1},{2,18},{18,2},{3,19},{19,3},{4,20},{20... | collective-permute-start | bytes 2359304 | tf_op jit(solution)/shard_map/ppermute | solution.py:564
  186.6 3.2 %collective-permute-done.26 = f32[1,512]{1,0:T(1,128)S(1)} collective-permute-done((f32[1,512]{1,0:T(1,128)S(1)}, f32[1,512]{1,0:T(1,128)S(1)}, u32[]{:S(2)}, u32[]{:S(2)}) %collective-permute-start.26) | collective-permute-done | bytes 2080 | tf_op jit(solution)/shard_map/ppermute | solution.py:464
  189.9 2.9 %collective-permute-start.28 = (f32[1,512]{1,0:T(1,128)S(1)}, f32[1,512]{1,0:T(1,128)S(1)}, u32[]{:S(2)}, u32[]{:S(2)}) collective-permute-start(f32[1,512]{1,0:T(1,128)S(1)} %log_add_fusion.1), channel_id=1, source_target_pairs={{1,0},{2,1},{3,2},{0,3},{5,4},{6,5},{7,6},{4,7},{9,8},{10,9},{11,1... | collective-permute-start | bytes 6152 | tf_op jit(solution)/shard_map/ppermute | solution.py:464
  193.8 2.9 %collective-permute-done.29 = f32[1,512]{1,0:T(1,128)S(1)} collective-permute-done((f32[1,512]{1,0:T(1,128)S(1)}, f32[1,512]{1,0:T(1,128)S(1)}, u32[]{:S(2)}, u32[]{:S(2)}) %collective-permute-start.29) | collective-permute-done | bytes 2080 | tf_op jit(solution)/shard_map/ppermute | solution.py:464
  197.1 3.3 %collective-permute-start.31 = (f32[1,512]{1,0:T(1,128)S(1)}, f32[1,512]{1,0:T(1,128)S(1)}, u32[]{:S(2)}, u32[]{:S(2)}) collective-permute-start(f32[1,512]{1,0:T(1,128)S(1)} %log_add_fusion.no_ref), channel_id=1, source_target_pairs={{0,16},{16,0},{1,17},{17,1},{2,18},{18,2},{3,19},{19,3},{4,20},{20... | collective-permute-start | bytes 6152 | tf_op jit(solution)/shard_map/ppermute | solution.py:565
  (103 shorter events, 50.4 us)
Async XLA Ops:
  6.5 47.1 %all-gather.3.cloned.1.call-start = ((), (), s32[]{:S(2)}) async-start(), calls=%async_computation.3 | async-start | bytes 7077888 | tf_op jit(solution)/shard_map/all_gather | solution.py:513
  7.3 91.9 %all-gather.5.cloned.1.call-start = ((), (), s32[]{:S(2)}) async-start(), calls=%async_computation.4 | async-start | bytes 7077888 | tf_op jit(solution)/shard_map/all_gather | solution.py:514
  8.0 127.7 %collective-permute-start.18 = (bf16[8192,768]{1,0:T(8,128)(2,1)}, bf16[8192,768]{1,0:T(8,128)(2,1)}, u32[]{:S(2)}, u32[]{:S(2)}) collective-permute-start(bf16[8192,768]{1,0:T(8,128)(2,1)} %refs_4_.1), channel_id=1, source_target_pairs={{0,16},{16,0},{1,17},{17,1},{2,18},{18,2},{3,19},{19,3},{4,20},{20... | collective-permute-start | bytes 37748744 | tf_op jit(solution)/shard_map/ppermute | solution.py:512
  36.2 21.0 %all-to-all-start.1 = ((bf16[16,64,512]{2,1,0:T(8,128)(2,1)}), bf16[16,64,512]{2,1,0:T(8,128)(2,1)S(1)}, u32[]{:S(2)}, u32[]{:S(2)}) async-start(bf16[16,64,512]{2,1,0:T(8,128)(2,1)} %get-tuple-element.31), calls=%async_computation.1 | async-start | bytes 2097152 | tf_op jit(solution)/shard_map/all_to_all | solution.py:531
  57.2 26.0 %all-to-all-start.2 = ((bf16[16,80,512]{2,1,0:T(8,128)(2,1)}), bf16[16,80,512]{2,1,0:T(8,128)(2,1)S(1)}, u32[]{:S(2)}, u32[]{:S(2)}) async-start(bf16[16,80,512]{2,1,0:T(8,128)(2,1)} %shard_map.130), calls=%async_computation.2 | async-start | bytes 2621440 | tf_op jit(solution)/shard_map/all_to_all | solution.py:534
  64.9 5.8 %collective-permute-start.1 = (bf16[64,512]{1,0:T(8,128)(2,1)S(1)}, bf16[64,512]{1,0:T(8,128)(2,1)S(1)}, u32[]{:S(2)}, u32[]{:S(2)}) collective-permute-start(bf16[64,512]{1,0:T(8,128)(2,1)S(1)} %shard_map.129), channel_id=1, source_target_pairs={{64,0},{96,32},{0,64},{32,96},{65,1},{97,33},{1,65},{33,97},{66,2}... | collective-permute-start | bytes 196616 | tf_op jit(solution)/shard_map/ppermute | solution.py:464
  66.4 6.9 %collective-permute-start.2 = (bf16[64,512]{1,0:T(8,128)(2,1)S(1)}, bf16[64,512]{1,0:T(8,128)(2,1)S(1)}, u32[]{:S(2)}, u32[]{:S(2)}) collective-permute-start(bf16[64,512]{1,0:T(8,128)(2,1)S(1)} %shard_map.129), channel_id=1, source_target_pairs={{96,0},{0,32},{32,64},{64,96},{97,1},{1,33},{33,65},{65,97},{98,2}... | collective-permute-start | bytes 196616 | tf_op jit(solution)/shard_map/ppermute | solution.py:464
  83.1 5.6 %collective-permute-start.3 = (bf16[4,64,512]{2,1,0:T(8,128)(2,1)S(1)}, bf16[4,64,512]{2,1,0:T(8,128)(2,1)S(1)}, u32[]{:S(2)}, u32[]{:S(2)}) collective-permute-start(bf16[4,64,512]{2,1,0:T(8,128)(2,1)S(1)} %pad_maximum_fusion.2), channel_id=1, source_target_pairs={{4,0},{5,1},{6,2},{7,3},{8,4},{9,5},{10,6},{11,7},{12,8},{13,9},{1... | collective-permute-start | bytes 786440 | tf_op jit(solution)/shard_map/ppermute | solution.py:475
  83.7 6.8 %collective-permute-start.4 = (bf16[4,64,512]{2,1,0:T(8,128)(2,1)S(1)}, bf16[4,64,512]{2,1,0:T(8,128)(2,1)S(1)}, u32[]{:S(2)}, u32[]{:S(2)}) collective-permute-start(bf16[4,64,512]{2,1,0:T(8,128)(2,1)S(1)} %pad_maximum_fusion.2), channel_id=1, source_target_pairs={{8,0},{9,1},{10,2},{11,3},{12,4},{13,5},{14,6},{15,7},{0,8},{1,9},... | collective-permute-start | bytes 786440 | tf_op jit(solution)/shard_map/ppermute | solution.py:475
  85.2 8.4 %collective-permute-start.5 = (bf16[4,64,512]{2,1,0:T(8,128)(2,1)S(1)}, bf16[4,64,512]{2,1,0:T(8,128)(2,1)S(1)}, u32[]{:S(2)}, u32[]{:S(2)}) collective-permute-start(bf16[4,64,512]{2,1,0:T(8,128)(2,1)S(1)} %pad_maximum_fusion.2), channel_id=1, source_target_pairs={{12,0},{13,1},{14,2},{15,3},{0,4},{1,5},{2,6},{3,7},{4,8},{5,9},{6... | collective-permute-start | bytes 786440 | tf_op jit(solution)/shard_map/ppermute | solution.py:475
  93.8 18.8 %collective-permute-start.10 = (bf16[4,4,64,512]{3,2,1,0:T(8,128)(2,1)S(1)}, bf16[4,4,64,512]{3,2,1,0:T(8,128)(2,1)S(1)}, u32[]{:S(2)}, u32[]{:S(2)}) collective-permute-start(bf16[4,4,64,512]{3,2,1,0:T(8,128)(2,1)S(1)} %pad_maximum_fusion.refs_2_), channel_id=1, source_target_pairs={{3,0},{0,1},{1,2},{2,3},{7,4},{4,5},{5,6},{6,7},{11,8},{8,9},{9,10... | collective-permute-start | bytes 3145736 | tf_op jit(solution)/shard_map/ppermute | solution.py:475
  94.7 18.0 %collective-permute-start.9 = (bf16[4,4,64,512]{3,2,1,0:T(8,128)(2,1)S(1)}, bf16[4,4,64,512]{3,2,1,0:T(8,128)(2,1)}, u32[]{:S(2)}, u32[]{:S(2)}) collective-permute-start(bf16[4,4,64,512]{3,2,1,0:T(8,128)(2,1)S(1)} %pad_maximum_fusion.refs_2_), channel_id=1, source_target_pairs={{1,0},{2,1},{3,2},{0,3},{5,4},{6,5},{7,6},{4,7},{9,8},{10,9},{11,1... | collective-permute-start | bytes 3145736 | tf_op jit(solution)/shard_map/ppermute | solution.py:475
  103.2 4.8 %collective-permute-start.7 = (bf16[64,512]{1,0:T(8,128)(2,1)}, bf16[64,512]{1,0:T(8,128)(2,1)S(1)}, u32[]{:S(2)}, u32[]{:S(2)}) collective-permute-start(bf16[64,512]{1,0:T(8,128)(2,1)} %shard_map.131), channel_id=1, source_target_pairs={{64,0},{96,32},{0,64},{32,96},{65,1},{97,33},{1,65},{33,97},{66,2}... | collective-permute-start | bytes 196616 | tf_op jit(solution)/shard_map/ppermute | solution.py:464
  106.6 5.1 %collective-permute-start.8 = (bf16[64,512]{1,0:T(8,128)(2,1)}, bf16[64,512]{1,0:T(8,128)(2,1)S(1)}, u32[]{:S(2)}, u32[]{:S(2)}) collective-permute-start(bf16[64,512]{1,0:T(8,128)(2,1)} %shard_map.131), channel_id=1, source_target_pairs={{96,0},{0,32},{32,64},{64,96},{97,1},{1,33},{33,65},{65,97},{98,2}... | collective-permute-start | bytes 196616 | tf_op jit(solution)/shard_map/ppermute | solution.py:464
  112.7 6.4 %collective-permute-start.11 = (bf16[4,64,512]{2,1,0:T(8,128)(2,1)S(1)}, bf16[4,64,512]{2,1,0:T(8,128)(2,1)S(1)}, u32[]{:S(2)}, u32[]{:S(2)}) collective-permute-start(bf16[4,64,512]{2,1,0:T(8,128)(2,1)S(1)} %pad_maximum_fusion.3), channel_id=1, source_target_pairs={{4,0},{5,1},{6,2},{7,3},{8,4},{9,5},{10,6},{11,7},{12,8},{13,9},{1... | collective-permute-start | bytes 786440 | tf_op jit(solution)/shard_map/ppermute | solution.py:475
  116.2 14.7 %collective-permute-start.14 = (bf16[2,4,64,512]{3,2,1,0:T(8,128)(2,1)S(1)}, bf16[2,4,64,512]{3,2,1,0:T(8,128)(2,1)S(1)}, u32[]{:S(2)}, u32[]{:S(2)}) collective-permute-start(bf16[2,4,64,512]{3,2,1,0:T(8,128)(2,1)S(1)} %slice.12), channel_id=1, source_target_pairs={{1,0},{2,1},{3,2},{0,3},{5,4},{6,5},{7,6},{4,7},{9,8},{10,9},{11,1... | collective-permute-start | bytes 1572872 | tf_op jit(solution)/shard_map/ppermute | solution.py:475
  118.7 13.5 %collective-permute-start.15 = (bf16[2,4,64,512]{3,2,1,0:T(8,128)(2,1)S(1)}, bf16[2,4,64,512]{3,2,1,0:T(8,128)(2,1)S(1)}, u32[]{:S(2)}, u32[]{:S(2)}) collective-permute-start(bf16[2,4,64,512]{3,2,1,0:T(8,128)(2,1)S(1)} %slice.13), channel_id=1, source_target_pairs={{3,0},{0,1},{1,2},{2,3},{7,4},{4,5},{5,6},{6,7},{11,8},{8,9},{9,10... | collective-permute-start | bytes 1572872 | tf_op jit(solution)/shard_map/ppermute | solution.py:475
  118.8 7.5 %collective-permute-start.12 = (bf16[4,64,512]{2,1,0:T(8,128)(2,1)S(1)}, bf16[4,64,512]{2,1,0:T(8,128)(2,1)S(1)}, u32[]{:S(2)}, u32[]{:S(2)}) collective-permute-start(bf16[4,64,512]{2,1,0:T(8,128)(2,1)S(1)} %pad_maximum_fusion.3), channel_id=1, source_target_pairs={{8,0},{9,1},{10,2},{11,3},{12,4},{13,5},{14,6},{15,7},{0,8},{1,9},... | collective-permute-start | bytes 786440 | tf_op jit(solution)/shard_map/ppermute | solution.py:475
  119.1 11.7 %collective-permute-start.13 = (bf16[4,64,512]{2,1,0:T(8,128)(2,1)S(1)}, bf16[4,64,512]{2,1,0:T(8,128)(2,1)S(1)}, u32[]{:S(2)}, u32[]{:S(2)}) collective-permute-start(bf16[4,64,512]{2,1,0:T(8,128)(2,1)S(1)} %pad_maximum_fusion.3), channel_id=1, source_target_pairs={{12,0},{13,1},{14,2},{15,3},{0,4},{1,5},{2,6},{3,7},{4,8},{5,9},{6... | collective-permute-start | bytes 786440 | tf_op jit(solution)/shard_map/ppermute | solution.py:475
  132.2 18.0 %collective-permute-start.16 = (bf16[4,4,64,512]{3,2,1,0:T(8,128)(2,1)S(1)}, bf16[4,4,64,512]{3,2,1,0:T(8,128)(2,1)S(1)}, u32[]{:S(2)}, u32[]{:S(2)}) collective-permute-start(bf16[4,4,64,512]{3,2,1,0:T(8,128)(2,1)S(1)} %pad_maximum_fusion.1.refs_2_), channel_id=1, source_target_pairs={{1,0},{2,1},{3,2},{0,3},{5,4},{6,5},{7,6},{4,7},{9,8},{10,9},{11,1... | collective-permute-start | bytes 3145736 | tf_op jit(solution)/shard_map/ppermute | solution.py:475
  134.5 15.8 %collective-permute-start.17 = (bf16[4,4,64,512]{3,2,1,0:T(8,128)(2,1)S(1)}, bf16[4,4,64,512]{3,2,1,0:T(8,128)(2,1)S(1)}, u32[]{:S(2)}, u32[]{:S(2)}) collective-permute-start(bf16[4,4,64,512]{3,2,1,0:T(8,128)(2,1)S(1)} %pad_maximum_fusion.1.refs_2_), channel_id=1, source_target_pairs={{3,0},{0,1},{1,2},{2,3},{7,4},{4,5},{5,6},{6,7},{11,8},{8,9},{9,10... | collective-permute-start | bytes 3145736 | tf_op jit(solution)/shard_map/ppermute | solution.py:475
  150.3 14.1 %collective-permute-start.19 = (bf16[2,4,64,512]{3,2,1,0:T(8,128)(2,1)S(1)}, bf16[2,4,64,512]{3,2,1,0:T(8,128)(2,1)S(1)}, u32[]{:S(2)}, u32[]{:S(2)}) collective-permute-start(bf16[2,4,64,512]{3,2,1,0:T(8,128)(2,1)S(1)} %slice.14), channel_id=1, source_target_pairs={{1,0},{2,1},{3,2},{0,3},{5,4},{6,5},{7,6},{4,7},{9,8},{10,9},{11,1... | collective-permute-start | bytes 1572872 | tf_op jit(solution)/shard_map/ppermute | solution.py:475
  153.1 11.4 %collective-permute-start.20 = (bf16[2,4,64,512]{3,2,1,0:T(8,128)(2,1)S(1)}, bf16[2,4,64,512]{3,2,1,0:T(8,128)(2,1)S(1)}, u32[]{:S(2)}, u32[]{:S(2)}) collective-permute-start(bf16[2,4,64,512]{3,2,1,0:T(8,128)(2,1)S(1)} %slice.15), channel_id=1, source_target_pairs={{3,0},{0,1},{1,2},{2,3},{7,4},{4,5},{5,6},{6,7},{11,8},{8,9},{9,10... | collective-permute-start | bytes 1572872 | tf_op jit(solution)/shard_map/ppermute | solution.py:475
  179.6 21.6 %collective-permute-start.24 = (f32[256,768]{1,0:T(8,128)}, f32[256,768]{1,0:T(8,128)S(1)}, u32[]{:S(2)}, u32[]{:S(2)}) collective-permute-start(f32[256,768]{1,0:T(8,128)} %get-tuple-element.55), channel_id=1, source_target_pairs={{0,16},{16,0},{1,17},{17,1},{2,18},{18,2},{3,19},{19,3},{4,20},{20... | collective-permute-start | bytes 2359304 | tf_op jit(solution)/shard_map/ppermute | solution.py:564
  (26 other events, 162.2 us)
Sparse Core Ops, SparseCore 0:
  9.0 44.5 all-gather.2
  55.4 43.7 all-gather.4
